TPU v7x, 256 devices: a whole 4x4x8 slice. The times are simulated.
256 devices in a mesh: dp: 16 (over y, x_hi, core), tm: 16 (over x_lo, z).
Axes of the slice: x: 4 (x_hi: 2, x_lo: 2; x = x_hi * 2 + x_lo), y: 4, z: 8, core: 2. Of those that a mesh axis runs over, the one named last changes fastest.
Arguments:
- frames_in: bfloat16 [16, 32, 128, 1024], P('dp', 'tm'), may hold values from -8 to 8
- gain: float32 [1024], replicated, may hold values from 0.5 to 1.5
- w_qkv: bfloat16 [1024, 1536], P(('dp', 'tm')), may hold values from -2 to 2
- w_out: bfloat16 [512, 1024], P(None, ('dp', 'tm')), may hold values from -0.25 to 0.25
- out_grad: bfloat16 [16, 32, 128, 1024], P('dp', 'tm'), may hold values from -6 to 6
Outputs:
- result: bfloat16 [16, 32, 128, 1024], P('dp', 'tm')
- grad_in: bfloat16 [16, 32, 128, 1024], P('dp', 'tm')
- grad_qkv: float32 [1024, 1536], P(('dp', 'tm'))
- grad_out: float32 [512, 1024], P(None, ('dp', 'tm'))
- grad_gain: float32 [1024], P(('dp', 'tm'))
All inputs are finite; a program needn't handle non-finite values.
Results may differ from a plain program's by a relative error of at most 0.01.
The roundings to bfloat16 on the way count: a program that leaves them out, or rounds other values in their place, can miss the bound.
Values may be sent and summed in bfloat16 or wider, within the bound.
No kernel may reach another device: no remote copies, remote signals or barrier semaphores. Data moves between devices by JAX's collectives and lax.ppermute only.
A program may use at most 64 MiB of HBM per device.

v0:
```python
import jax
import jax.numpy as jnp
from jax import lax
from jax.sharding import PartitionSpec as P

HEADS = 8
DH = 64


norm_eps = 1e-05


def split_heads(packed):
    frame_count, patch_count = (packed.shape[0], packed.shape[1])
    parts = packed.reshape(frame_count, patch_count, 3, HEADS, DH).transpose(2, 1, 3, 0, 4)
    return (parts[0], parts[1], parts[2])


def attend(packed):
    query, keys, values = split_heads(packed)
    scores = jnp.einsum(
        "phfd,phgd->phfg", query, keys, preferred_element_type=jnp.float32
    ) * DH ** (-0.5)
    top_val = jnp.max(scores, axis=-1, keepdims=True)
    expo = jnp.exp(scores - top_val)
    prob = expo / jnp.sum(expo, axis=-1, keepdims=True)
    prob_low = prob.astype(jnp.bfloat16)
    mixed = jnp.einsum(
        "phfg,phgd->phfd", prob_low, values, preferred_element_type=jnp.float32
    ).astype(jnp.bfloat16)
    patch_count, head_count, frame_count, head_dim = mixed.shape
    merged = mixed.transpose(2, 0, 1, 3).reshape(frame_count, patch_count, head_count * head_dim)
    return (merged, prob, prob_low)


def attend_back(packed, prob, prob_low, d_mixed):
    query, keys, values = split_heads(packed)
    frame_count, patch_count = (d_mixed.shape[0], d_mixed.shape[1])
    d_heads = d_mixed.reshape(frame_count, patch_count, HEADS, DH).transpose(1, 2, 0, 3)
    d_prob = jnp.einsum("phfd,phgd->phfg", d_heads, values, preferred_element_type=jnp.float32)
    d_values = jnp.einsum(
        "phfg,phfd->phgd", prob_low, d_heads, preferred_element_type=jnp.float32
    ).astype(jnp.bfloat16)
    inner = jnp.sum(d_prob * prob, axis=-1, keepdims=True)
    d_scores = (prob * (d_prob - inner) * DH ** (-0.5)).astype(jnp.bfloat16)
    d_query = jnp.einsum(
        "phfg,phgd->phfd", d_scores, keys, preferred_element_type=jnp.float32
    ).astype(jnp.bfloat16)
    d_keys = jnp.einsum(
        "phfg,phfd->phgd", d_scores, query, preferred_element_type=jnp.float32
    ).astype(jnp.bfloat16)
    stacked = jnp.stack([d_query, d_keys, d_values])
    return stacked.transpose(3, 1, 0, 2, 4).reshape(frame_count, patch_count, 3 * HEADS * DH)


def against_rows(left_rows, weight_full):
    return lax.dot_general(
        left_rows, weight_full, (((1,), (1,)), ((), ())), preferred_element_type=jnp.float32
    )


def transposed_product(left_rows, right_rows):
    return lax.dot_general(
        left_rows, right_rows, (((0,), (0,)), ((), ())), preferred_element_type=jnp.float32
    )


def body(frames_in, gain, w_qkv, w_out, out_grad):
    frame_count, patch_count, width = (frames_in.shape[1], frames_in.shape[2], frames_in.shape[3])
    row_count = frame_count * patch_count
    qkv_full = lax.all_gather(w_qkv, ("dp", "tm"), axis=0, tiled=True)
    out_full = lax.all_gather(w_out, ("dp", "tm"), axis=1, tiled=True)
    wide = frames_in.astype(jnp.float32)
    mean_val = jnp.mean(wide, axis=-1, keepdims=True)
    centred = wide - mean_val
    inv_std = lax.rsqrt(jnp.mean(centred * centred, axis=-1, keepdims=True) + norm_eps)
    normal_x = centred * inv_std
    normed = (normal_x * gain).astype(jnp.bfloat16)
    packed_local = jnp.dot(
        normed.reshape(row_count, width), qkv_full, preferred_element_type=jnp.float32
    ).astype(jnp.bfloat16)
    packed_local = packed_local.reshape(1, frame_count, patch_count, 3 * HEADS * DH)
    packed_time = lax.all_to_all(packed_local, "tm", split_axis=2, concat_axis=1, tiled=True)
    merged, prob, prob_low = attend(packed_time[0])
    mixed_back = lax.all_to_all(merged[None], "tm", split_axis=1, concat_axis=2, tiled=True)
    mixed_rows = mixed_back.reshape(row_count, HEADS * DH)
    projected = jnp.dot(mixed_rows, out_full, preferred_element_type=jnp.float32)
    result = (
        (wide.reshape(row_count, width) + projected).astype(jnp.bfloat16).reshape(frames_in.shape)
    )
    grad_rows = out_grad.reshape(row_count, width)
    out_partial = transposed_product(mixed_rows, grad_rows)
    d_mixed = against_rows(grad_rows, out_full).astype(jnp.bfloat16)
    d_time = lax.all_to_all(
        d_mixed.reshape(1, frame_count, patch_count, HEADS * DH),
        "tm",
        split_axis=2,
        concat_axis=1,
        tiled=True,
    )
    d_packed_time = attend_back(packed_time[0], prob, prob_low, d_time[0])
    d_packed = lax.all_to_all(
        d_packed_time[None], "tm", split_axis=1, concat_axis=2, tiled=True
    ).reshape(row_count, 3 * HEADS * DH)
    qkv_partial = transposed_product(normed.reshape(row_count, width), d_packed)
    d_normed = against_rows(d_packed, qkv_full).astype(jnp.bfloat16).reshape(frames_in.shape)
    d_wide = d_normed.astype(jnp.float32)
    gain_partial = jnp.sum(d_wide * normal_x, axis=(0, 1, 2))
    scaled = d_wide * gain
    d_input = inv_std * (
        scaled
        - jnp.mean(scaled, axis=-1, keepdims=True)
        - normal_x * jnp.mean(scaled * normal_x, axis=-1, keepdims=True)
    )
    grad_in = (out_grad.astype(jnp.float32) + d_input).astype(jnp.bfloat16)
    grad_qkv, grad_gain = (
        lax.psum_scatter(qkv_partial, ("dp", "tm"), scatter_dimension=0, tiled=True),
        lax.psum_scatter(gain_partial, ("dp", "tm"), scatter_dimension=0, tiled=True),
    )
    grad_out = lax.psum_scatter(out_partial, ("dp", "tm"), scatter_dimension=1, tiled=True)
    return (result, grad_in, grad_qkv, grad_out, grad_gain)


def solution(mesh):
    in_specs = (
        P("dp", "tm", None, None),
        P(),
        P(("dp", "tm"), None),
        P(None, ("dp", "tm")),
        P("dp", "tm", None, None),
    )
    out_specs = (
        P("dp", "tm", None, None),
        P("dp", "tm", None, None),
        P(("dp", "tm"), None),
        P(None, ("dp", "tm")),
        P(("dp", "tm")),
    )
    return jax.shard_map(body, mesh=mesh, in_specs=in_specs, out_specs=out_specs, check_vma=False)
```

profile of v0, /device:TPU:1, one launch (start us, length us, event | category | flops | bytes accessed | tf_op | source)
XLA Modules:
  0.0 1637.2 jit_solution(14597189449272445794)
XLA Ops:
  7.2 0.0 all-gather.7.cloned.1.call-start
  7.2 0.7 all-gather.7.cloned.1.call-update
  7.9 0.0 all-gather.5.cloned.1.call-start
  7.9 0.7 all-gather.5.cloned.1.call-update
  8.6 0.0 copy-start.1
  8.7 1.2 convert_reduce_fusion
  9.9 1.3 multiply_reduce_fusion.3
  11.3 532.2 %all-gather.7.cloned.1.call-done = bf16[256,4,512]{2,1,0:T(4,128)(2,1)} async-done(((bf16[1,4,512]{2,1,0:T(4,128)(2,1)}), bf16[256,4,512]{2,1,0:T(4,128)(2,1)}) %all-gather.7.cloned.1.call-update) | async-done | bytes 1048592 | tf_op jit(solution)/shard_map/all_gather | solution.py:72
  543.4 1.3 reshape.132
  544.8 0.0 copy-start
  544.8 0.0 copy-start.11
  544.8 0.4 convolution_convert_fusion.6
  545.3 1.0 copy.52
  546.2 6.3 all-to-all-start.2
  552.6 0.0 copy-done
  552.6 0.0 copy-done.11
  552.6 0.3 multiply_convert_fusion
  552.9 692.6 %all-gather.5.cloned.1.call-done = bf16[256,4,1536]{2,1,0:T(4,128)(2,1)} async-done(((bf16[1,4,1536]{2,1,0:T(4,128)(2,1)}), bf16[256,4,1536]{2,1,0:T(4,128)(2,1)}) %all-gather.5.cloned.1.call-update) | async-done | bytes 3145744 | tf_op jit(solution)/shard_map/all_gather | solution.py:71
  1245.5 5.9 reshape.130
  1251.4 0.0 copy-done.5
  1251.4 2.9 convolution_convert_fusion
  1254.3 1.7 copy.44
  1256.0 0.0 all-to-all-done.2
  1256.0 10.3 all-to-all-start
  1266.4 1.1 reshape_squeeze.8
  1267.5 18.6 %all-to-all-done = bf16[1,2,128,1536]{3,1,0,2:T(2,128)(2,1)S(1)} async-done(((bf16[1,2,128,1536]{3,1,0,2:T(2,128)(2,1)}), bf16[1,2,128,1536]{3,1,0,2:T(2,128)(2,1)S(1)}, u32[]{:S(2)}, u32[]{:S(2)}) %all-to-all-start) | async-done | bytes 786464 | tf_op jit(solution)/shard_map/all_to_all | solution.py:83
  1286.0 0.1 copy.74
  1286.1 1.0 copy.46
  1287.1 2.4 reshape_squeeze.7
  1289.5 2.2 copy.73
  1291.7 2.8 fusion.34
  1294.5 2.6 fusion.20
  1297.0 1.2 fusion.10
  1298.2 3.4 fusion.12
  1301.6 2.0 copy.49
  1303.7 2.1 broadcast_in_dim_reshape.6
  1305.8 6.3 all-to-all-start.1
  1312.1 3.5 fusion.11
  1315.7 1.9 fusion.13
  1317.6 0.0 copy-done.9
  1317.6 0.4 maximum_bitcast_fusion
  1318.0 0.6 copy.57
  1318.6 1.7 broadcast_in_dim_reshape.7
  1320.3 0.6 all-to-all-done.1
  1320.9 7.1 all-to-all-start.3
  1328.0 0.2 all-reduce.6.cloned.1.call-start
  1328.3 0.0 copy-start.7
  1328.3 0.7 copy-done.7
  1329.0 1.8 fusion.36
  1330.8 16.3 all-to-all-done.3
  1347.1 0.9 copy-done.3
  1348.0 1.2 copy.59
  1349.2 3.7 fusion.35
  1352.8 0.0 all-reduce.6.cloned.1.call-update
  1352.9 0.9 copy-done.8
  1353.8 1.3 fusion.7
  1355.1 3.0 multiply_reduce_fusion.2
  1358.0 0.4 multiply_reduce_fusion
  1358.5 76.5 %all-reduce.2 = f32[1024]{0:T(1024)S(1)} all-reduce(f32[1024]{0:T(1024)S(1)} %get-tuple-element.5), channel_id=4, replica_groups=mesh['dp'=16,'tm'=16] {'dp','tm'}, use_global_device_ids=true, to_apply=%region_10.0.clone | all-reduce | flops 1024 | bytes 8192
  1435.0 0.6 dynamic-slice.2
  1435.6 1.2 add_convert_fusion
  1436.8 191.1 %all-reduce.6.cloned.1.call-done = (f32[1024,1536]{1,0:T(8,128)}, f32[512,1024]{0,1:T(8,128)}) async-done(((f32[1024,1536]{1,0:T(8,128)}, f32[512,1024]{0,1:T(8,128)}), (f32[1024,1536]{1,0:T(8,128)}, f32[512,1024]{0,1:T(8,128)})) %all-reduce.6.cloned.1.call-update) | async-done | bytes 8388624
  1627.9 1.4 constant_dynamic-slice_fusion.1
  1629.3 1.3 constant_dynamic-slice_fusion
  (22 shorter events, 0.1 us)
Async XLA Ops:
  7.2 536.3 %all-gather.7.cloned.1.call-start = ((), (), s32[]{:S(2)}) async-start(), calls=%async_computation.5 | async-start | bytes 1052672 | tf_op jit(solution)/shard_map/all_gather | solution.py:72
  7.9 1237.6 %all-gather.5.cloned.1.call-start = ((), (), s32[]{:S(2)}) async-start(), calls=%async_computation.4 | async-start | bytes 3158016 | tf_op jit(solution)/shard_map/all_gather | solution.py:71
  8.6 536.2 %copy-start.1 = (bf16[1,2,128,1024]{3,2,1,0:T(8,128)(2,1)S(1)}, bf16[1,2,128,1024]{3,2,1,0:T(8,128)(2,1)}, u32[]{:S(2)}) copy-start(bf16[1,2,128,1024]{3,2,1,0:T(8,128)(2,1)} %param.9) | copy-start | bytes 1572868
  544.8 7.8 copy-start
  544.8 7.8 copy-start.11
  546.2 709.8 %all-to-all-start.2 = ((bf16[1,2,128,512]{3,1,0,2:T(2,128)(2,1)}), bf16[1,2,128,512]{3,1,0,2:T(2,128)(2,1)S(1)}, u32[]{:S(2)}, u32[]{:S(2)}) async-start(bf16[1,2,128,512]{3,1,0,2:T(2,128)(2,1)} %copy.52), calls=%async_computation.2 | async-start | bytes 524288 | tf_op jit(solution)/shard_map/all_to_all | solution.py:94
  552.9 698.5 %copy-start.5 = (bf16[1,2,128,1024]{3,2,1,0:T(8,128)(2,1)}, bf16[1,2,128,1024]{3,2,1,0:T(8,128)(2,1)S(1)}, u32[]{:S(2)}) copy-start(bf16[1,2,128,1024]{3,2,1,0:T(8,128)(2,1)S(1)} %multiply_convert_fusion) | copy-start | bytes 1572868
  1256.0 30.0 %all-to-all-start = ((bf16[1,2,128,1536]{3,1,0,2:T(2,128)(2,1)}), bf16[1,2,128,1536]{3,1,0,2:T(2,128)(2,1)S(1)}, u32[]{:S(2)}, u32[]{:S(2)}) async-start(bf16[1,2,128,1536]{3,1,0,2:T(2,128)(2,1)} %copy.44), calls=%async_computation | async-start | bytes 1572864 | tf_op jit(solution)/shard_map/all_to_all | solution.py:83
  1291.7 2.8 copy-start.4
  1294.5 2.6 copy-start.12
  1305.8 15.1 all-to-all-start.1
  1315.6 1.9 copy-start.9
  1315.6 1.9 copy-start.10
  1320.3 8.7 copy-start.2
  1320.9 26.2 %all-to-all-start.3 = ((bf16[1,32,8,1536]{3,2,0,1:T(8,128)(2,1)}), bf16[1,32,8,1536]{3,2,0,1:T(8,128)(2,1)S(1)}, u32[]{:S(2)}, u32[]{:S(2)}) async-start(bf16[1,32,8,1536]{3,2,0,1:T(8,128)(2,1)} %bitcast.106), calls=%async_computation.3 | async-start | bytes 1572864 | tf_op jit(solution)/shard_map/all_to_all | solution.py:102
  1328.0 299.9 %all-reduce.6.cloned.1.call-start = ((), (), s32[]{:S(2)}) async-start(), calls=%async_computation.6 | async-start | bytes 16777216
  1328.3 0.7 copy-start.7
  1329.0 20.2 %copy-start.6 = (bf16[1,2,128,1024]{3,2,1,0:T(8,128)(2,1)S(1)}, bf16[1,2,128,1024]{3,2,1,0:T(8,128)(2,1)}, u32[]{:S(2)}) copy-start(bf16[1,2,128,1024]{3,2,1,0:T(8,128)(2,1)} %copy-done.5) | copy-start | bytes 1572868
  1347.1 0.9 copy-start.3
  1352.8 0.9 copy-start.8
Sparse Core Ops, SparseCore 0:
  9.8 533.6 all-gather.6
  545.3 700.1 all-gather.4
  1353.0 274.8 all-reduce.5
where the time goes:
time: 1640 us
  waiting for transfers between devices  1450 us (88%)
  blocking collectives  76.5 us (5%)
  starting transfers between devices  30.5 us (2%)
  local copies, waits for them, and re-layouts  30.2 us (2%)
  matrix products  28.4 us (2%)
    all_gather x1, waiting for transfers between devices, body(): qkv_full = lax.all_gather(w_qkv, ('dp', 'tm'), axis=0, tiled=True)  693 us
    all_gather x1, waiting for transfers between devices, body(): out_full = lax.all_gather(w_out, ('dp', 'tm'), axis=1, tiled=True)  532 us
    unnamed x4, waiting for transfers between devices  192 us
    unnamed x1, blocking collectives  76.5 us
  transfers between devices with their start and end apart: 7, of which 6 were waited for; matrix products, arithmetic and copies ran while one was open for 2% of the time, Pallas kernels for 0%

commit v1 on v0

v1 whole, which is shorter than its diff:
```python
import functools

import jax
import jax.numpy as jnp
from jax import lax
from jax.experimental import pallas as pl
from jax.experimental.pallas import tpu as pltpu
from jax.sharding import Mesh, PartitionSpec as P

DP = ("y", "xh", "core")
TM = ("xl", "z")
GROUP = ("y", "xh")

D = 1024
DH = 64
HALF = 256
norm_eps = 1e-05
f32 = jnp.float32
bf16 = jnp.bfloat16

NN = (((1,), (0,)), ((), ()))
NT = (((1,), (1,)), ((), ()))
TN = (((0,), (0,)), ((), ()))


def mm(a, b, dims):
    return lax.dot_general(a, b, dims, preferred_element_type=f32)


def layer_stats(features):
    wide = features.astype(f32)
    centred = wide - jnp.mean(wide, axis=-1, keepdims=True)
    inv_std = lax.rsqrt(jnp.mean(centred * centred, axis=-1, keepdims=True) + norm_eps)
    return centred * inv_std, inv_std


def attention_kernel(patches, x_ref, og_ref, gain_ref, w_ref, normed_ref, mixed_ref, dpacked_ref):
    rows = x_ref.shape[1]
    row_patch = lax.broadcasted_iota(jnp.int32, (rows, rows), 0) % patches
    col_patch = lax.broadcasted_iota(jnp.int32, (rows, rows), 1) % patches
    same = row_patch == col_patch
    low_half = lax.broadcasted_iota(jnp.int32, (rows, 2 * DH), 1) < DH
    zero = jnp.zeros((rows, 2 * DH), bf16)
    for s in range(2):
        normal_x, _ = layer_stats(x_ref[s])
        normed = (normal_x * gain_ref[...]).astype(bf16)
        normed_ref[s] = normed
        packed = mm(normed, w_ref[:, : 3 * HALF], NN).astype(bf16)
        d_mixed = mm(og_ref[s], w_ref[:, 3 * HALF :], NN).astype(bf16)
        for pair in range(HALF // (2 * DH)):
            lo = pair * 2 * DH
            query = packed[:, lo : lo + 2 * DH]
            keys = packed[:, HALF + lo : HALF + lo + 2 * DH]
            values = packed[:, 2 * HALF + lo : 2 * HALF + lo + 2 * DH]
            d_heads = d_mixed[:, lo : lo + 2 * DH]
            parts = []
            for head in range(2):
                own = low_half if head == 0 else jnp.logical_not(low_half)
                scores = mm(jnp.where(own, query, zero), keys, NT) * DH ** (-0.5)
                scores = jnp.where(same, scores, -1e30)
                expo = jnp.exp(scores - jnp.max(scores, axis=-1, keepdims=True))
                prob = expo / jnp.sum(expo, axis=-1, keepdims=True)
                prob_low = prob.astype(bf16)
                mixed = mm(prob_low, values, NN)
                d_prob = mm(jnp.where(own, d_heads, zero), values, NT)
                d_values = mm(prob_low, d_heads, TN)
                inner = jnp.sum(d_prob * prob, axis=-1, keepdims=True)
                d_scores = (prob * (d_prob - inner) * DH ** (-0.5)).astype(bf16)
                d_query = mm(d_scores, keys, NN)
                d_keys = mm(d_scores, query, TN)
                parts.append((mixed, d_query, d_keys, d_values))
            mixed, d_query, d_keys, d_values = (
                jnp.where(low_half, a, b).astype(bf16) for a, b in zip(*parts)
            )
            mixed_ref[s, :, lo : lo + 2 * DH] = mixed
            dpacked_ref[s, :, lo : lo + 2 * DH] = d_query
            dpacked_ref[s, :, HALF + lo : HALF + lo + 2 * DH] = d_keys
            dpacked_ref[s, :, 2 * HALF + lo : 2 * HALF + lo + 2 * DH] = d_values


def gradient_kernel(normed_ref, og_ref, dpacked_ref, mixed_ref, g_ref):
    g_ref[:, : 3 * HALF] = mm(normed_ref[...], dpacked_ref[...], TN).astype(bf16)
    g_ref[:, 3 * HALF :] = mm(og_ref[...], mixed_ref[...], TN).astype(bf16)


def input_kernel(x_ref, og_ref, gain_ref, dp_mine_ref, dp_other_ref, w_mine_ref, w_other_ref, out_ref):
    d_normed = mm(dp_mine_ref[...], w_mine_ref[:, : 3 * HALF], NT)
    d_normed = d_normed + mm(dp_other_ref[...], w_other_ref[:, : 3 * HALF], NT)
    d_normed = d_normed.astype(bf16).astype(f32)
    normal_x, inv_std = layer_stats(x_ref[...])
    scaled = d_normed * gain_ref[...]
    d_input = inv_std * (
        scaled
        - jnp.mean(scaled, axis=-1, keepdims=True)
        - normal_x * jnp.mean(scaled * normal_x, axis=-1, keepdims=True)
    )
    out_ref[...] = (og_ref[...].astype(f32) + d_input).astype(bf16)


def result_kernel(x_ref, mixed_ref, w_mine_ref, w_other_ref, out_ref):
    projected = mm(mixed_ref[:, :HALF], w_mine_ref[...], NT)
    projected = projected + mm(mixed_ref[:, HALF:], w_other_ref[...], NT)
    out_ref[...] = (x_ref[...].astype(f32) + projected).astype(bf16)


def vmem_params():
    return pltpu.CompilerParams(vmem_limit_bytes=48 * 1024 * 1024)


def exchange(value):
    return lax.ppermute(value, "core", [(0, 1), (1, 0)])


def swap(value, axes):
    return lax.all_to_all(value, axes, split_axis=0, concat_axis=0, tiled=True)


def body(frames_in, gain, w_qkv, w_out, out_grad):
    _, frames, patch_count, width = frames_in.shape
    tm = 16
    group = 8
    patches = patch_count // tm
    per_peer = frames * patches
    rows = tm * per_peer
    shard = w_qkv.shape[0]
    core = lax.axis_index("core")
    gain_row = gain.reshape(1, width)

    def by_patch(value):
        value = value.reshape(frames, tm, patches, width).transpose(1, 0, 2, 3)
        return value.reshape(tm, per_peer, width)

    w_parts = jnp.concatenate([w_qkv.reshape(shard, 3, 2, HALF), w_out.T.reshape(shard, 1, 2, HALF)], axis=1)
    w_parts = w_parts.transpose(2, 0, 1, 3).reshape(1, 2 * shard, 4 * HALF)
    w_parts = jnp.broadcast_to(w_parts, (tm, 2 * shard, 4 * HALF))
    sent = jnp.concatenate([by_patch(frames_in), by_patch(out_grad), w_parts], axis=1)
    got = swap(sent.reshape(-1, width), TM).reshape(tm, 2 * per_peer + 2 * shard, width)
    x_own = got[:, :per_peer].reshape(rows, width)
    og_own = got[:, per_peer : 2 * per_peer].reshape(rows, width)
    w_got = got[:, 2 * per_peer :].reshape(tm, 2, shard, width)

    w_keep = lax.dynamic_index_in_dim(w_got, core, 1, keepdims=False).reshape(tm * shard, width)
    w_send = lax.dynamic_index_in_dim(w_got, 1 - core, 1, keepdims=False).reshape(tm * shard, width)
    w_recv = exchange(w_send)
    first = core == 0
    w_block = jnp.concatenate(
        [jnp.where(first, w_keep, w_recv), jnp.where(first, w_recv, w_keep)], axis=0
    )
    w_mine = swap(jnp.broadcast_to(w_block[None], (group,) + w_block.shape).reshape(width, width), GROUP)
    w_other = exchange(w_mine)

    x_both = jnp.stack([x_own, exchange(x_own)])
    og_both = jnp.stack([og_own, exchange(og_own)])

    normed, mixed, d_packed = pl.pallas_call(
        functools.partial(attention_kernel, patches),
        out_shape=(
            jax.ShapeDtypeStruct((2, rows, width), bf16),
            jax.ShapeDtypeStruct((2, rows, HALF), bf16),
            jax.ShapeDtypeStruct((2, rows, 3 * HALF), bf16),
        ),
        compiler_params=vmem_params(),
        cost_estimate=pl.CostEstimate(flops=3 * 10**9, bytes_accessed=8 * 2**20, transcendentals=2**19),
        name="attention",
    )(x_both, og_both, gain_row, w_mine)

    grads = pl.pallas_call(
        gradient_kernel,
        out_shape=jax.ShapeDtypeStruct((width, 4 * HALF), bf16),
        compiler_params=vmem_params(),
        cost_estimate=pl.CostEstimate(flops=10**9, bytes_accessed=6 * 2**20, transcendentals=0),
        name="gradients",
    )(
        normed.reshape(2 * rows, width),
        og_both.reshape(2 * rows, width),
        d_packed.reshape(2 * rows, 3 * HALF),
        mixed.reshape(2 * rows, HALF),
    )
    dp_other = exchange(d_packed[1])
    mixed_other = exchange(mixed[1])

    grads = swap(grads, GROUP).reshape(group, 2, tm, shard, width)
    grads = jnp.sum(grads.astype(f32), axis=0)
    grads = grads.transpose(1, 0, 2, 3).reshape(tm, 2 * shard, width).astype(bf16)

    grad_in = pl.pallas_call(
        input_kernel,
        out_shape=jax.ShapeDtypeStruct((rows, width), bf16),
        compiler_params=vmem_params(),
        cost_estimate=pl.CostEstimate(flops=10**9, bytes_accessed=6 * 2**20, transcendentals=0),
        name="input_gradient",
    )(x_own, og_own, gain_row, d_packed[0], dp_other, w_mine, w_other)

    mixed_own = jnp.concatenate([mixed[0], mixed_other], axis=1)
    mixed_own = mixed_own.reshape(tm, frames, patches, 2 * HALF).transpose(0, 2, 1, 3)
    mixed_own = mixed_own.reshape(tm, patches, frames * 2 * HALF)
    sent = jnp.concatenate([grad_in.reshape(tm, per_peer, width), mixed_own, grads], axis=1)
    got = swap(sent.reshape(-1, width), TM).reshape(sent.shape)
    grad_in = got[:, :per_peer].reshape(tm, frames, patches, width).transpose(1, 0, 2, 3)
    grad_in = grad_in.reshape(frames_in.shape)
    mixed_home = got[:, per_peer : per_peer + patches].reshape(tm, patches, frames, 2 * HALF)
    mixed_home = mixed_home.transpose(2, 0, 1, 3).reshape(rows, 2 * HALF)
    result = pl.pallas_call(
        result_kernel,
        out_shape=jax.ShapeDtypeStruct((rows, width), bf16),
        compiler_params=vmem_params(),
        cost_estimate=pl.CostEstimate(flops=3 * 10**8, bytes_accessed=3 * 2**20, transcendentals=0),
        name="result",
    )(frames_in.reshape(rows, width), mixed_home, w_mine[:, 3 * HALF :], w_other[:, 3 * HALF :])

    total = jnp.sum(got[:, per_peer + patches :].astype(f32), axis=0).reshape(2, shard, width)
    keep = lax.dynamic_index_in_dim(total, core, 0, keepdims=False)
    recv = exchange(lax.dynamic_index_in_dim(total, 1 - core, 0, keepdims=False))
    low = jnp.where(first, keep, recv).reshape(shard, 4, 1, HALF)
    high = jnp.where(first, recv, keep).reshape(shard, 4, 1, HALF)
    whole = jnp.concatenate([low, high], axis=2)
    grad_qkv = whole[:, :3].reshape(shard, 6 * HALF)
    grad_out = whole[:, 3].reshape(shard, 2 * HALF).T
    own_row = lax.axis_index(DP + TM) * shard
    grad_gain = jnp.sum(w_qkv.astype(f32) * grad_qkv, axis=1) / lax.dynamic_slice_in_dim(gain, own_row, shard)
    return (result.reshape(frames_in.shape), grad_in, grad_qkv, grad_out, grad_gain)


def solution(mesh):
    fine = Mesh(mesh.devices.reshape(4, 2, 2, 2, 8), DP + TM)
    in_specs = (
        P(DP, TM, None, None),
        P(),
        P(DP + TM, None),
        P(None, DP + TM),
        P(DP, TM, None, None),
    )
    out_specs = (
        P(DP, TM, None, None),
        P(DP, TM, None, None),
        P(DP + TM, None),
        P(None, DP + TM),
        P(DP + TM),
    )
    return jax.shard_map(body, mesh=fine, in_specs=in_specs, out_specs=out_specs, check_vma=False)
```

time: 1640 us -> 176 us (0.11)
  waiting for transfers between devices: 1450 us -> 108 us
  blocking collectives: 76.5 us -> 0 us
  matrix products: 28.4 us -> 0 us
  local copies, waits for them, and re-layouts: 30.2 us -> 12.7 us
    all_gather x2 -> x0, waiting for transfers between devices: 1220 us -> none  [the longest x1 693 us: body(): qkv_full = lax.all_gather(w_qkv, ('dp', 'tm'), axis=0, tiled=True)]
    unnamed x4 -> x0, waiting for transfers between devices: 192 us -> none
    unnamed x1 -> x0, blocking collectives: 76.5 us -> none
    all_to_all x4, waiting for transfers between devices: 35.4 us -> 104 us  [swap(): return lax.all_to_all(value, axes, split_axis=0, concat_axis=0, tiled=True)]
    dot_general x11 -> x0, matrix products: 25.6 us -> none  [the longest x2 5.45 us: transposed_product(): lax.dot_general(left_rows, right_rows, (((0,), (0,)), ((), ())), preferre...]
  transfers between devices with their start and end apart: 7 -> 11, of which waited for: 6 -> 7; matrix products, arithmetic and copies ran while one was open for 2% -> 4% of each run, Pallas kernels for 0% -> 6%
where the time goes in v1:
time: 176 us
  waiting for transfers between devices  108 us (61%)
  starting transfers between devices  33 us (19%)
  Pallas kernels  15.1 us (9%)
  local copies, waits for them, and re-layouts  12.7 us (7%)
  other arithmetic  6.29 us (4%)
    all_to_all x4, waiting for transfers between devices, swap(): return lax.all_to_all(value, axes, split_axis=0, concat_axis=0, tiled=True)  104 us
    all_to_all x4, starting transfers between devices, swap(): return lax.all_to_all(value, axes, split_axis=0, concat_axis=0, tiled=True)  24.6 us
    ppermute x7, starting transfers between devices, exchange(): return lax.ppermute(value, 'core', [(0, 1), (1, 0)])  8.39 us
    pallas_call x1, Pallas kernels, body(): pl.pallas_call(functools.partial(attention_kernel, patches), out_shape=(j...  7.47 us
    pallas_call x1, Pallas kernels, body(): pl.pallas_call(input_kernel, out_shape=jax.ShapeDtypeStruct((rows, width)...  3.69 us
  transfers between devices with their start and end apart: 11, of which 7 were waited for; matrix products, arithmetic and copies ran while one was open for 4% of the time, Pallas kernels for 6%

profile of v1, /device:TPU:1, one launch (start us, length us, event | category | flops | bytes accessed | tf_op | source)
XLA Modules:
  0.0 175.8 jit_solution(4492127778883583270)
XLA Ops:
  0.6 0.0 copy-start
  0.6 0.8 reshape.133
  1.4 0.7 reshape.132
  2.2 0.0 copy-done
  2.2 1.1 copy_bitcast_fusion.1
  3.4 1.2 pad_maximum_fusion
  4.6 10.0 %all-to-all-start = ((bf16[16,40,1024]{2,1,0:T(8,128)(2,1)}), bf16[16,40,1024]{2,1,0:T(8,128)(2,1)S(1)}, u32[]{:S(2)}, u32[]{:S(2)}) async-start(bf16[16,40,1024]{2,1,0:T(8,128)(2,1)} %pad_maximum_fusion), calls=%async_computation | async-start | bytes 2621440 | tf_op jit(solution)/shard_map/all_to_all | solution.py:115
  14.6 30.7 %all-to-all-done = bf16[16,40,1024]{2,1,0:T(8,128)(2,1)S(1)} async-done(((bf16[16,40,1024]{2,1,0:T(8,128)(2,1)}), bf16[16,40,1024]{2,1,0:T(8,128)(2,1)S(1)}, u32[]{:S(2)}, u32[]{:S(2)}) %all-to-all-start) | async-done | bytes 1310752 | tf_op jit(solution)/shard_map/all_to_all | solution.py:115
  45.3 0.1 reshape.137
  45.4 0.1 constant_dynamic-slice_fusion.1
  45.6 2.9 %collective-permute-start.2 = (bf16[64,1024]{1,0:T(8,128)(2,1)S(1)}, bf16[64,1024]{1,0:T(8,128)(2,1)S(1)}, u32[]{:S(2)}, u32[]{:S(2)}) collective-permute-start(bf16[64,1024]{1,0:T(8,128)(2,1)S(1)} %reshape.139), channel_id=1, source_target_pairs={{0,16},{16,0},{1,17},{17,1},{2,18},{18,2},{3,19},{19,3},{4,20},{20... | collective-permute-start | bytes 393224 | tf_op jit(solution)/shard_map/ppermute | solution.py:111
  48.5 1.0 collective-permute-done.2
  49.5 1.6 broadcast_in_dim.15
  51.1 6.4 %all-to-all-start.1 = ((bf16[8,128,1024]{2,1,0:T(8,128)(2,1)}), bf16[8,128,1024]{2,1,0:T(8,128)(2,1)}, u32[]{:S(2)}, u32[]{:S(2)}) async-start(bf16[8,128,1024]{2,1,0:T(8,128)(2,1)} %broadcast_in_dim.15), calls=%async_computation.1 | async-start | bytes 4194304 | tf_op jit(solution)/shard_map/all_to_all | solution.py:115
  57.5 0.1 fusion
  57.5 0.7 collective-permute-start
  58.3 0.1 collective-permute-start.1
  58.4 1.4 collective-permute-done
  59.8 0.0 copy-start.5
  59.8 1.1 pad_maximum_fusion.1.x_ref
  60.9 0.0 collective-permute-done.1
  60.9 0.1 pad_maximum_fusion.2.og_ref
  61.0 24.4 %all-to-all-done.1 = bf16[8,128,1024]{2,1,0:T(8,128)(2,1)} async-done(((bf16[8,128,1024]{2,1,0:T(8,128)(2,1)}), bf16[8,128,1024]{2,1,0:T(8,128)(2,1)}, u32[]{:S(2)}, u32[]{:S(2)}) %all-to-all-start.1) | async-done | bytes 2097184 | tf_op jit(solution)/shard_map/all_to_all | solution.py:115
  85.4 1.6 collective-permute-start.4
  87.0 0.0 copy-done.5
  87.0 1.2 copy-done.4
  88.2 7.5 %attention.1 = (bf16[2,256,1024]{2,1,0:T(8,128)(2,1)S(1)}, bf16[2,256,256]{2,1,0:T(8,128)(2,1)S(1)}, bf16[2,256,768]{2,1,0:T(8,128)(2,1)S(1)}) custom-call(bf16[2,256,1024]{2,1,0:T(8,128)(2,1)S(1)} %copy-done.4, bf16[2,256,1024]{2,1,0:T(8,128)(2,1)S(1)} %pad_maximum_fusion.2.og_ref, f32[1,1024]{1,0:T(1,128)S(1)} %bitcast.84, ...), custom_call_target="tpu_custom_call" | custom-call | flops 3000000000 | bytes 8388608 | tf_op jit(solution)/shard_map/attention/pallas_call | solution.py:155
  95.7 0.0 copy-start.2
  95.7 2.7 %gradients.1 = bf16[1024,1024]{1,0:T(8,128)(2,1)} custom-call(bf16[512,1024]{1,0:T(8,128)(2,1)S(1)} %bitcast.81, bf16[512,1024]{1,0:T(8,128)(2,1)S(1)} %bitcast.77, bf16[512,768]{1,0:T(8,128)(2,1)S(1)} %bitcast.78, bf16[512,256]{1,0:T(8,128)(2,1)S(1)} %bitcast.82), custom_call_target="tpu_custom_call" | custom-call | flops 1000000000 | bytes 6291456 | tf_op jit(solution)/shard_map/gradients/pallas_call | solution.py:167
  98.4 0.0 copy-done.2
  98.4 4.5 %all-to-all-start.2 = ((bf16[8,128,1024]{2,1,0:T(8,128)(2,1)}), bf16[8,128,1024]{2,1,0:T(8,128)(2,1)}, u32[]{:S(2)}, u32[]{:S(2)}) async-start(bf16[8,128,1024]{2,1,0:T(8,128)(2,1)} %bitcast.29), calls=%async_computation.2 | async-start | bytes 4194304 | tf_op jit(solution)/shard_map/all_to_all | solution.py:115
  102.9 0.8 slice_bitcast_fusion.1
  103.7 0.0 collective-permute-start.3
  103.7 0.0 copy-done.3
  103.7 0.8 collective-permute-start.5
  104.5 1.1 collective-permute-done.5
  105.6 25.9 %all-to-all-done.2 = bf16[8,128,1024]{2,1,0:T(8,128)(2,1)} async-done(((bf16[8,128,1024]{2,1,0:T(8,128)(2,1)}), bf16[8,128,1024]{2,1,0:T(8,128)(2,1)}, u32[]{:S(2)}, u32[]{:S(2)}) %all-to-all-start.2) | async-done | bytes 2097184 | tf_op jit(solution)/shard_map/all_to_all | solution.py:115
  131.5 2.0 %reduce_sum.30 = bf16[128,1024]{1,0:T(8,128)(2,1)S(1)} reduce(bf16[8,128,1024]{2,1,0:T(8,128)(2,1)} %all-to-all-done.2, bf16[]{:T(256)} %constant.45.clone.1), dimensions={0}, to_apply=%region_0.1 | reduce | flops 917504 | bytes 2359298 | tf_op jit(solution)/shard_map/reduce_sum | solution.py:183
  133.5 0.1 convert_element_type.18
  133.6 0.1 copy.25
  133.7 0.2 copy.26
  133.8 0.0 collective-permute-done.3.dp_other_ref
  133.8 0.0 collective-permute-done.4.w_other_ref
  133.9 3.7 %input_gradient.1 = bf16[256,1024]{1,0:T(8,128)(2,1)S(1)} custom-call(bf16[256,1024]{1,0:T(8,128)(2,1)S(1)} %bitcast.76, bf16[256,1024]{1,0:T(8,128)(2,1)S(1)} %bitcast.73, f32[1,1024]{1,0:T(1,128)S(1)} %bitcast.85, bf16[256,768]{1,0:T(8,128)(2,1)S(1)} %get-tuple-element.14.dp_mine_ref, bf16[256,768]{1,0:T(8,128)(2,1)S(1)} %collective-permute-done.3.dp_other_ref, ...), custom_call_target="tpu_custom_call" | custom-call | flops 1000000000 | bytes 6291456 | tf_op jit(solution)/shard_map/input_gradient/pallas_call | solution.py:186
  137.6 1.1 pad_maximum_fusion.3
  138.6 3.7 %all-to-all-start.3 = ((bf16[16,32,1024]{2,1,0:T(8,128)(2,1)}), bf16[16,32,1024]{2,1,0:T(8,128)(2,1)S(1)}, u32[]{:S(2)}, u32[]{:S(2)}) async-start(bf16[16,32,1024]{2,1,0:T(8,128)(2,1)} %pad_maximum_fusion.3), calls=%async_computation.3 | async-start | bytes 2097152 | tf_op jit(solution)/shard_map/all_to_all | solution.py:115
  142.3 1.1 slice.60.w_mine_ref
  143.4 0.0 copy-start.1
  143.4 1.1 slice.61.w_other_ref
  144.6 23.3 %all-to-all-done.3 = bf16[16,32,1024]{2,1,0:T(8,128)(2,1)S(1)} async-done(((bf16[16,32,1024]{2,1,0:T(8,128)(2,1)}), bf16[16,32,1024]{2,1,0:T(8,128)(2,1)S(1)}, u32[]{:S(2)}, u32[]{:S(2)}) %all-to-all-start.3) | async-done | bytes 1048608 | tf_op jit(solution)/shard_map/all_to_all | solution.py:115
  167.8 0.9 reshape.146
  168.7 1.0 copy.27
  169.7 0.0 copy-start.7
  169.8 2.3 %collective-permute-start.6 = (f32[4,1024]{1,0:T(4,128)S(1)}, f32[4,1024]{1,0:T(4,128)S(1)}, u32[]{:S(2)}, u32[]{:S(2)}) collective-permute-start(f32[4,1024]{1,0:T(4,128)S(1)} %dynamic-slice_bitcast_fusion), channel_id=1, source_target_pairs={{0,16},{16,0},{1,17},{17,1},{2,18},{18,2},{3,19},{19,3},{4,20},{20... | collective-permute-start | bytes 49160 | tf_op jit(solution)/shard_map/ppermute | solution.py:111
  172.1 0.8 copy_bitcast_fusion
  173.0 0.0 copy-done.1
  173.0 1.3 result.1
  174.2 0.0 collective-permute-done.6
  174.4 0.0 copy-start.6
  174.4 0.6 copy.32
  175.0 0.0 copy-done.7
  175.0 0.1 multiply_reduce_fusion
  175.2 0.6 dynamic-slice_divide_fusion
  175.8 0.0 copy-done.6
  (27 shorter events, 0.5 us)
Async XLA Ops:
  0.6 1.6 copy-start
  4.6 40.8 %all-to-all-start = ((bf16[16,40,1024]{2,1,0:T(8,128)(2,1)}), bf16[16,40,1024]{2,1,0:T(8,128)(2,1)S(1)}, u32[]{:S(2)}, u32[]{:S(2)}) async-start(bf16[16,40,1024]{2,1,0:T(8,128)(2,1)} %pad_maximum_fusion), calls=%async_computation | async-start | bytes 2621440 | tf_op jit(solution)/shard_map/all_to_all | solution.py:115
  45.6 3.9 %collective-permute-start.2 = (bf16[64,1024]{1,0:T(8,128)(2,1)S(1)}, bf16[64,1024]{1,0:T(8,128)(2,1)S(1)}, u32[]{:S(2)}, u32[]{:S(2)}) collective-permute-start(bf16[64,1024]{1,0:T(8,128)(2,1)S(1)} %reshape.139), channel_id=1, source_target_pairs={{0,16},{16,0},{1,17},{17,1},{2,18},{18,2},{3,19},{19,3},{4,20},{20... | collective-permute-start | bytes 393224 | tf_op jit(solution)/shard_map/ppermute | solution.py:111
  51.1 34.3 %all-to-all-start.1 = ((bf16[8,128,1024]{2,1,0:T(8,128)(2,1)}), bf16[8,128,1024]{2,1,0:T(8,128)(2,1)}, u32[]{:S(2)}, u32[]{:S(2)}) async-start(bf16[8,128,1024]{2,1,0:T(8,128)(2,1)} %broadcast_in_dim.15), calls=%async_computation.1 | async-start | bytes 4194304 | tf_op jit(solution)/shard_map/all_to_all | solution.py:115
  57.5 2.3 %collective-permute-start = (bf16[256,1024]{1,0:T(8,128)(2,1)S(1)}, bf16[256,1024]{1,0:T(8,128)(2,1)S(1)}, u32[]{:S(2)}, u32[]{:S(2)}) collective-permute-start(bf16[256,1024]{1,0:T(8,128)(2,1)S(1)} %bitcast.74), channel_id=1, source_target_pairs={{0,16},{16,0},{1,17},{17,1},{2,18},{18,2},{3,19},{19,3},{4,20},{20... | collective-permute-start | bytes 1572872 | tf_op jit(solution)/shard_map/ppermute | solution.py:111
  58.3 2.6 %collective-permute-start.1 = (bf16[256,1024]{1,0:T(8,128)(2,1)S(1)}, bf16[256,1024]{1,0:T(8,128)(2,1)S(1)}, u32[]{:S(2)}, u32[]{:S(2)}) collective-permute-start(bf16[256,1024]{1,0:T(8,128)(2,1)S(1)} %bitcast.71), channel_id=1, source_target_pairs={{0,16},{16,0},{1,17},{17,1},{2,18},{18,2},{3,19},{19,3},{4,20},{20... | collective-permute-start | bytes 1572872 | tf_op jit(solution)/shard_map/ppermute | solution.py:111
  59.8 27.2 %copy-start.5 = (f32[1024]{0:T(1024)S(1)}, f32[1024]{0:T(1024)}, u32[]{:S(2)}) copy-start(f32[1024]{0:T(1024)} %param.6) | copy-start | bytes 12292
  85.4 48.4 %collective-permute-start.4 = (bf16[1024,1024]{1,0:T(8,128)(2,1)}, bf16[1024,1024]{1,0:T(8,128)(2,1)}, u32[]{:S(2)}, u32[]{:S(2)}) collective-permute-start(bf16[1024,1024]{1,0:T(8,128)(2,1)} %bitcast.16.w_ref.w_mine_ref), channel_id=1, source_target_pairs={{0,16},{16,0},{1,17},{17,1},{2,18},{18,2},{3,19},{19,3},{4,20},{20... | collective-permute-start | bytes 6291464 | tf_op jit(solution)/shard_map/ppermute | solution.py:111
  87.0 1.2 copy-start.4
  95.7 2.7 %copy-start.2 = (bf16[2,256,256]{2,1,0:T(8,128)(2,1)}, bf16[2,256,256]{2,1,0:T(8,128)(2,1)S(1)}, u32[]{:S(2)}) copy-start(bf16[2,256,256]{2,1,0:T(8,128)(2,1)S(1)} %get-tuple-element.9) | copy-start | bytes 786436
  98.4 5.3 %copy-start.3 = (bf16[2,256,256]{2,1,0:T(8,128)(2,1)S(1)}, bf16[2,256,256]{2,1,0:T(8,128)(2,1)}, u32[]{:S(2)}) copy-start(bf16[2,256,256]{2,1,0:T(8,128)(2,1)} %copy-done.2) | copy-start | bytes 786436
  98.4 33.1 %all-to-all-start.2 = ((bf16[8,128,1024]{2,1,0:T(8,128)(2,1)}), bf16[8,128,1024]{2,1,0:T(8,128)(2,1)}, u32[]{:S(2)}, u32[]{:S(2)}) async-start(bf16[8,128,1024]{2,1,0:T(8,128)(2,1)} %bitcast.29), calls=%async_computation.2 | async-start | bytes 4194304 | tf_op jit(solution)/shard_map/all_to_all | solution.py:115
  103.7 30.2 %collective-permute-start.3 = (bf16[256,768]{1,0:T(8,128)(2,1)}, bf16[256,768]{1,0:T(8,128)(2,1)S(1)}, u32[]{:S(2)}, u32[]{:S(2)}) collective-permute-start(bf16[256,768]{1,0:T(8,128)(2,1)} %get-tuple-element.13), channel_id=1, source_target_pairs={{0,16},{16,0},{1,17},{17,1},{2,18},{18,2},{3,19},{19,3},{4,20},{20... | collective-permute-start | bytes 1179656 | tf_op jit(solution)/shard_map/ppermute | solution.py:111
  103.7 1.9 %collective-permute-start.5 = (bf16[256,256]{1,0:T(8,128)(2,1)S(1)}, bf16[256,256]{1,0:T(8,128)(2,1)S(1)}, u32[]{:S(2)}, u32[]{:S(2)}) collective-permute-start(bf16[256,256]{1,0:T(8,128)(2,1)S(1)} %get-tuple-element.16), channel_id=1, source_target_pairs={{0,16},{16,0},{1,17},{17,1},{2,18},{18,2},{3,19},{19,3},{4,20},{20... | collective-permute-start | bytes 393224 | tf_op jit(solution)/shard_map/ppermute | solution.py:111
  138.6 29.2 %all-to-all-start.3 = ((bf16[16,32,1024]{2,1,0:T(8,128)(2,1)}), bf16[16,32,1024]{2,1,0:T(8,128)(2,1)S(1)}, u32[]{:S(2)}, u32[]{:S(2)}) async-start(bf16[16,32,1024]{2,1,0:T(8,128)(2,1)} %pad_maximum_fusion.3), calls=%async_computation.3 | async-start | bytes 2097152 | tf_op jit(solution)/shard_map/all_to_all | solution.py:115
  143.4 29.6 %copy-start.1 = (bf16[1,2,128,1024]{3,2,1,0:T(8,128)(2,1)S(1)}, bf16[1,2,128,1024]{3,2,1,0:T(8,128)(2,1)}, u32[]{:S(2)}) copy-start(bf16[1,2,128,1024]{3,2,1,0:T(8,128)(2,1)} %param.5) | copy-start | bytes 1572868
  169.7 5.3 %copy-start.7 = (bf16[4,1536]{1,0:T(4,128)(2,1)S(1)}, bf16[4,1536]{1,0:T(4,128)(2,1)}, u32[]{:S(2)}) copy-start(bf16[4,1536]{1,0:T(4,128)(2,1)} %param.7) | copy-start | bytes 36868
  169.8 4.4 %collective-permute-start.6 = (f32[4,1024]{1,0:T(4,128)S(1)}, f32[4,1024]{1,0:T(4,128)S(1)}, u32[]{:S(2)}, u32[]{:S(2)}) collective-permute-start(f32[4,1024]{1,0:T(4,128)S(1)} %dynamic-slice_bitcast_fusion), channel_id=1, source_target_pairs={{0,16},{16,0},{1,17},{17,1},{2,18},{18,2},{3,19},{19,3},{4,20},{20... | collective-permute-start | bytes 49160 | tf_op jit(solution)/shard_map/ppermute | solution.py:111
  174.4 1.4 copy-start.6

commit v2 on v1

v2 whole, which is shorter than its diff:
```python
import functools

import jax
import jax.numpy as jnp
from jax import lax
from jax.experimental import pallas as pl
from jax.experimental.pallas import tpu as pltpu
from jax.sharding import Mesh, PartitionSpec as P

DP = ("y", "xh", "core")
TM = ("xl", "z")
Y_SIZE, XH_SIZE, TM_SIZE = 4, 2, 16

D = 1024
DH = 64
HALF = 256
norm_eps = 1e-05
f32 = jnp.float32
bf16 = jnp.bfloat16

NN = (((1,), (0,)), ((), ()))
NT = (((1,), (1,)), ((), ()))
TN = (((0,), (0,)), ((), ()))

SMEM = pl.BlockSpec(memory_space=pltpu.SMEM)
VMEM = pl.BlockSpec(memory_space=pltpu.VMEM)
HBM = pl.BlockSpec(memory_space=pl.ANY)


def mm(a, b, dims):
    return lax.dot_general(a, b, dims, preferred_element_type=f32)


def layer_stats(features):
    wide = features.astype(f32)
    centred = wide - jnp.mean(wide, axis=-1, keepdims=True)
    inv_std = lax.rsqrt(jnp.mean(centred * centred, axis=-1, keepdims=True) + norm_eps)
    return centred * inv_std, inv_std


def attend(pair, same, low_half, packed, d_mixed):
    lo = pair * 2 * DH
    query = packed[:, lo : lo + 2 * DH]
    keys = packed[:, HALF + lo : HALF + lo + 2 * DH]
    values = packed[:, 2 * HALF + lo : 2 * HALF + lo + 2 * DH]
    d_heads = d_mixed[:, lo : lo + 2 * DH]
    zero = jnp.zeros_like(query)
    parts = []
    for own in (low_half, jnp.logical_not(low_half)):
        scores = mm(jnp.where(own, query * DH ** (-0.5), zero), keys, NT)
        scores = jnp.where(same, scores, -1e30)
        expo = jnp.exp(scores - jnp.max(scores, axis=-1, keepdims=True))
        prob = expo * (1.0 / jnp.sum(expo, axis=-1, keepdims=True))
        prob_low = prob.astype(bf16)
        mixed = mm(prob_low, values, NN)
        d_prob = mm(jnp.where(own, d_heads, zero), values, NT)
        d_values = mm(prob_low, d_heads, TN)
        inner = jnp.sum(d_prob * prob, axis=-1, keepdims=True)
        d_scores = (prob * (d_prob - inner)).astype(bf16)
        d_query = mm(d_scores, keys, NN) * DH ** (-0.5)
        d_keys = mm(d_scores, query, TN) * DH ** (-0.5)
        parts.append((mixed, d_query, d_keys, d_values))
    return [jnp.where(low_half, a, b).astype(bf16) for a, b in zip(*parts)]


def pack_weights_kernel(w_qkv_ref, w_out_ref, out_ref):
    qkv, out = w_qkv_ref[...].astype(f32), w_out_ref[...].astype(f32)
    halves = []
    for half in range(2):
        parts = [qkv[:, (2 * part + half) * HALF : (2 * part + half + 1) * HALF] for part in range(3)]
        halves.append(jnp.concatenate(parts + [out[:, half * HALF : (half + 1) * HALF]], axis=1))
    both = jnp.concatenate(halves, axis=0)
    out_ref[...] = jnp.broadcast_to(both[None], out_ref.shape).astype(bf16)


def fetch(pairs, sems, first=0):
    copies = [pltpu.make_async_copy(src, dst, sems.at[first + i]) for i, (src, dst) in enumerate(pairs)]
    for copy in copies:
        copy.start()
    return copies


def wait_all(copies):
    for copy in copies:
        copy.wait()


def sample(patches, got, gain_ref, weights, normed, mixed, dpacked, before_weights, after_weights):
    rows = normed.shape[0]
    row_patch = lax.broadcasted_iota(jnp.int32, (rows, rows), 0) % patches
    col_patch = lax.broadcasted_iota(jnp.int32, (rows, rows), 1) % patches
    same = row_patch == col_patch
    low_half = lax.broadcasted_iota(jnp.int32, (rows, 2 * DH), 1) < DH
    per_peer = got.shape[1] // 2
    normal_x, _ = layer_stats(got[:, :per_peer, :].reshape(rows, D))
    normed[...] = (normal_x * gain_ref[...]).astype(bf16)
    before_weights()
    packed = mm(normed[...], weights[:, : 3 * HALF], NN).astype(bf16)
    d_mixed = mm(got[:, per_peer:, :].reshape(rows, D), weights[:, 3 * HALF :], NN).astype(bf16)
    after_weights()
    for pair in range(HALF // (2 * DH)):
        lo = pair * 2 * DH
        outs = attend(pair, same, low_half, packed, d_mixed)
        mixed[:, lo : lo + 2 * DH] = outs[0]
        for part in range(3):
            at = part * HALF + lo
            dpacked[:, at : at + 2 * DH] = outs[1 + part]


def own_kernel(patches, place_ref, got_ref, gain_ref, *refs):
    pieces, (w_out_ref, normed_ref, mixed_ref, dpacked_ref) = refs[:8], refs[8:12]
    got, weights, normed, mixed, dpacked, sems = refs[12:]
    (copy_got,) = fetch([(got_ref, got)], sems)
    block = pieces[0].shape[0]
    starts = [pl.multiple_of(place_ref[i] * block, block) for i in range(8)]
    copies = fetch([(p, weights.at[pl.ds(at, block), :]) for p, at in zip(pieces, starts)], sems, 1)
    results = []

    def before_weights():
        results.extend(fetch([(normed, normed_ref)], sems, 9))
        wait_all(copies)

    def after_weights():
        results.extend(fetch([(weights, w_out_ref)], sems, 10))

    copy_got.wait()
    sample(patches, got, gain_ref, weights, normed, mixed, dpacked, before_weights, after_weights)
    results.extend(fetch([(mixed, mixed_ref), (dpacked, dpacked_ref)], sems, 11))
    wait_all(results)


def other_kernel(patches, place_ref, got_own_ref, got_ref, gain_ref, w_ref, *refs):
    (normed_ref, mixed_ref, dpacked_ref, mixed_out_ref, dpacked_out_ref), outs = refs[:5], refs[5:13]
    got, weights, og, normed, mixed, dpacked, grads, own, peers, sems = refs[13:]
    per_peer = og.shape[2]
    copies = fetch(
        [
            (got_ref, got),
            (w_ref, weights),
            (got_own_ref.at[:, per_peer:, :], og.at[0]),
            (normed_ref, normed.at[0]),
            (mixed_ref, mixed.at[0]),
            (dpacked_ref, dpacked.at[0]),
        ],
        sems,
    )

    def before_weights():
        wait_all(copies[1:])

    def after_weights():
        og[1] = got[:, per_peer:, :]

    copies[0].wait()
    sample(patches, got, gain_ref, weights, normed.at[1], mixed.at[1], dpacked.at[1], before_weights, after_weights)
    results = fetch([(mixed.at[1], mixed_out_ref), (dpacked.at[1], dpacked_out_ref)], sems)
    rows = normed.shape[1]
    block = own.shape[1]
    pair_rows = 2 * block
    all_dpacked = dpacked[...].reshape(2 * rows, 3 * HALF)
    all_mixed = mixed[...].reshape(2 * rows, HALF)
    for step in (1, 2, 3, 0):
        columns = pl.ds(pl.multiple_of(place_ref[8 + step] * pair_rows, pair_rows), pair_rows)
        grads[:, : 3 * HALF] = mm(normed[:, :, columns].reshape(2 * rows, pair_rows), all_dpacked, TN)
        grads[:, 3 * HALF :] = mm(og[:, :, :, columns].reshape(2 * rows, pair_rows), all_mixed, TN)
        for side in range(XH_SIZE):
            start = pl.multiple_of(place_ref[12 + side] * block, block)
            slot = own.at[side] if step == 0 else peers.at[side * (Y_SIZE - 1) + step - 1]
            slot[...] = grads[pl.ds(start, block), :].astype(slot.dtype)
            results += fetch([(slot, outs[side * Y_SIZE + step])], sems, 4 + len(results))
    wait_all(results)


def input_kernel(*refs):
    sources, (gain_ref, out_ref), scratch = refs[:7], refs[7:9], refs[9:]
    got, dp_mine, dp_other, mixed, mixed_other, w_mine, w_other, sems = scratch
    copies = fetch(
        [
            (sources[0], got),
            (sources[1], dp_mine),
            (sources[2], dp_other),
            (sources[3], mixed),
            (sources[4], mixed_other),
            (sources[5].at[:, : 3 * HALF], w_mine),
            (sources[6].at[:, : 3 * HALF], w_other),
        ],
        sems,
    )
    rows = dp_other.shape[0]
    per_peer = got.shape[1] // 2
    copies[0].wait()
    normal_x, inv_std = layer_stats(got[:, :per_peer, :].reshape(rows, D))
    wait_all(copies[1:])
    d_normed = mm(dp_mine[...], w_mine[...], NT) + mm(dp_other[...], w_other[...], NT)
    d_normed = d_normed.astype(bf16).astype(f32)
    scaled = d_normed * gain_ref[...]
    d_input = inv_std * (
        scaled
        - jnp.mean(scaled, axis=-1, keepdims=True)
        - normal_x * jnp.mean(scaled * normal_x, axis=-1, keepdims=True)
    )
    og = got[:, per_peer:, :].reshape(rows, D).astype(f32)
    grad_in = (og + d_input).astype(bf16)
    peers = got.shape[0]
    out_ref[:, :per_peer, :] = grad_in[:, : D // 2].reshape(peers, per_peer, D // 2)
    out_ref[:, per_peer : 2 * per_peer, :] = grad_in[:, D // 2 :].reshape(peers, per_peer, D // 2)
    out_ref[:, 2 * per_peer :, :HALF] = mixed[...].reshape(peers, per_peer, HALF)
    out_ref[:, 2 * per_peer :, HALF:] = mixed_other[...].reshape(peers, per_peer, HALF)


def sum_kernel(own_ref, a_ref, b_ref, c_ref, across_ref, out_ref):
    total = own_ref[...] + a_ref[...].astype(f32) + b_ref[...].astype(f32) + c_ref[...].astype(f32)
    total = total + across_ref[...].astype(f32)
    shard = 4
    low, high = (total.reshape(2, -1, 2 * shard, D)[core] for core in range(2))
    top = lax.broadcasted_iota(jnp.int32, low.shape, 1) < shard
    even = jnp.where(top, low, pltpu.roll(high, shard, 1))
    odd = jnp.where(top, pltpu.roll(low, shard, 1), high)
    out_ref[...] = jnp.stack([even, odd], axis=1).reshape(out_ref.shape).astype(bf16)


def home_kernel(got_ref, x_ref, w_mine_ref, w_other_ref, result_ref, grad_ref, got, x, w_mine, w_other, result, grad, sems):
    output = slice(3 * HALF, 4 * HALF)
    wait_all(
        fetch(
            [(got_ref, got), (x_ref, x), (w_mine_ref.at[:, output], w_mine), (w_other_ref.at[:, output], w_other)],
            sems,
        )
    )
    peers, _, width = got.shape
    frames, count, _ = x.shape
    patches = count // peers
    per_peer = frames * patches

    def by_frame(part):
        wide = got[:, part * per_peer : (part + 1) * per_peer, :].astype(f32)
        wide = wide.reshape(peers, frames, patches, width)
        return [wide[:, f].reshape(count, width).astype(bf16) for f in range(frames)]

    low, high, heads = by_frame(0), by_frame(1), by_frame(2)
    for f in range(frames):
        grad[f, :, :width] = low[f]
        grad[f, :, width:] = high[f]
    results = fetch([(grad, grad_ref)], sems)
    for f in range(frames):
        projected = mm(heads[f][:, :HALF], w_mine[...], NT) + mm(heads[f][:, HALF:], w_other[...], NT)
        result[f] = (x[f].astype(f32) + projected).astype(bf16)
    wait_all(results + fetch([(result, result_ref)], sems, 1))


def vmem_params():
    return pltpu.CompilerParams(vmem_limit_bytes=60 * 1024 * 1024)


def exchange(value):
    return lax.ppermute(value, "core", [(0, 1), (1, 0)])


def swap(value, axes):
    return lax.all_to_all(value, axes, split_axis=0, concat_axis=0, tiled=True)


def along_y(value, step):
    return lax.ppermute(value, "y", [(i, (i + step) % Y_SIZE) for i in range(Y_SIZE)])


def across_x(value):
    return lax.ppermute(value, "xh", [(0, 1), (1, 0)])


def body(frames_in, gain, w_qkv, w_out, out_grad):
    _, frames, patch_count, width = frames_in.shape
    tm = TM_SIZE
    patches = patch_count // tm
    per_peer = frames * patches
    rows = tm * per_peer
    shard = w_qkv.shape[0]
    core = lax.axis_index("core")
    first = core == 0
    y, xh = lax.axis_index("y"), lax.axis_index("xh")
    gain_row = gain.reshape(1, width)

    def by_patch(value):
        value = value.reshape(frames, tm, patches, width).transpose(1, 0, 2, 3)
        return value.reshape(tm, per_peer, width)

    w_parts = pl.pallas_call(
        pack_weights_kernel,
        out_shape=jax.ShapeDtypeStruct((tm, 2 * shard, width), bf16),
        in_specs=[VMEM] * 2,
        compiler_params=vmem_params(),
        cost_estimate=pl.CostEstimate(flops=0, bytes_accessed=2**18, transcendentals=0),
        name="pack_weights",
    )(w_qkv, w_out.T)
    w_got = swap(w_parts.reshape(-1, width), TM).reshape(tm, 2, shard, width)

    w_keep = lax.dynamic_index_in_dim(w_got, core, 1, keepdims=False).reshape(tm * shard, width)
    w_send = lax.dynamic_index_in_dim(w_got, 1 - core, 1, keepdims=False).reshape(tm * shard, width)
    w_recv = exchange(w_send)
    w_block = jnp.concatenate(
        [jnp.where(first, w_keep, w_recv), jnp.where(first, w_recv, w_keep)], axis=0
    )
    block = w_block.shape[0]

    sent = jnp.concatenate([by_patch(frames_in), by_patch(out_grad)], axis=1)
    sent, w_block = lax.optimization_barrier((sent, w_block))
    got = swap(sent.reshape(-1, width), TM).reshape(tm, 2 * per_peer, width)

    pieces, places = [], []
    for side, part in enumerate((w_block, across_x(w_block))):
        for step in range(Y_SIZE):
            pieces.append(part if step == 0 else along_y(part, step))
            places.append(((y + Y_SIZE - step) % Y_SIZE) * 2 + (xh ^ side))
    places += [(y + step) % Y_SIZE for step in range(Y_SIZE)] + [xh, xh ^ 1]
    place = jnp.stack(places).astype(jnp.int32)
    got, *pieces = lax.optimization_barrier((got, *pieces))
    got_other = exchange(got)

    shape = jax.ShapeDtypeStruct
    sample_shapes = (shape((rows, HALF), bf16), shape((rows, 3 * HALF), bf16))
    w_mine, normed, mixed, d_packed = pl.pallas_call(
        functools.partial(own_kernel, patches),
        in_specs=[SMEM, HBM, VMEM] + [HBM] * 8,
        out_specs=(HBM,) * 4,
        out_shape=(shape((width, width), bf16), shape((rows, width), bf16)) + sample_shapes,
        scratch_shapes=[
            pltpu.VMEM(got.shape, bf16),
            pltpu.VMEM((width, width), bf16),
            pltpu.VMEM((rows, width), bf16),
            pltpu.VMEM((rows, HALF), bf16),
            pltpu.VMEM((rows, 3 * HALF), bf16),
            pltpu.SemaphoreType.DMA((13,)),
        ],
        compiler_params=vmem_params(),
        cost_estimate=pl.CostEstimate(flops=2 * 10**9, bytes_accessed=6 * 2**20, transcendentals=2**18),
        name="own_sample",
    )(place, got, gain_row, *pieces)
    w_mine, got_other = lax.optimization_barrier((w_mine, got_other))
    w_other = exchange(w_mine)

    half_shape, own_shape = shape((block, width), bf16), shape((block, width), f32)
    mixed_2, d_packed_2, *grad_pieces = pl.pallas_call(
        functools.partial(other_kernel, patches),
        in_specs=[SMEM, HBM, HBM, VMEM] + [HBM] * 4,
        out_specs=(HBM,) * 10,
        out_shape=sample_shapes + ((own_shape,) + (half_shape,) * (Y_SIZE - 1)) * 2,
        scratch_shapes=[
            pltpu.VMEM(got.shape, bf16),
            pltpu.VMEM((width, width), bf16),
            pltpu.VMEM((2, tm, per_peer, width), bf16),
            pltpu.VMEM((2, rows, width), bf16),
            pltpu.VMEM((2, rows, HALF), bf16),
            pltpu.VMEM((2, rows, 3 * HALF), bf16),
            pltpu.VMEM((2 * block, width), f32),
            pltpu.VMEM((2, block, width), f32),
            pltpu.VMEM((6, block, width), bf16),
            pltpu.SemaphoreType.DMA((16,)),
        ],
        compiler_params=vmem_params(),
        cost_estimate=pl.CostEstimate(flops=3 * 10**9, bytes_accessed=10 * 2**20, transcendentals=2**18),
        name="other_sample",
    )(place, got, got_other, gain_row, w_mine, normed, mixed, d_packed)
    dp_other = exchange(d_packed_2)
    mixed_other = exchange(mixed_2)

    received = [along_y(grad_pieces[Y_SIZE + step], step) for step in range(1, Y_SIZE)]
    partial = grad_pieces[Y_SIZE] + sum(piece.astype(f32) for piece in received)
    received = [along_y(grad_pieces[step], step) for step in range(1, Y_SIZE)]
    grads = pl.pallas_call(
        sum_kernel,
        in_specs=[VMEM] * 5,
        out_shape=shape((tm, 2 * shard, width), bf16),
        compiler_params=vmem_params(),
        cost_estimate=pl.CostEstimate(flops=10000000000, bytes_accessed=2 * 2**20, transcendentals=0),
        name="sum_blocks",
    )(grad_pieces[0], *received, across_x(partial.astype(bf16)))

    sent = pl.pallas_call(
        input_kernel,
        out_shape=shape((tm, 3 * per_peer, width // 2), bf16),
        in_specs=[HBM] * 7 + [VMEM],
        scratch_shapes=[
            pltpu.VMEM(got.shape, bf16),
            pltpu.VMEM((rows, 3 * HALF), bf16),
            pltpu.VMEM((rows, 3 * HALF), bf16),
            pltpu.VMEM((rows, HALF), bf16),
            pltpu.VMEM((rows, HALF), bf16),
            pltpu.VMEM((width, 3 * HALF), bf16),
            pltpu.VMEM((width, 3 * HALF), bf16),
            pltpu.SemaphoreType.DMA((7,)),
        ],
        compiler_params=vmem_params(),
        cost_estimate=pl.CostEstimate(flops=10**9, bytes_accessed=6 * 2**20, transcendentals=0),
        name="input_gradient",
    )(got, d_packed, dp_other, mixed, mixed_other, w_mine, w_other, gain_row)
    got = swap(sent.reshape(-1, width // 2), TM).reshape(sent.shape)
    grads, got = lax.optimization_barrier((grads, got))
    local = shape(frames_in.shape[1:], bf16)
    result, grad_in = pl.pallas_call(
        home_kernel,
        in_specs=[HBM] * 4,
        out_specs=(HBM,) * 2,
        out_shape=(local,) * 2,
        scratch_shapes=[
            pltpu.VMEM(sent.shape, bf16),
            pltpu.VMEM(local.shape, bf16),
            pltpu.VMEM((width, HALF), bf16),
            pltpu.VMEM((width, HALF), bf16),
            pltpu.VMEM(local.shape, bf16),
            pltpu.VMEM(local.shape, bf16),
            pltpu.SemaphoreType.DMA((4,)),
        ],
        compiler_params=vmem_params(),
        cost_estimate=pl.CostEstimate(flops=3 * 10**8, bytes_accessed=4 * 2**20, transcendentals=0),
        name="home",
    )(got, frames_in[0], w_mine, w_other)

    grads = swap(grads.reshape(-1, width), TM)
    grads, result, grad_in = lax.optimization_barrier((grads, result, grad_in))
    total = jnp.sum(grads.reshape(tm, 2, shard, width).astype(f32), axis=0)
    keep = lax.dynamic_index_in_dim(total, core, 0, keepdims=False)
    recv = exchange(lax.dynamic_index_in_dim(total, 1 - core, 0, keepdims=False))
    low = jnp.where(first, keep, recv).reshape(shard, 4, 1, HALF)
    high = jnp.where(first, recv, keep).reshape(shard, 4, 1, HALF)
    whole = jnp.concatenate([low, high], axis=2)
    grad_qkv = whole[:, :3].reshape(shard, 6 * HALF)
    grad_out = whole[:, 3].reshape(shard, 2 * HALF).T
    own_row = lax.axis_index(DP + TM) * shard
    grad_gain = jnp.sum(w_qkv.astype(f32) * grad_qkv, axis=1) / lax.dynamic_slice_in_dim(gain, own_row, shard)
    return (result[None], grad_in[None], grad_qkv, grad_out, grad_gain)


def solution(mesh):
    fine = Mesh(mesh.devices.reshape(Y_SIZE, XH_SIZE, 2, 2, 8), DP + TM)
    in_specs = (
        P(DP, TM, None, None),
        P(),
        P(DP + TM, None),
        P(None, DP + TM),
        P(DP, TM, None, None),
    )
    out_specs = (
        P(DP, TM, None, None),
        P(DP, TM, None, None),
        P(DP + TM, None),
        P(None, DP + TM),
        P(DP + TM),
    )
    return jax.shard_map(body, mesh=fine, in_specs=in_specs, out_specs=out_specs, check_vma=False)
```

time: 176 us -> 142 us (0.81)
  waiting for transfers between devices: 108 us -> 45.6 us
  starting transfers between devices: 33 us -> 56 us
  Pallas kernels: 15.1 us -> 27.1 us
  local copies, waits for them, and re-layouts: 12.7 us -> 7.71 us
  other arithmetic: 6.29 us -> 3.73 us
    all_to_all x4, waiting for transfers between devices: 104 us -> 11.9 us  [swap(): return lax.all_to_all(value, axes, split_axis=0, concat_axis=0, tiled=True)]
    ppermute x0 -> x14, waiting for transfers between devices: none -> 32.7 us  [the longest x12 21.3 us: along_y(): lax.ppermute(value, 'y', [(i, (i + step) % Y_SIZE) for i in range(Y_SIZE)])]
    ppermute x0 -> x14, starting transfers between devices: none -> 19 us  [the longest x12 14.7 us: along_y(): lax.ppermute(value, 'y', [(i, (i + step) % Y_SIZE) for i in range(Y_SIZE)])]
    pallas_call x4 -> x6, Pallas kernels: 15.1 us -> 27.1 us  [the longest x1 8.42 us: body(): pl.pallas_call(functools.partial(other_kernel, patches), in_specs=[SMEM,...]
    all_to_all x4, starting transfers between devices: 24.6 us -> 29.2 us  [swap(): return lax.all_to_all(value, axes, split_axis=0, concat_axis=0, tiled=True)]
    unnamed x19 -> x45, local copies, waits for them, and re-layouts: 1.88 us -> 5.43 us
    reshape x8 -> x1, local copies, waits for them, and re-layouts: 3.33 us -> 0.1 us  [body(): w_got = swap(w_parts.reshape(-1, width), TM).reshape(tm, 2, shard, width)]
    ppermute x7 -> x6, waiting for transfers between devices: 3.51 us -> 0.92 us  [exchange(): return lax.ppermute(value, 'core', [(0, 1), (1, 0)])]
  transfers between devices with their start and end apart: 11 -> 24, of which waited for: 7 -> 13; matrix products, arithmetic and copies ran while one was open for 4% -> 3% of each run, Pallas kernels for 6% -> 18%
where the time goes in v2:
time: 142 us; the launch traced here: 141 us
  starting transfers between devices  56 us (39%)
  waiting for transfers between devices  45.6 us (32%)
  Pallas kernels  27.1 us (19%)
  local copies, waits for them, and re-layouts  7.71 us (5%)
  other arithmetic  3.73 us (3%)
    all_to_all x4, starting transfers between devices, swap(): return lax.all_to_all(value, axes, split_axis=0, concat_axis=0, tiled=True)  29.2 us
    ppermute x12, waiting for transfers between devices, along_y(): lax.ppermute(value, 'y', [(i, (i + step) % Y_SIZE) for i in range(Y_SIZE)])  21.3 us
    ppermute x12, starting transfers between devices, along_y(): lax.ppermute(value, 'y', [(i, (i + step) % Y_SIZE) for i in range(Y_SIZE)])  14.7 us
    all_to_all x4, waiting for transfers between devices, swap(): return lax.all_to_all(value, axes, split_axis=0, concat_axis=0, tiled=True)  11.9 us
    ppermute x2, waiting for transfers between devices, across_x(): return lax.ppermute(value, 'xh', [(0, 1), (1, 0)])  11.5 us
    pallas_call x1, Pallas kernels, body(): pl.pallas_call(functools.partial(other_kernel, patches), in_specs=[SMEM,...  8.42 us
    ppermute x6, starting transfers between devices, exchange(): return lax.ppermute(value, 'core', [(0, 1), (1, 0)])  7.72 us
    pallas_call x1, Pallas kernels, body(): pl.pallas_call(functools.partial(own_kernel, patches), in_specs=[SMEM, HB...  6.15 us
  transfers between devices with their start and end apart: 24, of which 13 were waited for; matrix products, arithmetic and copies ran while one was open for 3% of the time, Pallas kernels for 18%

profile of v2, /device:TPU:1, one launch (start us, length us, event | category | flops | bytes accessed | tf_op | source)
XLA Modules:
  0.0 141.1 jit_solution(17763051802657291833)
XLA Ops:
  0.6 0.0 copy-start
  0.6 1.5 %pack_weights.1 = bf16[16,8,1024]{2,1,0:T(8,128)(2,1)} custom-call(bf16[4,1536]{1,0:T(4,128)(2,1)} %w_qkv_ref.1, bf16[4,512]{1,0:T(4,128)(2,1)} %bitcast.64), custom_call_target="tpu_custom_call" | custom-call | bytes 262144 | tf_op jit(solution)/shard_map/pack_weights/pallas_call | solution.py:287
  2.1 10.0 %all-to-all-start = ((bf16[16,8,1024]{2,1,0:T(8,128)(2,1)}), bf16[16,8,1024]{2,1,0:T(8,128)(2,1)S(1)}, u32[]{:S(2)}, u32[]{:S(2)}) async-start(bf16[16,8,1024]{2,1,0:T(8,128)(2,1)} %pack_weights.1), calls=%async_computation | async-start | bytes 524288 | tf_op jit(solution)/shard_map/all_to_all | solution.py:260
  12.2 1.1 copy_bitcast_fusion
  13.4 7.6 %all-to-all-done = bf16[16,8,1024]{2,1,0:T(8,128)(2,1)S(1)} async-done(((bf16[16,8,1024]{2,1,0:T(8,128)(2,1)}), bf16[16,8,1024]{2,1,0:T(8,128)(2,1)S(1)}, u32[]{:S(2)}, u32[]{:S(2)}) %all-to-all-start) | async-done | bytes 262176 | tf_op jit(solution)/shard_map/all_to_all | solution.py:260
  20.9 0.1 reshape.73
  21.0 0.1 dynamic-slice_bitcast_fusion.1
  21.2 2.4 %collective-permute-start = (bf16[64,1024]{1,0:T(8,128)(2,1)S(1)}, bf16[64,1024]{1,0:T(8,128)(2,1)S(1)}, u32[]{:S(2)}, u32[]{:S(2)}) collective-permute-start(bf16[64,1024]{1,0:T(8,128)(2,1)S(1)} %reshape.75), channel_id=1, source_target_pairs={{0,16},{16,0},{1,17},{17,1},{2,18},{18,2},{3,19},{19,3},{4,20},{20... | collective-permute-start | bytes 393224 | tf_op jit(solution)/shard_map/ppermute | solution.py:256
  23.6 1.1 pad_maximum_fusion
  24.7 0.0 collective-permute-done
  24.8 0.0 copy-start.6
  24.8 4.2 %all-to-all-start.1 = ((bf16[16,32,1024]{2,1,0:T(8,128)(2,1)}), bf16[16,32,1024]{2,1,0:T(8,128)(2,1)S(1)}, u32[]{:S(2)}, u32[]{:S(2)}) async-start(bf16[16,32,1024]{2,1,0:T(8,128)(2,1)} %pad_maximum_fusion), calls=%async_computation.1 | async-start | bytes 2097152 | tf_op jit(solution)/shard_map/all_to_all | solution.py:260
  29.1 2.5 %collective-permute-start.4 = (bf16[128,1024]{1,0:T(8,128)(2,1)S(1)}, bf16[128,1024]{1,0:T(8,128)(2,1)S(1)}, u32[]{:S(2)}, u32[]{:S(2)}) collective-permute-start(bf16[128,1024]{1,0:T(8,128)(2,1)S(1)} %pad_maximum_fusion.1.refs_0_), channel_id=1, source_target_pairs={{0,32},{32,0},{1,33},{33,1},{2,34},{34,2},{3,35},{35,3},{4,36},{36... | collective-permute-start | bytes 786440 | tf_op jit(solution)/shard_map/ppermute | solution.py:268
  31.6 2.7 %collective-permute-start.3 = (bf16[128,1024]{1,0:T(8,128)(2,1)S(1)}, bf16[128,1024]{1,0:T(8,128)(2,1)S(1)}, u32[]{:S(2)}, u32[]{:S(2)}) collective-permute-start(bf16[128,1024]{1,0:T(8,128)(2,1)S(1)} %pad_maximum_fusion.1.refs_0_), channel_id=1, source_target_pairs={{0,192},{64,0},{128,64},{192,128},{1,193},{65,1},{129,65},{193,129... | collective-permute-start | bytes 786440 | tf_op jit(solution)/shard_map/ppermute | solution.py:264
  34.3 0.3 collective-permute-start.2
  34.7 0.7 collective-permute-start.1
  35.4 7.5 %collective-permute-done.4.refs_4_ = bf16[128,1024]{1,0:T(8,128)(2,1)S(1)} collective-permute-done((bf16[128,1024]{1,0:T(8,128)(2,1)S(1)}, bf16[128,1024]{1,0:T(8,128)(2,1)S(1)}, u32[]{:S(2)}, u32[]{:S(2)}) %collective-permute-start.4) | collective-permute-done | bytes 262176 | tf_op jit(solution)/shard_map/ppermute | solution.py:268
  42.9 2.7 %collective-permute-start.7 = (bf16[128,1024]{1,0:T(8,128)(2,1)S(1)}, bf16[128,1024]{1,0:T(8,128)(2,1)S(1)}, u32[]{:S(2)}, u32[]{:S(2)}) collective-permute-start(bf16[128,1024]{1,0:T(8,128)(2,1)S(1)} %collective-permute-done.4.refs_4_), channel_id=1, source_target_pairs={{0,192},{64,0},{128,64},{192,128},{1,193},{65,1},{129,65},{193,129... | collective-permute-start | bytes 786440 | tf_op jit(solution)/shard_map/ppermute | solution.py:264
  45.6 0.3 collective-permute-start.6
  46.0 0.7 collective-permute-start.5
  46.7 3.0 %collective-permute-done.1.refs_1_ = bf16[128,1024]{1,0:T(8,128)(2,1)S(1)} collective-permute-done((bf16[128,1024]{1,0:T(8,128)(2,1)S(1)}, bf16[128,1024]{1,0:T(8,128)(2,1)S(1)}, u32[]{:S(2)}, u32[]{:S(2)}) %collective-permute-start.1) | collective-permute-done | bytes 262176 | tf_op jit(solution)/shard_map/ppermute | solution.py:264
  49.7 1.3 collective-permute-done.7.refs_7_
  51.0 2.5 %collective-permute-done.6.refs_6_ = bf16[128,1024]{1,0:T(8,128)(2,1)S(1)} collective-permute-done((bf16[128,1024]{1,0:T(8,128)(2,1)S(1)}, bf16[128,1024]{1,0:T(8,128)(2,1)S(1)}, u32[]{:S(2)}, u32[]{:S(2)}) %collective-permute-start.6) | collective-permute-done | bytes 262176 | tf_op jit(solution)/shard_map/ppermute | solution.py:264
  53.5 0.7 copy-done.16
  54.2 6.9 %collective-permute-done.5.refs_5_ = bf16[128,1024]{1,0:T(8,128)(2,1)} collective-permute-done((bf16[128,1024]{1,0:T(8,128)(2,1)S(1)}, bf16[128,1024]{1,0:T(8,128)(2,1)}, u32[]{:S(2)}, u32[]{:S(2)}) %collective-permute-start.5) | collective-permute-done | bytes 262176 | tf_op jit(solution)/shard_map/ppermute | solution.py:264
  61.1 0.6 collective-permute-start.8
  61.7 0.7 stack.59.place_ref
  62.4 6.1 %own_sample.1 = (bf16[1024,1024]{1,0:T(8,128)(2,1)}, bf16[256,1024]{1,0:T(8,128)(2,1)}, bf16[256,256]{1,0:T(8,128)(2,1)}, bf16[256,768]{1,0:T(8,128)(2,1)}) custom-call(s32[14]{0:T(128)} %stack.59.place_ref, bf16[16,32,1024]{2,1,0:T(8,128)(2,1)} %copy-done.2, f32[1,1024]{1,0:T(1,128)} %bitcast.61, bf16[128,1024]{1,0:T(8,128)(2,1)} %copy-done.6, ...), custom_call_target="tpu_custom_call" | custom-call | flops 2000000000 | bytes 6291456 | tf_op jit(solution)/shard_map/own_sample/pallas_call | solution.py:321
  68.6 0.5 collective-permute-start.18
  69.1 0.5 copy-done.10
  69.5 8.4 %other_sample.1 = (bf16[256,256]{1,0:T(8,128)(2,1)}, bf16[256,768]{1,0:T(8,128)(2,1)}, f32[128,1024]{1,0:T(8,128)}, bf16[128,1024]{1,0:T(8,128)(2,1)}, bf16[128,...) custom-call(s32[14]{0:T(128)} %stack.59.place_ref, ...), custom_call_target="tpu_custom_call" | custom-call | flops 3000000000 | bytes 10485760 | tf_op jit(solution)/shard_map/other_sample/pallas_call | solution.py:342
  78.0 0.3 collective-permute-start.16
  78.3 0.3 collective-permute-start.17
  78.6 1.5 %collective-permute-start.13 = (bf16[128,1024]{1,0:T(8,128)(2,1)}, bf16[128,1024]{1,0:T(8,128)(2,1)S(1)}, u32[]{:S(2)}, u32[]{:S(2)}) collective-permute-start(bf16[128,1024]{1,0:T(8,128)(2,1)} %get-tuple-element.62), channel_id=1, source_target_pairs={{0,128},{64,192},{128,0},{192,64},{1,129},{65,193},{129,1},{193,65... | collective-permute-start | bytes 786440 | tf_op jit(solution)/shard_map/ppermute | solution.py:264
  80.1 0.1 collective-permute-done.17.refs_4_
  80.2 0.6 copy-done.7
  80.8 1.1 collective-permute-start.14
  81.9 0.7 copy-done.5
  82.7 1.3 copy-done.1
  84.0 5.5 %input_gradient.1 = bf16[16,48,512]{2,1,0:T(8,128)(2,1)} custom-call(bf16[16,32,1024]{2,1,0:T(8,128)(2,1)} %copy-done.2, bf16[256,768]{1,0:T(8,128)(2,1)} %get-tuple-element.55.refs_2_.refs_1_, bf16[256,768]{1,0:T(8,128)(2,1)} %copy-done.5, bf16[256,256]{1,0:T(8,128)(2,1)} %get-tuple-element.54.refs_1_.refs_3_, bf16[256,256]{1,0:T(8,128)(2,1)} %copy-done.7, ...), custom_call_target="tpu_custom_call" | custom-call | flops 1000000000 | bytes 6291456 | tf_op jit(solution)/shard_map/input_gradient/pallas_call | solution.py:378
  89.4 8.0 %all-to-all-start.2 = ((bf16[16,48,512]{2,1,0:T(8,128)(2,1)}), bf16[16,48,512]{2,1,0:T(8,128)(2,1)S(1)}, u32[]{:S(2)}, u32[]{:S(2)}) async-start(bf16[16,48,512]{2,1,0:T(8,128)(2,1)} %input_gradient.1), calls=%async_computation.2 | async-start | bytes 1572864 | tf_op jit(solution)/shard_map/all_to_all | solution.py:260
  97.5 0.7 collective-permute-start.9
  98.1 1.9 %collective-permute-start.10 = (bf16[128,1024]{1,0:T(8,128)(2,1)}, bf16[128,1024]{1,0:T(8,128)(2,1)S(1)}, u32[]{:S(2)}, u32[]{:S(2)}) collective-permute-start(bf16[128,1024]{1,0:T(8,128)(2,1)} %get-tuple-element.58), channel_id=1, source_target_pairs={{0,128},{64,192},{128,0},{192,64},{1,129},{65,193},{129,1},{193,65... | collective-permute-start | bytes 786440 | tf_op jit(solution)/shard_map/ppermute | solution.py:264
  100.0 2.0 %collective-permute-start.11 = (bf16[128,1024]{1,0:T(8,128)(2,1)}, bf16[128,1024]{1,0:T(8,128)(2,1)S(1)}, u32[]{:S(2)}, u32[]{:S(2)}) collective-permute-start(bf16[128,1024]{1,0:T(8,128)(2,1)} %get-tuple-element.59), channel_id=1, source_target_pairs={{0,192},{64,0},{128,64},{192,128},{1,193},{65,1},{129,65},{193,129... | collective-permute-start | bytes 786440 | tf_op jit(solution)/shard_map/ppermute | solution.py:264
  102.0 1.1 add_convert_fusion
  103.1 1.8 %collective-permute-start.15 = (bf16[128,1024]{1,0:T(8,128)(2,1)S(1)}, bf16[128,1024]{1,0:T(8,128)(2,1)S(1)}, u32[]{:S(2)}, u32[]{:S(2)}) collective-permute-start(bf16[128,1024]{1,0:T(8,128)(2,1)S(1)} %add_convert_fusion), channel_id=1, source_target_pairs={{0,32},{32,0},{1,33},{33,1},{2,34},{34,2},{3,35},{35,3},{4,36},{36... | collective-permute-start | bytes 786440 | tf_op jit(solution)/shard_map/ppermute | solution.py:268
  104.9 1.1 collective-permute-done.9.a_ref
  106.0 5.1 %collective-permute-done.10.b_ref = bf16[128,1024]{1,0:T(8,128)(2,1)S(1)} collective-permute-done((bf16[128,1024]{1,0:T(8,128)(2,1)}, bf16[128,1024]{1,0:T(8,128)(2,1)S(1)}, u32[]{:S(2)}, u32[]{:S(2)}) %collective-permute-start.10) | collective-permute-done | bytes 262176 | tf_op jit(solution)/shard_map/ppermute | solution.py:264
  111.1 1.4 collective-permute-done.11.c_ref
  112.5 4.0 %collective-permute-done.15.across_ref = bf16[128,1024]{1,0:T(8,128)(2,1)S(1)} collective-permute-done((bf16[128,1024]{1,0:T(8,128)(2,1)S(1)}, bf16[128,1024]{1,0:T(8,128)(2,1)S(1)}, u32[]{:S(2)}, u32[]{:S(2)}) %collective-permute-start.15) | collective-permute-done | bytes 262176 | tf_op jit(solution)/shard_map/ppermute | solution.py:268
  116.5 0.7 copy-done.20
  117.2 2.2 %sum_blocks.1 = bf16[16,8,1024]{2,1,0:T(8,128)(2,1)} custom-call(f32[128,1024]{1,0:T(8,128)} %get-tuple-element.56.own_ref, bf16[128,1024]{1,0:T(8,128)(2,1)} %copy-done.17, bf16[128,1024]{1,0:T(8,128)(2,1)} %copy-done.18, bf16[128,1024]{1,0:T(8,128)(2,1)} %copy-done.19, bf16[128,1024]{1,0:T(8,128)(2,1)} %copy-done.20), custom_call_target="tpu_custom_call" | custom-call | flops 10000000000 | bytes 2097152 | tf_op jit(solution)/shard_map/sum_blocks/pallas_call | solution.py:369
  119.4 6.9 %all-to-all-start.3 = ((bf16[16,8,1024]{2,1,0:T(8,128)(2,1)}), bf16[16,8,1024]{2,1,0:T(8,128)(2,1)S(1)}, u32[]{:S(2)}, u32[]{:S(2)}) async-start(bf16[16,8,1024]{2,1,0:T(8,128)(2,1)} %sum_blocks.1), calls=%async_computation.3 | async-start | bytes 524288 | tf_op jit(solution)/shard_map/all_to_all | solution.py:260
  126.4 0.0 copy-start.9
  126.4 3.4 %home.1 = (bf16[2,128,1024]{2,1,0:T(8,128)(2,1)}, bf16[2,128,1024]{2,1,0:T(8,128)(2,1)}) custom-call(bf16[16,48,512]{2,1,0:T(8,128)(2,1)} %copy-done.3, bf16[2,128,1024]{2,1,0:T(8,128)(2,1)} %bitcast.56, bf16[1024,1024]{1,0:T(8,128)(2,1)} %get-tuple-element.52.w_ref.refs_5_.w_mine_ref, bf16[1024,1024]{1,0:T(8,128)(2,1)} %copy-done.1), custom_call_target="tpu_custom_call" | custom-call | flops 300000000 | bytes 4194304 | tf_op jit(solution)/shard_map/home/pallas_call | solution.py:399
  129.8 4.4 %all-to-all-done.3 = bf16[16,8,1024]{2,1,0:T(8,128)(2,1)S(1)} async-done(((bf16[16,8,1024]{2,1,0:T(8,128)(2,1)}), bf16[16,8,1024]{2,1,0:T(8,128)(2,1)S(1)}, u32[]{:S(2)}, u32[]{:S(2)}) %all-to-all-start.3) | async-done | bytes 262176 | tf_op jit(solution)/shard_map/all_to_all | solution.py:260
  134.2 0.2 reshape.80
  134.3 0.1 reduce_sum.18
  134.4 3.6 %collective-permute-start.19 = (f32[4,1024]{1,0:T(4,128)S(1)}, f32[4,1024]{1,0:T(4,128)S(1)}, u32[]{:S(2)}, u32[]{:S(2)}) collective-permute-start(f32[4,1024]{1,0:T(4,128)S(1)} %dynamic-slice_bitcast_fusion.2), channel_id=1, source_target_pairs={{0,16},{16,0},{1,17},{17,1},{2,18},{18,2},{3,19},{19,3},{4,20},{20... | collective-permute-start | bytes 49160 | tf_op jit(solution)/shard_map/ppermute | solution.py:256
  138.1 0.8 collective-permute-done.19
  139.0 0.6 copy.27
  139.7 0.0 copy-start.8
  139.7 0.1 multiply_reduce_fusion
  139.8 1.3 dynamic-slice_divide_fusion
  (57 shorter events, 0.3 us)
Async XLA Ops:
  0.6 11.6 %copy-start = (bf16[1,2,128,1024]{3,2,1,0:T(8,128)(2,1)S(1)}, bf16[1,2,128,1024]{3,2,1,0:T(8,128)(2,1)}, u32[]{:S(2)}) copy-start(bf16[1,2,128,1024]{3,2,1,0:T(8,128)(2,1)} %param.9) | copy-start | bytes 1572868
  2.1 18.8 %all-to-all-start = ((bf16[16,8,1024]{2,1,0:T(8,128)(2,1)}), bf16[16,8,1024]{2,1,0:T(8,128)(2,1)S(1)}, u32[]{:S(2)}, u32[]{:S(2)}) async-start(bf16[16,8,1024]{2,1,0:T(8,128)(2,1)} %pack_weights.1), calls=%async_computation | async-start | bytes 524288 | tf_op jit(solution)/shard_map/all_to_all | solution.py:260
  21.2 3.6 %collective-permute-start = (bf16[64,1024]{1,0:T(8,128)(2,1)S(1)}, bf16[64,1024]{1,0:T(8,128)(2,1)S(1)}, u32[]{:S(2)}, u32[]{:S(2)}) collective-permute-start(bf16[64,1024]{1,0:T(8,128)(2,1)S(1)} %reshape.75), channel_id=1, source_target_pairs={{0,16},{16,0},{1,17},{17,1},{2,18},{18,2},{3,19},{19,3},{4,20},{20... | collective-permute-start | bytes 393224 | tf_op jit(solution)/shard_map/ppermute | solution.py:256
  24.8 37.6 %copy-start.6 = (bf16[128,1024]{1,0:T(8,128)(2,1)}, bf16[128,1024]{1,0:T(8,128)(2,1)S(1)}, u32[]{:S(2)}) copy-start(bf16[128,1024]{1,0:T(8,128)(2,1)S(1)} %pad_maximum_fusion.1.refs_0_) | copy-start | bytes 786436
  24.8 36.3 %all-to-all-start.1 = ((bf16[16,32,1024]{2,1,0:T(8,128)(2,1)}), bf16[16,32,1024]{2,1,0:T(8,128)(2,1)S(1)}, u32[]{:S(2)}, u32[]{:S(2)}) async-start(bf16[16,32,1024]{2,1,0:T(8,128)(2,1)} %pad_maximum_fusion), calls=%async_computation.1 | async-start | bytes 2097152 | tf_op jit(solution)/shard_map/all_to_all | solution.py:260
  29.1 13.8 %collective-permute-start.4 = (bf16[128,1024]{1,0:T(8,128)(2,1)S(1)}, bf16[128,1024]{1,0:T(8,128)(2,1)S(1)}, u32[]{:S(2)}, u32[]{:S(2)}) collective-permute-start(bf16[128,1024]{1,0:T(8,128)(2,1)S(1)} %pad_maximum_fusion.1.refs_0_), channel_id=1, source_target_pairs={{0,32},{32,0},{1,33},{33,1},{2,34},{34,2},{3,35},{35,3},{4,36},{36... | collective-permute-start | bytes 786440 | tf_op jit(solution)/shard_map/ppermute | solution.py:268
  31.6 14.4 %collective-permute-start.3 = (bf16[128,1024]{1,0:T(8,128)(2,1)S(1)}, bf16[128,1024]{1,0:T(8,128)(2,1)S(1)}, u32[]{:S(2)}, u32[]{:S(2)}) collective-permute-start(bf16[128,1024]{1,0:T(8,128)(2,1)S(1)} %pad_maximum_fusion.1.refs_0_), channel_id=1, source_target_pairs={{0,192},{64,0},{128,64},{192,128},{1,193},{65,1},{129,65},{193,129... | collective-permute-start | bytes 786440 | tf_op jit(solution)/shard_map/ppermute | solution.py:264
  34.3 12.3 %collective-permute-start.2 = (bf16[128,1024]{1,0:T(8,128)(2,1)S(1)}, bf16[128,1024]{1,0:T(8,128)(2,1)S(1)}, u32[]{:S(2)}, u32[]{:S(2)}) collective-permute-start(bf16[128,1024]{1,0:T(8,128)(2,1)S(1)} %pad_maximum_fusion.1.refs_0_), channel_id=1, source_target_pairs={{0,128},{64,192},{128,0},{192,64},{1,129},{65,193},{129,1},{193,65... | collective-permute-start | bytes 786440 | tf_op jit(solution)/shard_map/ppermute | solution.py:264
  34.7 15.0 %collective-permute-start.1 = (bf16[128,1024]{1,0:T(8,128)(2,1)S(1)}, bf16[128,1024]{1,0:T(8,128)(2,1)S(1)}, u32[]{:S(2)}, u32[]{:S(2)}) collective-permute-start(bf16[128,1024]{1,0:T(8,128)(2,1)S(1)} %pad_maximum_fusion.1.refs_0_), channel_id=1, source_target_pairs={{0,64},{64,128},{128,192},{192,0},{1,65},{65,129},{129,193},{193,1... | collective-permute-start | bytes 786440 | tf_op jit(solution)/shard_map/ppermute | solution.py:264
  42.9 19.5 %copy-start.11 = (bf16[128,1024]{1,0:T(8,128)(2,1)}, bf16[128,1024]{1,0:T(8,128)(2,1)S(1)}, u32[]{:S(2)}) copy-start(bf16[128,1024]{1,0:T(8,128)(2,1)S(1)} %collective-permute-done.4.refs_4_) | copy-start | bytes 786436
  42.9 8.1 %collective-permute-start.7 = (bf16[128,1024]{1,0:T(8,128)(2,1)S(1)}, bf16[128,1024]{1,0:T(8,128)(2,1)S(1)}, u32[]{:S(2)}, u32[]{:S(2)}) collective-permute-start(bf16[128,1024]{1,0:T(8,128)(2,1)S(1)} %collective-permute-done.4.refs_4_), channel_id=1, source_target_pairs={{0,192},{64,0},{128,64},{192,128},{1,193},{65,1},{129,65},{193,129... | collective-permute-start | bytes 786440 | tf_op jit(solution)/shard_map/ppermute | solution.py:264
  45.6 7.9 %collective-permute-start.6 = (bf16[128,1024]{1,0:T(8,128)(2,1)S(1)}, bf16[128,1024]{1,0:T(8,128)(2,1)S(1)}, u32[]{:S(2)}, u32[]{:S(2)}) collective-permute-start(bf16[128,1024]{1,0:T(8,128)(2,1)S(1)} %collective-permute-done.4.refs_4_), channel_id=1, source_target_pairs={{0,128},{64,192},{128,0},{192,64},{1,129},{65,193},{129,1},{193,65... | collective-permute-start | bytes 786440 | tf_op jit(solution)/shard_map/ppermute | solution.py:264
  46.0 15.1 %copy-start.12 = (bf16[128,1024]{1,0:T(8,128)(2,1)}, bf16[128,1024]{1,0:T(8,128)(2,1)S(1)}, u32[]{:S(2)}) copy-start(bf16[128,1024]{1,0:T(8,128)(2,1)S(1)} %collective-permute-done.3.refs_3_) | copy-start | bytes 786436
  46.0 15.1 %collective-permute-start.5 = (bf16[128,1024]{1,0:T(8,128)(2,1)S(1)}, bf16[128,1024]{1,0:T(8,128)(2,1)}, u32[]{:S(2)}, u32[]{:S(2)}) collective-permute-start(bf16[128,1024]{1,0:T(8,128)(2,1)S(1)} %collective-permute-done.4.refs_4_), channel_id=1, source_target_pairs={{0,64},{64,128},{128,192},{192,0},{1,65},{65,129},{129,193},{193,1... | collective-permute-start | bytes 786440 | tf_op jit(solution)/shard_map/ppermute | solution.py:264
  46.7 14.4 %copy-start.13 = (bf16[128,1024]{1,0:T(8,128)(2,1)}, bf16[128,1024]{1,0:T(8,128)(2,1)S(1)}, u32[]{:S(2)}) copy-start(bf16[128,1024]{1,0:T(8,128)(2,1)S(1)} %collective-permute-done.2.refs_2_) | copy-start | bytes 786436
  49.7 11.4 %copy-start.14 = (bf16[128,1024]{1,0:T(8,128)(2,1)}, bf16[128,1024]{1,0:T(8,128)(2,1)S(1)}, u32[]{:S(2)}) copy-start(bf16[128,1024]{1,0:T(8,128)(2,1)S(1)} %collective-permute-done.1.refs_1_) | copy-start | bytes 786436
  51.0 10.1 %copy-start.15 = (bf16[128,1024]{1,0:T(8,128)(2,1)}, bf16[128,1024]{1,0:T(8,128)(2,1)S(1)}, u32[]{:S(2)}) copy-start(bf16[128,1024]{1,0:T(8,128)(2,1)S(1)} %collective-permute-done.7.refs_7_) | copy-start | bytes 786436
  53.5 0.7 copy-start.16
  61.1 1.3 copy-start.2
  61.1 7.4 %collective-permute-start.8 = (bf16[16,32,1024]{2,1,0:T(8,128)(2,1)S(1)}, bf16[16,32,1024]{2,1,0:T(8,128)(2,1)S(1)}, u32[]{:S(2)}, u32[]{:S(2)}) collective-permute-start(bf16[16,32,1024]{2,1,0:T(8,128)(2,1)S(1)} %all-to-all-done.1.got_ref.got_own_ref.refs_0_), channel_id=1, source_target_pairs={{0,16},{16,0},{1,17},{17,1},{2,18},{18,2},{3,19},{19,3},{4,20},{20... | collective-permute-start | bytes 3145736 | tf_op jit(solution)/shard_map/ppermute | solution.py:256
  68.6 1.0 copy-start.10
  68.6 13.3 %collective-permute-start.18 = (bf16[1024,1024]{1,0:T(8,128)(2,1)}, bf16[1024,1024]{1,0:T(8,128)(2,1)S(1)}, u32[]{:S(2)}, u32[]{:S(2)}) collective-permute-start(bf16[1024,1024]{1,0:T(8,128)(2,1)} %get-tuple-element.52.w_ref.refs_5_.w_mine_ref), channel_id=1, source_target_pairs={{0,16},{16,0},{1,17},{17,1},{2,18},{18,2},{3,19},{19,3},{4,20},{20... | collective-permute-start | bytes 6291464 | tf_op jit(solution)/shard_map/ppermute | solution.py:256
  78.0 3.9 %collective-permute-start.16 = (bf16[256,768]{1,0:T(8,128)(2,1)}, bf16[256,768]{1,0:T(8,128)(2,1)S(1)}, u32[]{:S(2)}, u32[]{:S(2)}) collective-permute-start(bf16[256,768]{1,0:T(8,128)(2,1)} %get-tuple-element.64), channel_id=1, source_target_pairs={{0,16},{16,0},{1,17},{17,1},{2,18},{18,2},{3,19},{19,3},{4,20},{20... | collective-permute-start | bytes 1179656 | tf_op jit(solution)/shard_map/ppermute | solution.py:256
  78.3 1.9 %collective-permute-start.17 = (bf16[256,256]{1,0:T(8,128)(2,1)}, bf16[256,256]{1,0:T(8,128)(2,1)S(1)}, u32[]{:S(2)}, u32[]{:S(2)}) collective-permute-start(bf16[256,256]{1,0:T(8,128)(2,1)} %get-tuple-element.65), channel_id=1, source_target_pairs={{0,16},{16,0},{1,17},{17,1},{2,18},{18,2},{3,19},{19,3},{4,20},{20... | collective-permute-start | bytes 393224 | tf_op jit(solution)/shard_map/ppermute | solution.py:256
  78.6 21.4 %collective-permute-start.12 = (bf16[128,1024]{1,0:T(8,128)(2,1)}, bf16[128,1024]{1,0:T(8,128)(2,1)S(1)}, u32[]{:S(2)}, u32[]{:S(2)}) collective-permute-start(bf16[128,1024]{1,0:T(8,128)(2,1)} %get-tuple-element.61), channel_id=1, source_target_pairs={{0,64},{64,128},{128,192},{192,0},{1,65},{65,129},{129,193},{193,1... | collective-permute-start | bytes 786440 | tf_op jit(solution)/shard_map/ppermute | solution.py:264
  78.6 23.4 %collective-permute-start.13 = (bf16[128,1024]{1,0:T(8,128)(2,1)}, bf16[128,1024]{1,0:T(8,128)(2,1)S(1)}, u32[]{:S(2)}, u32[]{:S(2)}) collective-permute-start(bf16[128,1024]{1,0:T(8,128)(2,1)} %get-tuple-element.62), channel_id=1, source_target_pairs={{0,128},{64,192},{128,0},{192,64},{1,129},{65,193},{129,1},{193,65... | collective-permute-start | bytes 786440 | tf_op jit(solution)/shard_map/ppermute | solution.py:264
  80.2 0.6 copy-start.7
  80.8 21.2 %copy-start.4 = (f32[128,1024]{1,0:T(8,128)S(1)}, f32[128,1024]{1,0:T(8,128)}, u32[]{:S(2)}) copy-start(f32[128,1024]{1,0:T(8,128)} %get-tuple-element.60) | copy-start | bytes 1572868
  80.8 21.2 %collective-permute-start.14 = (bf16[128,1024]{1,0:T(8,128)(2,1)}, bf16[128,1024]{1,0:T(8,128)(2,1)}, u32[]{:S(2)}, u32[]{:S(2)}) collective-permute-start(bf16[128,1024]{1,0:T(8,128)(2,1)} %get-tuple-element.63), channel_id=1, source_target_pairs={{0,192},{64,0},{128,64},{192,128},{1,193},{65,1},{129,65},{193,129... | collective-permute-start | bytes 786440 | tf_op jit(solution)/shard_map/ppermute | solution.py:264
  81.9 0.7 copy-start.5
  82.7 1.3 copy-start.1
  89.4 30.0 %all-to-all-start.2 = ((bf16[16,48,512]{2,1,0:T(8,128)(2,1)}), bf16[16,48,512]{2,1,0:T(8,128)(2,1)S(1)}, u32[]{:S(2)}, u32[]{:S(2)}) async-start(bf16[16,48,512]{2,1,0:T(8,128)(2,1)} %input_gradient.1), calls=%async_computation.2 | async-start | bytes 1572864 | tf_op jit(solution)/shard_map/all_to_all | solution.py:260
  97.5 8.5 %collective-permute-start.9 = (bf16[128,1024]{1,0:T(8,128)(2,1)}, bf16[128,1024]{1,0:T(8,128)(2,1)S(1)}, u32[]{:S(2)}, u32[]{:S(2)}) collective-permute-start(bf16[128,1024]{1,0:T(8,128)(2,1)} %get-tuple-element.57), channel_id=1, source_target_pairs={{0,64},{64,128},{128,192},{192,0},{1,65},{65,129},{129,193},{193,1... | collective-permute-start | bytes 786440 | tf_op jit(solution)/shard_map/ppermute | solution.py:264
  98.1 12.9 %collective-permute-start.10 = (bf16[128,1024]{1,0:T(8,128)(2,1)}, bf16[128,1024]{1,0:T(8,128)(2,1)S(1)}, u32[]{:S(2)}, u32[]{:S(2)}) collective-permute-start(bf16[128,1024]{1,0:T(8,128)(2,1)} %get-tuple-element.58), channel_id=1, source_target_pairs={{0,128},{64,192},{128,0},{192,64},{1,129},{65,193},{129,1},{193,65... | collective-permute-start | bytes 786440 | tf_op jit(solution)/shard_map/ppermute | solution.py:264
  100.0 12.5 %collective-permute-start.11 = (bf16[128,1024]{1,0:T(8,128)(2,1)}, bf16[128,1024]{1,0:T(8,128)(2,1)S(1)}, u32[]{:S(2)}, u32[]{:S(2)}) collective-permute-start(bf16[128,1024]{1,0:T(8,128)(2,1)} %get-tuple-element.59), channel_id=1, source_target_pairs={{0,192},{64,0},{128,64},{192,128},{1,193},{65,1},{129,65},{193,129... | collective-permute-start | bytes 786440 | tf_op jit(solution)/shard_map/ppermute | solution.py:264
  103.1 13.4 %collective-permute-start.15 = (bf16[128,1024]{1,0:T(8,128)(2,1)S(1)}, bf16[128,1024]{1,0:T(8,128)(2,1)S(1)}, u32[]{:S(2)}, u32[]{:S(2)}) collective-permute-start(bf16[128,1024]{1,0:T(8,128)(2,1)S(1)} %add_convert_fusion), channel_id=1, source_target_pairs={{0,32},{32,0},{1,33},{33,1},{2,34},{34,2},{3,35},{35,3},{4,36},{36... | collective-permute-start | bytes 786440 | tf_op jit(solution)/shard_map/ppermute | solution.py:268
  106.0 10.5 %copy-start.17 = (bf16[128,1024]{1,0:T(8,128)(2,1)}, bf16[128,1024]{1,0:T(8,128)(2,1)S(1)}, u32[]{:S(2)}) copy-start(bf16[128,1024]{1,0:T(8,128)(2,1)S(1)} %collective-permute-done.9.a_ref) | copy-start | bytes 786436
  111.1 5.4 %copy-start.18 = (bf16[128,1024]{1,0:T(8,128)(2,1)}, bf16[128,1024]{1,0:T(8,128)(2,1)S(1)}, u32[]{:S(2)}) copy-start(bf16[128,1024]{1,0:T(8,128)(2,1)S(1)} %collective-permute-done.10.b_ref) | copy-start | bytes 786436
  112.5 4.0 %copy-start.19 = (bf16[128,1024]{1,0:T(8,128)(2,1)}, bf16[128,1024]{1,0:T(8,128)(2,1)S(1)}, u32[]{:S(2)}) copy-start(bf16[128,1024]{1,0:T(8,128)(2,1)S(1)} %collective-permute-done.11.c_ref) | copy-start | bytes 786436
  116.5 0.7 copy-start.20
  119.4 6.9 %copy-start.3 = (bf16[16,48,512]{2,1,0:T(8,128)(2,1)}, bf16[16,48,512]{2,1,0:T(8,128)(2,1)S(1)}, u32[]{:S(2)}) copy-start(bf16[16,48,512]{2,1,0:T(8,128)(2,1)S(1)} %all-to-all-done.2.got_ref) | copy-start | bytes 2359300
  119.4 14.7 %all-to-all-start.3 = ((bf16[16,8,1024]{2,1,0:T(8,128)(2,1)}), bf16[16,8,1024]{2,1,0:T(8,128)(2,1)S(1)}, u32[]{:S(2)}, u32[]{:S(2)}) async-start(bf16[16,8,1024]{2,1,0:T(8,128)(2,1)} %sum_blocks.1), calls=%async_computation.3 | async-start | bytes 524288 | tf_op jit(solution)/shard_map/all_to_all | solution.py:260
  126.4 13.3 %copy-start.9 = (bf16[4,1536]{1,0:T(4,128)(2,1)S(1)}, bf16[4,1536]{1,0:T(4,128)(2,1)}, u32[]{:S(2)}) copy-start(bf16[4,1536]{1,0:T(4,128)(2,1)} %w_qkv_ref.1) | copy-start | bytes 36868
  134.4 4.5 %collective-permute-start.19 = (f32[4,1024]{1,0:T(4,128)S(1)}, f32[4,1024]{1,0:T(4,128)S(1)}, u32[]{:S(2)}, u32[]{:S(2)}) collective-permute-start(f32[4,1024]{1,0:T(4,128)S(1)} %dynamic-slice_bitcast_fusion.2), channel_id=1, source_target_pairs={{0,16},{16,0},{1,17},{17,1},{2,18},{18,2},{3,19},{19,3},{4,20},{20... | collective-permute-start | bytes 49160 | tf_op jit(solution)/shard_map/ppermute | solution.py:256
  139.7 1.4 %copy-start.8 = (f32[4,1536]{1,0:T(4,128)}, f32[4,1536]{1,0:T(4,128)S(1)}, u32[]{:S(2)}) copy-start(f32[4,1536]{1,0:T(4,128)S(1)} %reshape.79) | copy-start | bytes 73732

commit v3 on v2

v3 whole, which is shorter than its diff:
```python
import functools

import jax
import jax.numpy as jnp
from jax import lax
from jax.experimental import pallas as pl
from jax.experimental.pallas import tpu as pltpu
from jax.sharding import Mesh, PartitionSpec as P

DP = ("y", "xh", "core")
TM = ("xl", "z")
Y_SIZE, XH_SIZE, TM_SIZE = 4, 2, 16

D = 1024
DH = 64
HALF = 256
norm_eps = 1e-05
f32 = jnp.float32
bf16 = jnp.bfloat16

NN = (((1,), (0,)), ((), ()))
NT = (((1,), (1,)), ((), ()))
TN = (((0,), (0,)), ((), ()))

VMEM = pl.BlockSpec(memory_space=pltpu.VMEM)
ANY = pl.BlockSpec(memory_space=pl.ANY)


def mm(a, b, dims):
    return lax.dot_general(a, b, dims, preferred_element_type=f32)


def layer_stats(features):
    wide = features.astype(f32)
    centred = wide - jnp.mean(wide, axis=-1, keepdims=True)
    inv_std = lax.rsqrt(jnp.mean(centred * centred, axis=-1, keepdims=True) + norm_eps)
    return centred * inv_std, inv_std


def pack_weights_kernel(w_qkv_ref, w_out_ref, out_ref):
    qkv, out = w_qkv_ref[...].astype(f32), w_out_ref[...].astype(f32)
    halves = []
    for half in range(2):
        parts = [qkv[:, (2 * part + half) * HALF : (2 * part + half + 1) * HALF] for part in range(3)]
        halves.append(jnp.concatenate(parts + [out[:, half * HALF : (half + 1) * HALF]], axis=1))
    both = jnp.concatenate(halves, axis=0)
    out_ref[...] = jnp.broadcast_to(both[None], out_ref.shape).astype(bf16)


def fetch(pairs, sems, first=0):
    copies = [pltpu.make_async_copy(src, dst, sems.at[first + i]) for i, (src, dst) in enumerate(pairs)]
    for copy in copies:
        copy.start()
    return copies


def wait_all(copies):
    for copy in copies:
        copy.wait()


CHUNK = 64


def sample(patches, got, gain_ref, weights, normed, mixed, dpacked, slots, before_weights):
    scores, d_probs, low_probs, d_scores = slots
    rows = normed.shape[0]
    per_peer = got.shape[1] // 2
    group = 4
    for peer in range(0, got.shape[0], group):
        features = got[peer : peer + group, :per_peer, :].reshape(group * per_peer, D)
        normal_x, _ = layer_stats(features)
        normed[peer * per_peer : (peer + group) * per_peer, :] = (normal_x * gain_ref[...]).astype(bf16)
    before_weights()
    packed = mm(normed[...], weights[:, : 3 * HALF], NN).astype(bf16)
    d_mixed = mm(got[:, per_peer:, :].reshape(rows, D), weights[:, 3 * HALF :], NN).astype(bf16)
    row_patch = lax.broadcasted_iota(jnp.int32, (CHUNK, rows), 0) % patches
    col_patch = lax.broadcasted_iota(jnp.int32, (CHUNK, rows), 1) % patches
    bias = jnp.where(row_patch == col_patch, 0.0, -1e30)
    low_half = lax.broadcasted_iota(jnp.int32, (rows, 2 * DH), 1) < DH
    zero = jnp.zeros((rows, 2 * DH), bf16)
    heads = HALF // DH

    def part(index, head):
        lo = index * HALF + head // 2 * 2 * DH
        return packed[:, lo : lo + 2 * DH]

    def d_part(head):
        lo = head // 2 * 2 * DH
        return d_mixed[:, lo : lo + 2 * DH]

    for head in range(heads):
        own = low_half if head % 2 == 0 else jnp.logical_not(low_half)
        query = jnp.where(own, part(0, head) * DH ** (-0.5), zero)
        scores[head] = mm(query, part(1, head), NT)
        d_probs[head] = mm(jnp.where(own, d_part(head), zero), part(2, head), NT)
    for pair in range(heads // 2):
        outs = []
        for head in (2 * pair, 2 * pair + 1):
            for at in range(0, rows, CHUNK):
                score = scores[head, at : at + CHUNK, :] + bias
                expo = jnp.exp(score - jnp.max(score, axis=-1, keepdims=True))
                prob = expo * (1.0 / jnp.sum(expo, axis=-1, keepdims=True))
                low_probs[head, at : at + CHUNK, :] = prob.astype(bf16)
                d_prob = d_probs[head, at : at + CHUNK, :]
                inner = jnp.sum(d_prob * prob, axis=-1, keepdims=True)
                d_scores[head, at : at + CHUNK, :] = (prob * (d_prob - inner)).astype(bf16)
            outs.append(
                (
                    mm(low_probs[head], part(2, head), NN),
                    mm(d_scores[head], part(1, head), NN) * DH ** (-0.5),
                    mm(d_scores[head], part(0, head), TN) * DH ** (-0.5),
                    mm(low_probs[head], d_part(head), TN),
                )
            )
        outs = [jnp.where(low_half, low, high).astype(bf16) for low, high in zip(*outs)]
        lo = pair * 2 * DH
        mixed[:, lo : lo + 2 * DH] = outs[0]
        for index in range(3):
            at = index * HALF + lo
            dpacked[:, at : at + 2 * DH] = outs[1 + index]


def block_of(step, side):
    y, xh = lax.axis_index("y"), lax.axis_index("xh")
    return lax.rem(y + step + Y_SIZE, Y_SIZE) * XH_SIZE + lax.rem(xh + side, XH_SIZE)


def arrived_kernel(*refs):
    refs[-1][...] = jnp.zeros_like(refs[-1])


def layer_kernel(patches, got_own_ref, got_other_ref, gain_ref, token_ref, *refs):
    pieces, outs, grad_refs, scratch = refs[:8], refs[8:13], refs[13:21], refs[21:]
    w_ref, mixed_own_ref, dnormed_own_ref, mixed_other_ref, dnormed_other_ref = outs
    got, weights, normed, mixed, dpacked, dnormed, grads, own, peers = scratch[:9]
    slots, (sems, out_sems) = scratch[9:13], scratch[13:]
    copies = fetch([(got_own_ref, got.at[0])], sems)
    block = own.shape[1]
    places = [block_of(-(i % Y_SIZE), i // Y_SIZE) for i in range(8)]
    starts = [pl.multiple_of(place * block, block) for place in places]
    copies += fetch([(p, weights.at[pl.ds(at, block), :]) for p, at in zip(pieces, starts)], sems, 1)
    copies += fetch([(got_other_ref, got.at[1])], sems, 9)
    results = []
    per_peer = got.shape[2] // 2

    def before_weights():
        wait_all(copies[1:9])
        results.extend(fetch([(weights.at[:, 3 * HALF :], w_ref)], out_sems))

    copies[0].wait()
    arguments = (got.at[0], gain_ref, weights, normed.at[0], mixed.at[0], dpacked.at[0])
    sample(patches, *arguments, slots, before_weights)
    dnormed[0] = mm(dpacked[0], weights[:, : 3 * HALF], NT)
    results += fetch([(mixed.at[0], mixed_own_ref), (dnormed.at[0], dnormed_own_ref)], out_sems, 1)
    copies[9].wait()
    arguments = (got.at[1], gain_ref, weights, normed.at[1], mixed.at[1], dpacked.at[1])
    sample(patches, *arguments, slots, lambda: None)
    dnormed[1] = mm(dpacked[1], weights[:, : 3 * HALF], NT)
    results += fetch([(mixed.at[1], mixed_other_ref), (dnormed.at[1], dnormed_other_ref)], out_sems, 3)
    rows = normed.shape[1]
    pair_rows = 2 * block
    all_dpacked = dpacked[...].reshape(2 * rows, 3 * HALF)
    all_mixed = mixed[...].reshape(2 * rows, HALF)
    y, xh = lax.axis_index("y"), lax.axis_index("xh")
    for step in (1, 2, 3, 0):
        start = pl.multiple_of(lax.rem(y + step, Y_SIZE) * pair_rows, pair_rows)
        columns = pl.ds(start, pair_rows)
        grads[:, : 3 * HALF] = mm(normed[:, :, columns].reshape(2 * rows, pair_rows), all_dpacked, TN)
        grads[:, 3 * HALF :] = mm(got[:, :, per_peer:, columns].reshape(2 * rows, pair_rows), all_mixed, TN)
        for side in range(XH_SIZE):
            start = pl.multiple_of(lax.rem(xh + side, XH_SIZE) * block, block)
            slot = own.at[side] if step == 0 else peers.at[side * (Y_SIZE - 1) + step - 1]
            slot[...] = grads[pl.ds(start, block), :].astype(slot.dtype)
            results += fetch([(slot, grad_refs[side * Y_SIZE + step])], out_sems, len(results))
    wait_all(results)


def input_kernel(got_ref, mine_ref, mixed_ref, other, mixed_other, gain_ref, out_ref, got, mine, mixed, out, sems):
    copies = fetch([(got_ref, got), (mine_ref, mine), (mixed_ref, mixed)], sems)
    peers, per_peer = got.shape[0], got.shape[1] // 2
    wait_all(copies)
    results = []
    group = 4
    half = (group, per_peer, D // 2)
    for peer in range(0, peers, group):
        at = slice(peer, peer + group)
        rows = slice(peer * per_peer, (peer + group) * per_peer)
        normal_x, inv_std = layer_stats(got[at, :per_peer, :].reshape(group * per_peer, D))
        scaled = (mine[rows, :] + other[rows, :]).astype(bf16).astype(f32) * gain_ref[...]
        d_input = inv_std * (
            scaled
            - jnp.mean(scaled, axis=-1, keepdims=True)
            - normal_x * jnp.mean(scaled * normal_x, axis=-1, keepdims=True)
        )
        grad_in = (got[at, per_peer:, :].reshape(group * per_peer, D).astype(f32) + d_input).astype(bf16)
        out[at, :per_peer, :] = grad_in[:, : D // 2].reshape(half)
        out[at, per_peer : 2 * per_peer, :] = grad_in[:, D // 2 :].reshape(half)
        out[at, 2 * per_peer :, :HALF] = mixed[rows, :].reshape(group, per_peer, HALF)
        out[at, 2 * per_peer :, HALF:] = mixed_other[rows, :].reshape(group, per_peer, HALF)
        results += fetch([(out.at[at], out_ref.at[at])], sems, 3 + len(results))
    wait_all(results)


def sum_kernel(own_ref, a_ref, b_ref, c_ref, across_ref, out_ref):
    total = own_ref[...] + a_ref[...].astype(f32) + b_ref[...].astype(f32) + c_ref[...].astype(f32)
    total = total + across_ref[...].astype(f32)
    shard = 4
    low, high = (total.reshape(2, -1, 2 * shard, D)[core] for core in range(2))
    top = lax.broadcasted_iota(jnp.int32, low.shape, 1) < shard
    even = jnp.where(top, low, pltpu.roll(high, shard, 1))
    odd = jnp.where(top, pltpu.roll(low, shard, 1), high)
    out_ref[...] = jnp.stack([even, odd], axis=1).reshape(out_ref.shape).astype(bf16)


def home_kernel(got_ref, x_ref, w_mine_ref, w_other_ref, result_ref, grad_ref, got, x, w_mine, w_other, result, grad, sems):
    wait_all(
        fetch(
            [(got_ref, got), (x_ref, x), (w_mine_ref, w_mine), (w_other_ref, w_other)],
            sems,
        )
    )
    peers, _, width = got.shape
    frames, count, _ = x.shape
    patches = count // peers
    per_peer = frames * patches

    def by_frame(part):
        wide = got[:, part * per_peer : (part + 1) * per_peer, :].astype(f32)
        wide = wide.reshape(peers, frames, patches, width)
        return [wide[:, f].reshape(count, width).astype(bf16) for f in range(frames)]

    low, high, heads = by_frame(0), by_frame(1), by_frame(2)
    for f in range(frames):
        grad[f, :, :width] = low[f]
        grad[f, :, width:] = high[f]
    results = fetch([(grad, grad_ref)], sems)
    for f in range(frames):
        projected = mm(heads[f][:, :HALF], w_mine[...], NT) + mm(heads[f][:, HALF:], w_other[...], NT)
        result[f] = (x[f].astype(f32) + projected).astype(bf16)
    wait_all(results + fetch([(result, result_ref)], sems, 1))


def vmem_params(mib=60):
    return pltpu.CompilerParams(vmem_limit_bytes=mib * 2**20)


def exchange(value):
    return lax.ppermute(value, "core", [(0, 1), (1, 0)])


def swap(value, axes):
    return lax.all_to_all(value, axes, split_axis=0, concat_axis=0, tiled=True)


def along_y(value, step):
    return lax.ppermute(value, "y", [(i, (i + step) % Y_SIZE) for i in range(Y_SIZE)])


def across_x(value):
    return lax.ppermute(value, "xh", [(0, 1), (1, 0)])


def body(frames_in, gain, w_qkv, w_out, out_grad):
    _, frames, patch_count, width = frames_in.shape
    tm = TM_SIZE
    patches = patch_count // tm
    per_peer = frames * patches
    rows = tm * per_peer
    shard = w_qkv.shape[0]
    core = lax.axis_index("core")
    first = core == 0
    gain_row = gain.reshape(1, width)

    def by_patch(value):
        value = value.reshape(frames, tm, patches, width).transpose(1, 0, 2, 3)
        return value.reshape(tm, per_peer, width)

    w_parts = pl.pallas_call(
        pack_weights_kernel,
        out_shape=jax.ShapeDtypeStruct((tm, 2 * shard, width), bf16),
        in_specs=[VMEM] * 2,
        compiler_params=vmem_params(),
        cost_estimate=pl.CostEstimate(flops=0, bytes_accessed=2**18, transcendentals=0),
        name="pack_weights",
    )(w_qkv, w_out.T)
    w_got = swap(w_parts.reshape(-1, width), TM).reshape(tm, 2, shard, width)

    w_keep = lax.dynamic_index_in_dim(w_got, core, 1, keepdims=False).reshape(tm * shard, width)
    w_send = lax.dynamic_index_in_dim(w_got, 1 - core, 1, keepdims=False).reshape(tm * shard, width)
    w_recv = exchange(w_send)
    w_block = jnp.concatenate(
        [jnp.where(first, w_keep, w_recv), jnp.where(first, w_recv, w_keep)], axis=0
    )
    block = w_block.shape[0]

    sent = jnp.concatenate([by_patch(frames_in), by_patch(out_grad)], axis=1)
    sent, w_block = lax.optimization_barrier((sent, w_block))
    got = swap(sent.reshape(-1, width), TM).reshape(tm, 2 * per_peer, width)

    pieces = []
    for part in (w_block, across_x(w_block)):
        pieces += [part] + [along_y(part, step) for step in range(1, Y_SIZE)]
    got_other = exchange(got)

    shape = jax.ShapeDtypeStruct
    token = pl.pallas_call(
        arrived_kernel,
        in_specs=[ANY] * 8,
        out_specs=VMEM,
        out_shape=shape((8, 128), f32),
        compiler_params=vmem_params(),
        cost_estimate=pl.CostEstimate(flops=2 * 10**10, bytes_accessed=4 * 2**20, transcendentals=0),
        name="arrived",
    )(*pieces)

    sample_shapes = (shape((rows, HALF), bf16), shape((rows, width), f32))
    half_shape, own_shape = shape((block, width), bf16), shape((block, width), f32)
    w_mine, mixed, d_normed, mixed_2, d_normed_2, *grad_pieces = pl.pallas_call(
        functools.partial(layer_kernel, patches),
        in_specs=[ANY, ANY, VMEM, VMEM] + [ANY] * 8,
        out_specs=(ANY,) * 13,
        out_shape=(shape((width, HALF), bf16),)
        + sample_shapes * 2 + ((own_shape,) + (half_shape,) * (Y_SIZE - 1)) * 2,
        scratch_shapes=[
            pltpu.VMEM((2,) + got.shape, bf16),
            pltpu.VMEM((width, width), bf16),
            pltpu.VMEM((2, rows, width), bf16),
            pltpu.VMEM((2, rows, HALF), bf16),
            pltpu.VMEM((2, rows, 3 * HALF), bf16),
            pltpu.VMEM((2, rows, width), f32),
            pltpu.VMEM((2 * block, width), f32),
            pltpu.VMEM((2, block, width), f32),
            pltpu.VMEM((6, block, width), bf16),
            pltpu.VMEM((HALF // DH, rows, rows), f32),
            pltpu.VMEM((HALF // DH, rows, rows), f32),
            pltpu.VMEM((HALF // DH, rows, rows), bf16),
            pltpu.VMEM((HALF // DH, rows, rows), bf16),
            pltpu.SemaphoreType.DMA((10,)),
            pltpu.SemaphoreType.DMA((13,)),
        ],
        compiler_params=vmem_params(),
        cost_estimate=pl.CostEstimate(flops=3 * 10**10, bytes_accessed=10 * 2**20, transcendentals=2**19),
        name="layer",
    )(got, got_other, gain_row, token, *pieces)
    w_other = exchange(w_mine)
    d_normed_other = exchange(d_normed_2)
    mixed_other = exchange(mixed_2)

    received = [along_y(grad_pieces[Y_SIZE + step], step) for step in range(1, Y_SIZE)]
    partial = grad_pieces[Y_SIZE] + sum(piece.astype(f32) for piece in received)
    received = [along_y(grad_pieces[step], step) for step in range(1, Y_SIZE)]
    grads = pl.pallas_call(
        sum_kernel,
        in_specs=[VMEM] * 5,
        out_shape=shape((tm, 2 * shard, width), bf16),
        compiler_params=vmem_params(8),
        cost_estimate=pl.CostEstimate(flops=10**10, bytes_accessed=2 * 2**20, transcendentals=0),
        name="sum_blocks",
    )(grad_pieces[0], *received, across_x(partial.astype(bf16)))

    sent = pl.pallas_call(
        input_kernel,
        out_shape=shape((tm, 3 * per_peer, width // 2), bf16),
        in_specs=[ANY] * 3 + [VMEM] * 3,
        out_specs=ANY,
        scratch_shapes=[
            pltpu.VMEM(got.shape, bf16),
            pltpu.VMEM((rows, width), f32),
            pltpu.VMEM((rows, HALF), bf16),
            pltpu.VMEM((tm, 3 * per_peer, width // 2), bf16),
            pltpu.SemaphoreType.DMA((11,)),
        ],
        compiler_params=vmem_params(56),
        cost_estimate=pl.CostEstimate(flops=10**9, bytes_accessed=6 * 2**20, transcendentals=0),
        name="input_gradient",
    )(got, d_normed, mixed, d_normed_other, mixed_other, gain_row)
    got = swap(sent.reshape(-1, width // 2), TM).reshape(sent.shape)
    grads, got = lax.optimization_barrier((grads, got))
    local = shape(frames_in.shape[1:], bf16)
    result, grad_in = pl.pallas_call(
        home_kernel,
        in_specs=[ANY] * 4,
        out_specs=(ANY,) * 2,
        out_shape=(local,) * 2,
        scratch_shapes=[
            pltpu.VMEM(sent.shape, bf16),
            pltpu.VMEM(local.shape, bf16),
            pltpu.VMEM((width, HALF), bf16),
            pltpu.VMEM((width, HALF), bf16),
            pltpu.VMEM(local.shape, bf16),
            pltpu.VMEM(local.shape, bf16),
            pltpu.SemaphoreType.DMA((4,)),
        ],
        compiler_params=vmem_params(),
        cost_estimate=pl.CostEstimate(flops=3 * 10**8, bytes_accessed=4 * 2**20, transcendentals=0),
        name="home",
    )(got, frames_in[0], w_mine, w_other)

    grads = swap(grads.reshape(-1, width), TM)
    grads, result, grad_in = lax.optimization_barrier((grads, result, grad_in))
    total = jnp.sum(grads.reshape(tm, 2, shard, width).astype(f32), axis=0)
    keep = lax.dynamic_index_in_dim(total, core, 0, keepdims=False)
    recv = exchange(lax.dynamic_index_in_dim(total, 1 - core, 0, keepdims=False))
    low = jnp.where(first, keep, recv).reshape(shard, 4, 1, HALF)
    high = jnp.where(first, recv, keep).reshape(shard, 4, 1, HALF)
    whole = jnp.concatenate([low, high], axis=2)
    grad_qkv = whole[:, :3].reshape(shard, 6 * HALF)
    grad_out = whole[:, 3].reshape(shard, 2 * HALF).T
    own_row = lax.axis_index(DP + TM) * shard
    grad_gain = jnp.sum(w_qkv.astype(f32) * grad_qkv, axis=1) / lax.dynamic_slice_in_dim(gain, own_row, shard)
    return (result[None], grad_in[None], grad_qkv, grad_out, grad_gain)


def solution(mesh):
    fine = Mesh(mesh.devices.reshape(Y_SIZE, XH_SIZE, 2, 2, 8), DP + TM)
    in_specs = (
        P(DP, TM, None, None),
        P(),
        P(DP + TM, None),
        P(None, DP + TM),
        P(DP, TM, None, None),
    )
    out_specs = (
        P(DP, TM, None, None),
        P(DP, TM, None, None),
        P(DP + TM, None),
        P(None, DP + TM),
        P(DP + TM),
    )
    return jax.shard_map(body, mesh=fine, in_specs=in_specs, out_specs=out_specs, check_vma=False)
```

time: 142 us -> 134 us (0.944)
  Pallas kernels: 27.1 us -> 21.5 us
  starting transfers between devices: 56 us -> 60 us
  local copies, waits for them, and re-layouts: 7.71 us -> 4.85 us
  waiting for transfers between devices: 45.6 us -> 43 us
    ppermute x12, waiting for transfers between devices: 21.3 us -> 10.3 us  [along_y(): lax.ppermute(value, 'y', [(i, (i + step) % Y_SIZE) for i in range(Y_SIZE)])]
    all_to_all x4, waiting for transfers between devices: 11.9 us -> 20.6 us  [swap(): return lax.all_to_all(value, axes, split_axis=0, concat_axis=0, tiled=True)]
    ppermute x6, starting transfers between devices: 7.72 us -> 12.1 us  [exchange(): return lax.ppermute(value, 'core', [(0, 1), (1, 0)])]
    pallas_call x3, Pallas kernels: 17.9 us -> 14.7 us  [the longest x1 10.7 us: body(): pl.pallas_call(functools.partial(layer_kernel, patches), in_specs=[ANY, A...]
    unnamed x45 -> x39, local copies, waits for them, and re-layouts: 5.43 us -> 4.29 us
  transfers between devices with their start and end apart: 24 -> 24, of which waited for: 13 -> 12; matrix products, arithmetic and copies ran while one was open for 3% -> 1% of each run, Pallas kernels for 18% -> 7%
where the time goes in v3:
time: 134 us; the launch traced here: 133 us
  starting transfers between devices  60 us (45%)
  waiting for transfers between devices  43 us (32%)
  Pallas kernels  21.5 us (16%)
  local copies, waits for them, and re-layouts  4.85 us (4%)
  other arithmetic  2.81 us (2%)
    all_to_all x4, starting transfers between devices, swap(): return lax.all_to_all(value, axes, split_axis=0, concat_axis=0, tiled=True)  28.6 us
    all_to_all x4, waiting for transfers between devices, swap(): return lax.all_to_all(value, axes, split_axis=0, concat_axis=0, tiled=True)  20.6 us
    ppermute x12, starting transfers between devices, along_y(): lax.ppermute(value, 'y', [(i, (i + step) % Y_SIZE) for i in range(Y_SIZE)])  15 us
    ppermute x6, starting transfers between devices, exchange(): return lax.ppermute(value, 'core', [(0, 1), (1, 0)])  12.1 us
    pallas_call x1, Pallas kernels, body(): pl.pallas_call(functools.partial(layer_kernel, patches), in_specs=[ANY, A...  10.7 us
    ppermute x12, waiting for transfers between devices, along_y(): lax.ppermute(value, 'y', [(i, (i + step) % Y_SIZE) for i in range(Y_SIZE)])  10.3 us
    ppermute x2, waiting for transfers between devices, across_x(): return lax.ppermute(value, 'xh', [(0, 1), (1, 0)])  10.1 us
    pallas_call x1, Pallas kernels, body(): pl.pallas_call(input_kernel, out_shape=shape((tm, 3 * per_peer, width //...  4.42 us
  transfers between devices with their start and end apart: 24, of which 12 were waited for; matrix products, arithmetic and copies ran while one was open for 1% of the time, Pallas kernels for 7%

profile of v3, /device:TPU:1, one launch (start us, length us, event | category | flops | bytes accessed | tf_op | source)
XLA Modules:
  0.0 133.2 jit_solution(7541651987892877771)
XLA Ops:
  0.6 0.0 copy-start
  0.6 0.0 copy-start.4
  0.7 1.5 %pack_weights.1 = bf16[16,8,1024]{2,1,0:T(8,128)(2,1)} custom-call(bf16[4,1536]{1,0:T(4,128)(2,1)} %w_qkv_ref.1, bf16[4,512]{1,0:T(4,128)(2,1)} %bitcast.49), custom_call_target="tpu_custom_call" | custom-call | bytes 262144 | tf_op jit(solution)/shard_map/pack_weights/pallas_call | solution.py:279
  2.2 10.0 %all-to-all-start = ((bf16[16,8,1024]{2,1,0:T(8,128)(2,1)}), bf16[16,8,1024]{2,1,0:T(8,128)(2,1)S(1)}, u32[]{:S(2)}, u32[]{:S(2)}) async-start(bf16[16,8,1024]{2,1,0:T(8,128)(2,1)} %pack_weights.1), calls=%async_computation | async-start | bytes 524288 | tf_op jit(solution)/shard_map/all_to_all | solution.py:253
  12.3 0.1 copy_bitcast_fusion
  12.4 8.6 %all-to-all-done = bf16[16,8,1024]{2,1,0:T(8,128)(2,1)S(1)} async-done(((bf16[16,8,1024]{2,1,0:T(8,128)(2,1)}), bf16[16,8,1024]{2,1,0:T(8,128)(2,1)S(1)}, u32[]{:S(2)}, u32[]{:S(2)}) %all-to-all-start) | async-done | bytes 262176 | tf_op jit(solution)/shard_map/all_to_all | solution.py:253
  21.0 0.1 reshape.73
  21.1 0.1 dynamic-slice_bitcast_fusion.1
  21.2 2.4 %collective-permute-start = (bf16[64,1024]{1,0:T(8,128)(2,1)S(1)}, bf16[64,1024]{1,0:T(8,128)(2,1)S(1)}, u32[]{:S(2)}, u32[]{:S(2)}) collective-permute-start(bf16[64,1024]{1,0:T(8,128)(2,1)S(1)} %reshape.75), channel_id=1, source_target_pairs={{0,16},{16,0},{1,17},{17,1},{2,18},{18,2},{3,19},{19,3},{4,20},{20... | collective-permute-start | bytes 393224 | tf_op jit(solution)/shard_map/ppermute | solution.py:249
  23.7 1.1 pad_maximum_fusion
  24.9 4.2 %all-to-all-start.1 = ((bf16[16,32,1024]{2,1,0:T(8,128)(2,1)}), bf16[16,32,1024]{2,1,0:T(8,128)(2,1)S(1)}, u32[]{:S(2)}, u32[]{:S(2)}) async-start(bf16[16,32,1024]{2,1,0:T(8,128)(2,1)} %pad_maximum_fusion), calls=%async_computation.1 | async-start | bytes 2097152 | tf_op jit(solution)/shard_map/all_to_all | solution.py:253
  29.1 2.5 %collective-permute-start.5 = (bf16[128,1024]{1,0:T(8,128)(2,1)S(1)}, bf16[128,1024]{1,0:T(8,128)(2,1)S(1)}, u32[]{:S(2)}, u32[]{:S(2)}) collective-permute-start(bf16[128,1024]{1,0:T(8,128)(2,1)S(1)} %pad_maximum_fusion.1.refs_0_), channel_id=1, source_target_pairs={{0,32},{32,0},{1,33},{33,1},{2,34},{34,2},{3,35},{35,3},{4,36},{36... | collective-permute-start | bytes 786440 | tf_op jit(solution)/shard_map/ppermute | solution.py:261
  31.7 2.7 %collective-permute-start.4 = (bf16[128,1024]{1,0:T(8,128)(2,1)S(1)}, bf16[128,1024]{1,0:T(8,128)(2,1)S(1)}, u32[]{:S(2)}, u32[]{:S(2)}) collective-permute-start(bf16[128,1024]{1,0:T(8,128)(2,1)S(1)} %pad_maximum_fusion.1.refs_0_), channel_id=1, source_target_pairs={{0,192},{64,0},{128,64},{192,128},{1,193},{65,1},{129,65},{193,129... | collective-permute-start | bytes 786440 | tf_op jit(solution)/shard_map/ppermute | solution.py:257
  34.4 0.3 collective-permute-start.3
  34.8 0.7 collective-permute-start.2
  35.4 7.6 %collective-permute-done.5.refs_4_ = bf16[128,1024]{1,0:T(8,128)(2,1)S(1)} collective-permute-done((bf16[128,1024]{1,0:T(8,128)(2,1)S(1)}, bf16[128,1024]{1,0:T(8,128)(2,1)S(1)}, u32[]{:S(2)}, u32[]{:S(2)}) %collective-permute-start.5) | collective-permute-done | bytes 262176 | tf_op jit(solution)/shard_map/ppermute | solution.py:261
  43.0 2.7 %collective-permute-start.8 = (bf16[128,1024]{1,0:T(8,128)(2,1)S(1)}, bf16[128,1024]{1,0:T(8,128)(2,1)}, u32[]{:S(2)}, u32[]{:S(2)}) collective-permute-start(bf16[128,1024]{1,0:T(8,128)(2,1)S(1)} %collective-permute-done.5.refs_4_), channel_id=1, source_target_pairs={{0,192},{64,0},{128,64},{192,128},{1,193},{65,1},{129,65},{193,129... | collective-permute-start | bytes 786440 | tf_op jit(solution)/shard_map/ppermute | solution.py:257
  45.7 0.3 collective-permute-start.7
  46.1 0.0 collective-permute-done.4.refs_3_
  46.1 0.7 collective-permute-start.6
  46.8 0.7 copy-done.17
  47.5 7.0 %all-to-all-done.1.got_own_ref.got_ref = bf16[16,32,1024]{2,1,0:T(8,128)(2,1)S(1)} async-done(((bf16[16,32,1024]{2,1,0:T(8,128)(2,1)}), bf16[16,32,1024]{2,1,0:T(8,128)(2,1)S(1)}, u32[]{:S(2)}, u32[]{:S(2)}) %all-to-all-start.1) | async-done | bytes 1048608 | tf_op jit(solution)/shard_map/all_to_all | solution.py:253
  54.5 2.7 %collective-permute-start.1 = (bf16[16,32,1024]{2,1,0:T(8,128)(2,1)S(1)}, bf16[16,32,1024]{2,1,0:T(8,128)(2,1)S(1)}, u32[]{:S(2)}, u32[]{:S(2)}) collective-permute-start(bf16[16,32,1024]{2,1,0:T(8,128)(2,1)S(1)} %all-to-all-done.1.got_own_ref.got_ref), channel_id=1, source_target_pairs={{0,16},{16,0},{1,17},{17,1},{2,18},{18,2},{3,19},{19,3},{4,20},{20... | collective-permute-start | bytes 3145736 | tf_op jit(solution)/shard_map/ppermute | solution.py:249
  57.2 4.0 %collective-permute-done.6.refs_5_ = bf16[128,1024]{1,0:T(8,128)(2,1)} collective-permute-done((bf16[128,1024]{1,0:T(8,128)(2,1)S(1)}, bf16[128,1024]{1,0:T(8,128)(2,1)}, u32[]{:S(2)}, u32[]{:S(2)}) %collective-permute-start.6) | collective-permute-done | bytes 262176 | tf_op jit(solution)/shard_map/ppermute | solution.py:257
  61.2 0.6 arrived.1.token_ref
  61.8 0.0 collective-permute-done.1.got_other_ref
  61.8 1.0 copy-done.13
  62.8 10.7 %layer.1 = (bf16[1024,256]{1,0:T(8,128)(2,1)}, bf16[256,256]{1,0:T(8,128)(2,1)}, f32[256,1024]{1,0:T(8,128)}, bf16[256,256]{1,0:T(8,128)(2,1)}, f32[256,1024]{1,...) custom-call(bf16[16,32,1024]{2,1,0:T(8,128)(2,1)} %copy-done.2, ...), custom_call_target="tpu_custom_call" | custom-call | flops 30000001024 | bytes 10485760 | tf_op jit(solution)/shard_map/layer/pallas_call | solution.py:319
  73.5 0.6 collective-permute-start.16
  74.1 1.5 %collective-permute-start.13 = (bf16[128,1024]{1,0:T(8,128)(2,1)}, bf16[128,1024]{1,0:T(8,128)(2,1)S(1)}, u32[]{:S(2)}, u32[]{:S(2)}) collective-permute-start(bf16[128,1024]{1,0:T(8,128)(2,1)} %get-tuple-element.35), channel_id=1, source_target_pairs={{0,128},{64,192},{128,0},{192,64},{1,129},{65,193},{129,1},{193,65... | collective-permute-start | bytes 786440 | tf_op jit(solution)/shard_map/ppermute | solution.py:257
  75.6 1.2 collective-permute-start.14
  76.8 0.9 collective-permute-start.17
  77.7 1.2 collective-permute-done.17.mixed_other
  78.9 0.7 copy-done.10
  79.5 0.4 copy-done.5
  79.9 4.4 %input_gradient.1 = bf16[16,48,512]{2,1,0:T(8,128)(2,1)} custom-call(bf16[16,32,1024]{2,1,0:T(8,128)(2,1)} %copy-done.2, f32[256,1024]{1,0:T(8,128)} %get-tuple-element.37.mine_ref, bf16[256,256]{1,0:T(8,128)(2,1)} %get-tuple-element.38.mixed_ref, f32[256,1024]{1,0:T(8,128)} %copy-done.5, bf16[256,256]{1,0:T(8,128)(2,1)} %copy-done.10, f32[1,1024]{1,0:T(1,128)} %bitcast.48), custom_call_target="tpu_custom_call" | custom-call | flops 1000000000 | bytes 6291456 | tf_op jit(solution)/shard_map/input_gradient/pallas_call | solution.py:362
  84.3 0.0 copy-start.6
  84.3 7.9 %all-to-all-start.2 = ((bf16[16,48,512]{2,1,0:T(8,128)(2,1)}), bf16[16,48,512]{2,1,0:T(8,128)(2,1)S(1)}, u32[]{:S(2)}, u32[]{:S(2)}) async-start(bf16[16,48,512]{2,1,0:T(8,128)(2,1)} %input_gradient.1), calls=%async_computation.2 | async-start | bytes 1572864 | tf_op jit(solution)/shard_map/all_to_all | solution.py:253
  92.3 0.0 copy-start.1
  92.3 0.6 collective-permute-start.9
  92.9 2.4 %collective-permute-start.10 = (bf16[128,1024]{1,0:T(8,128)(2,1)}, bf16[128,1024]{1,0:T(8,128)(2,1)S(1)}, u32[]{:S(2)}, u32[]{:S(2)}) collective-permute-start(bf16[128,1024]{1,0:T(8,128)(2,1)} %get-tuple-element.31), channel_id=1, source_target_pairs={{0,128},{64,192},{128,0},{192,64},{1,129},{65,193},{129,1},{193,65... | collective-permute-start | bytes 786440 | tf_op jit(solution)/shard_map/ppermute | solution.py:257
  95.3 1.8 %collective-permute-start.11 = (bf16[128,1024]{1,0:T(8,128)(2,1)S(1)}, bf16[128,1024]{1,0:T(8,128)(2,1)S(1)}, u32[]{:S(2)}, u32[]{:S(2)}) collective-permute-start(bf16[128,1024]{1,0:T(8,128)(2,1)S(1)} %copy-done.14), channel_id=1, source_target_pairs={{0,192},{64,0},{128,64},{192,128},{1,193},{65,1},{129,65},{193,129... | collective-permute-start | bytes 786440 | tf_op jit(solution)/shard_map/ppermute | solution.py:257
  97.1 0.1 add_convert_fusion
  97.2 1.8 %collective-permute-start.15 = (bf16[128,1024]{1,0:T(8,128)(2,1)S(1)}, bf16[128,1024]{1,0:T(8,128)(2,1)S(1)}, u32[]{:S(2)}, u32[]{:S(2)}) collective-permute-start(bf16[128,1024]{1,0:T(8,128)(2,1)S(1)} %add_convert_fusion), channel_id=1, source_target_pairs={{0,32},{32,0},{1,33},{33,1},{2,34},{34,2},{3,35},{35,3},{4,36},{36... | collective-permute-start | bytes 786440 | tf_op jit(solution)/shard_map/ppermute | solution.py:261
  99.1 1.8 %collective-permute-start.18 = (bf16[1024,256]{1,0:T(8,128)(2,1)S(1)}, bf16[1024,256]{1,0:T(8,128)(2,1)S(1)}, u32[]{:S(2)}, u32[]{:S(2)}) collective-permute-start(bf16[1024,256]{1,0:T(8,128)(2,1)S(1)} %copy-done.7), channel_id=1, source_target_pairs={{0,16},{16,0},{1,17},{17,1},{2,18},{18,2},{3,19},{19,3},{4,20},{20... | collective-permute-start | bytes 1572872 | tf_op jit(solution)/shard_map/ppermute | solution.py:249
  100.8 0.2 collective-permute-done.9.a_ref
  101.0 5.9 %collective-permute-done.10.b_ref = bf16[128,1024]{1,0:T(8,128)(2,1)S(1)} collective-permute-done((bf16[128,1024]{1,0:T(8,128)(2,1)}, bf16[128,1024]{1,0:T(8,128)(2,1)S(1)}, u32[]{:S(2)}, u32[]{:S(2)}) %collective-permute-start.10) | collective-permute-done | bytes 262176 | tf_op jit(solution)/shard_map/ppermute | solution.py:257
  106.9 0.3 collective-permute-done.11.c_ref
  107.2 2.6 %collective-permute-done.15.across_ref = bf16[128,1024]{1,0:T(8,128)(2,1)S(1)} collective-permute-done((bf16[128,1024]{1,0:T(8,128)(2,1)S(1)}, bf16[128,1024]{1,0:T(8,128)(2,1)S(1)}, u32[]{:S(2)}, u32[]{:S(2)}) %collective-permute-start.15) | collective-permute-done | bytes 262176 | tf_op jit(solution)/shard_map/ppermute | solution.py:261
  109.8 0.9 sum_blocks.1
  110.7 1.3 all-to-all-done.2.got_ref
  112.0 6.4 %all-to-all-start.3 = ((bf16[16,8,1024]{2,1,0:T(8,128)(2,1)}), bf16[16,8,1024]{2,1,0:T(8,128)(2,1)S(1)}, u32[]{:S(2)}, u32[]{:S(2)}) async-start(bf16[16,8,1024]{2,1,0:T(8,128)(2,1)} %sum_blocks.1), calls=%async_computation.3 | async-start | bytes 524288 | tf_op jit(solution)/shard_map/all_to_all | solution.py:253
  118.4 0.8 copy-done.8
  119.2 3.4 %home.1 = (bf16[2,128,1024]{2,1,0:T(8,128)(2,1)}, bf16[2,128,1024]{2,1,0:T(8,128)(2,1)}) custom-call(bf16[16,48,512]{2,1,0:T(8,128)(2,1)} %copy-done.3, bf16[2,128,1024]{2,1,0:T(8,128)(2,1)} %bitcast.42, bf16[1024,256]{1,0:T(8,128)(2,1)} %get-tuple-element.43.w_mine_ref, bf16[1024,256]{1,0:T(8,128)(2,1)} %copy-done.8), custom_call_target="tpu_custom_call" | custom-call | flops 300000000 | bytes 4194304 | tf_op jit(solution)/shard_map/home/pallas_call | solution.py:381
  122.5 0.0 copy-start.12
  122.5 3.6 %all-to-all-done.3 = bf16[16,8,1024]{2,1,0:T(8,128)(2,1)S(1)} async-done(((bf16[16,8,1024]{2,1,0:T(8,128)(2,1)}), bf16[16,8,1024]{2,1,0:T(8,128)(2,1)S(1)}, u32[]{:S(2)}, u32[]{:S(2)}) %all-to-all-start.3) | async-done | bytes 262176 | tf_op jit(solution)/shard_map/all_to_all | solution.py:253
  126.2 0.2 reshape.80
  126.3 0.1 reduce_sum.18
  126.4 3.7 %collective-permute-start.19 = (f32[4,1024]{1,0:T(4,128)S(1)}, f32[4,1024]{1,0:T(4,128)S(1)}, u32[]{:S(2)}, u32[]{:S(2)}) collective-permute-start(f32[4,1024]{1,0:T(4,128)S(1)} %dynamic-slice_bitcast_fusion.2), channel_id=1, source_target_pairs={{0,16},{16,0},{1,17},{17,1},{2,18},{18,2},{3,19},{19,3},{4,20},{20... | collective-permute-start | bytes 49160 | tf_op jit(solution)/shard_map/ppermute | solution.py:249
  130.2 0.8 collective-permute-done.19
  131.1 0.6 copy.27
  131.8 0.0 copy-start.11
  131.8 0.1 multiply_reduce_fusion
  131.9 1.3 dynamic-slice_divide_fusion
  (50 shorter events, 0.3 us)
Async XLA Ops:
  0.6 11.6 %copy-start = (bf16[1,2,128,1024]{3,2,1,0:T(8,128)(2,1)S(1)}, bf16[1,2,128,1024]{3,2,1,0:T(8,128)(2,1)}, u32[]{:S(2)}) copy-start(bf16[1,2,128,1024]{3,2,1,0:T(8,128)(2,1)} %param.9) | copy-start | bytes 1572868
  0.6 11.6 %copy-start.4 = (bf16[1,2,128,1024]{3,2,1,0:T(8,128)(2,1)S(1)}, bf16[1,2,128,1024]{3,2,1,0:T(8,128)(2,1)}, u32[]{:S(2)}) copy-start(bf16[1,2,128,1024]{3,2,1,0:T(8,128)(2,1)} %param.5) | copy-start | bytes 1572868
  2.2 18.8 %all-to-all-start = ((bf16[16,8,1024]{2,1,0:T(8,128)(2,1)}), bf16[16,8,1024]{2,1,0:T(8,128)(2,1)S(1)}, u32[]{:S(2)}, u32[]{:S(2)}) async-start(bf16[16,8,1024]{2,1,0:T(8,128)(2,1)} %pack_weights.1), calls=%async_computation | async-start | bytes 524288 | tf_op jit(solution)/shard_map/all_to_all | solution.py:253
  21.2 3.6 %collective-permute-start = (bf16[64,1024]{1,0:T(8,128)(2,1)S(1)}, bf16[64,1024]{1,0:T(8,128)(2,1)S(1)}, u32[]{:S(2)}, u32[]{:S(2)}) collective-permute-start(bf16[64,1024]{1,0:T(8,128)(2,1)S(1)} %reshape.75), channel_id=1, source_target_pairs={{0,16},{16,0},{1,17},{17,1},{2,18},{18,2},{3,19},{19,3},{4,20},{20... | collective-permute-start | bytes 393224 | tf_op jit(solution)/shard_map/ppermute | solution.py:249
  24.9 36.3 %copy-start.9 = (bf16[128,1024]{1,0:T(8,128)(2,1)}, bf16[128,1024]{1,0:T(8,128)(2,1)S(1)}, u32[]{:S(2)}) copy-start(bf16[128,1024]{1,0:T(8,128)(2,1)S(1)} %pad_maximum_fusion.1.refs_0_) | copy-start | bytes 786436
  24.9 29.6 %all-to-all-start.1 = ((bf16[16,32,1024]{2,1,0:T(8,128)(2,1)}), bf16[16,32,1024]{2,1,0:T(8,128)(2,1)S(1)}, u32[]{:S(2)}, u32[]{:S(2)}) async-start(bf16[16,32,1024]{2,1,0:T(8,128)(2,1)} %pad_maximum_fusion), calls=%async_computation.1 | async-start | bytes 2097152 | tf_op jit(solution)/shard_map/all_to_all | solution.py:253
  29.1 13.9 %collective-permute-start.5 = (bf16[128,1024]{1,0:T(8,128)(2,1)S(1)}, bf16[128,1024]{1,0:T(8,128)(2,1)S(1)}, u32[]{:S(2)}, u32[]{:S(2)}) collective-permute-start(bf16[128,1024]{1,0:T(8,128)(2,1)S(1)} %pad_maximum_fusion.1.refs_0_), channel_id=1, source_target_pairs={{0,32},{32,0},{1,33},{33,1},{2,34},{34,2},{3,35},{35,3},{4,36},{36... | collective-permute-start | bytes 786440 | tf_op jit(solution)/shard_map/ppermute | solution.py:261
  31.7 14.4 %collective-permute-start.4 = (bf16[128,1024]{1,0:T(8,128)(2,1)S(1)}, bf16[128,1024]{1,0:T(8,128)(2,1)S(1)}, u32[]{:S(2)}, u32[]{:S(2)}) collective-permute-start(bf16[128,1024]{1,0:T(8,128)(2,1)S(1)} %pad_maximum_fusion.1.refs_0_), channel_id=1, source_target_pairs={{0,192},{64,0},{128,64},{192,128},{1,193},{65,1},{129,65},{193,129... | collective-permute-start | bytes 786440 | tf_op jit(solution)/shard_map/ppermute | solution.py:257
  34.4 12.4 %collective-permute-start.3 = (bf16[128,1024]{1,0:T(8,128)(2,1)S(1)}, bf16[128,1024]{1,0:T(8,128)(2,1)S(1)}, u32[]{:S(2)}, u32[]{:S(2)}) collective-permute-start(bf16[128,1024]{1,0:T(8,128)(2,1)S(1)} %pad_maximum_fusion.1.refs_0_), channel_id=1, source_target_pairs={{0,128},{64,192},{128,0},{192,64},{1,129},{65,193},{129,1},{193,65... | collective-permute-start | bytes 786440 | tf_op jit(solution)/shard_map/ppermute | solution.py:257
  34.8 22.5 %collective-permute-start.2 = (bf16[128,1024]{1,0:T(8,128)(2,1)S(1)}, bf16[128,1024]{1,0:T(8,128)(2,1)}, u32[]{:S(2)}, u32[]{:S(2)}) collective-permute-start(bf16[128,1024]{1,0:T(8,128)(2,1)S(1)} %pad_maximum_fusion.1.refs_0_), channel_id=1, source_target_pairs={{0,64},{64,128},{128,192},{192,0},{1,65},{65,129},{129,193},{193,1... | collective-permute-start | bytes 786440 | tf_op jit(solution)/shard_map/ppermute | solution.py:257
  43.0 18.2 %copy-start.15 = (bf16[128,1024]{1,0:T(8,128)(2,1)}, bf16[128,1024]{1,0:T(8,128)(2,1)S(1)}, u32[]{:S(2)}) copy-start(bf16[128,1024]{1,0:T(8,128)(2,1)S(1)} %collective-permute-done.5.refs_4_) | copy-start | bytes 786436
  43.0 14.2 %collective-permute-start.8 = (bf16[128,1024]{1,0:T(8,128)(2,1)S(1)}, bf16[128,1024]{1,0:T(8,128)(2,1)}, u32[]{:S(2)}, u32[]{:S(2)}) collective-permute-start(bf16[128,1024]{1,0:T(8,128)(2,1)S(1)} %collective-permute-done.5.refs_4_), channel_id=1, source_target_pairs={{0,192},{64,0},{128,64},{192,128},{1,193},{65,1},{129,65},{193,129... | collective-permute-start | bytes 786440 | tf_op jit(solution)/shard_map/ppermute | solution.py:257
  45.7 11.5 %collective-permute-start.7 = (bf16[128,1024]{1,0:T(8,128)(2,1)S(1)}, bf16[128,1024]{1,0:T(8,128)(2,1)}, u32[]{:S(2)}, u32[]{:S(2)}) collective-permute-start(bf16[128,1024]{1,0:T(8,128)(2,1)S(1)} %collective-permute-done.5.refs_4_), channel_id=1, source_target_pairs={{0,128},{64,192},{128,0},{192,64},{1,129},{65,193},{129,1},{193,65... | collective-permute-start | bytes 786440 | tf_op jit(solution)/shard_map/ppermute | solution.py:257
  46.1 15.1 %copy-start.16 = (bf16[128,1024]{1,0:T(8,128)(2,1)}, bf16[128,1024]{1,0:T(8,128)(2,1)S(1)}, u32[]{:S(2)}) copy-start(bf16[128,1024]{1,0:T(8,128)(2,1)S(1)} %collective-permute-done.4.refs_3_) | copy-start | bytes 786436
  46.1 15.1 %collective-permute-start.6 = (bf16[128,1024]{1,0:T(8,128)(2,1)S(1)}, bf16[128,1024]{1,0:T(8,128)(2,1)}, u32[]{:S(2)}, u32[]{:S(2)}) collective-permute-start(bf16[128,1024]{1,0:T(8,128)(2,1)S(1)} %collective-permute-done.5.refs_4_), channel_id=1, source_target_pairs={{0,64},{64,128},{128,192},{192,0},{1,65},{65,129},{129,193},{193,1... | collective-permute-start | bytes 786440 | tf_op jit(solution)/shard_map/ppermute | solution.py:257
  46.8 0.7 copy-start.17
  54.5 7.3 %copy-start.2 = (bf16[16,32,1024]{2,1,0:T(8,128)(2,1)}, bf16[16,32,1024]{2,1,0:T(8,128)(2,1)S(1)}, u32[]{:S(2)}) copy-start(bf16[16,32,1024]{2,1,0:T(8,128)(2,1)S(1)} %all-to-all-done.1.got_own_ref.got_ref) | copy-start | bytes 3145732
  54.5 7.3 %collective-permute-start.1 = (bf16[16,32,1024]{2,1,0:T(8,128)(2,1)S(1)}, bf16[16,32,1024]{2,1,0:T(8,128)(2,1)S(1)}, u32[]{:S(2)}, u32[]{:S(2)}) collective-permute-start(bf16[16,32,1024]{2,1,0:T(8,128)(2,1)S(1)} %all-to-all-done.1.got_own_ref.got_ref), channel_id=1, source_target_pairs={{0,16},{16,0},{1,17},{17,1},{2,18},{18,2},{3,19},{19,3},{4,20},{20... | collective-permute-start | bytes 3145736 | tf_op jit(solution)/shard_map/ppermute | solution.py:249
  61.8 1.0 copy-start.13
  73.5 5.4 %collective-permute-start.16 = (f32[256,1024]{1,0:T(8,128)}, f32[256,1024]{1,0:T(8,128)S(1)}, u32[]{:S(2)}, u32[]{:S(2)}) collective-permute-start(f32[256,1024]{1,0:T(8,128)} %get-tuple-element.39), channel_id=1, source_target_pairs={{0,16},{16,0},{1,17},{17,1},{2,18},{18,2},{3,19},{19,3},{4,20},{20... | collective-permute-start | bytes 3145736 | tf_op jit(solution)/shard_map/ppermute | solution.py:249
  74.1 21.2 %collective-permute-start.12 = (bf16[128,1024]{1,0:T(8,128)(2,1)}, bf16[128,1024]{1,0:T(8,128)(2,1)S(1)}, u32[]{:S(2)}, u32[]{:S(2)}) collective-permute-start(bf16[128,1024]{1,0:T(8,128)(2,1)} %get-tuple-element.34), channel_id=1, source_target_pairs={{0,64},{64,128},{128,192},{192,0},{1,65},{65,129},{129,193},{193,1... | collective-permute-start | bytes 786440 | tf_op jit(solution)/shard_map/ppermute | solution.py:257
  74.1 23.0 %collective-permute-start.13 = (bf16[128,1024]{1,0:T(8,128)(2,1)}, bf16[128,1024]{1,0:T(8,128)(2,1)S(1)}, u32[]{:S(2)}, u32[]{:S(2)}) collective-permute-start(bf16[128,1024]{1,0:T(8,128)(2,1)} %get-tuple-element.35), channel_id=1, source_target_pairs={{0,128},{64,192},{128,0},{192,64},{1,129},{65,193},{129,1},{193,65... | collective-permute-start | bytes 786440 | tf_op jit(solution)/shard_map/ppermute | solution.py:257
  75.6 21.5 %collective-permute-start.14 = (bf16[128,1024]{1,0:T(8,128)(2,1)}, bf16[128,1024]{1,0:T(8,128)(2,1)S(1)}, u32[]{:S(2)}, u32[]{:S(2)}) collective-permute-start(bf16[128,1024]{1,0:T(8,128)(2,1)} %get-tuple-element.36), channel_id=1, source_target_pairs={{0,192},{64,0},{128,64},{192,128},{1,193},{65,1},{129,65},{193,129... | collective-permute-start | bytes 786440 | tf_op jit(solution)/shard_map/ppermute | solution.py:257
  76.8 2.1 %collective-permute-start.17 = (bf16[256,256]{1,0:T(8,128)(2,1)}, bf16[256,256]{1,0:T(8,128)(2,1)S(1)}, u32[]{:S(2)}, u32[]{:S(2)}) collective-permute-start(bf16[256,256]{1,0:T(8,128)(2,1)} %get-tuple-element.40), channel_id=1, source_target_pairs={{0,16},{16,0},{1,17},{17,1},{2,18},{18,2},{3,19},{19,3},{4,20},{20... | collective-permute-start | bytes 393224 | tf_op jit(solution)/shard_map/ppermute | solution.py:249
  78.9 0.7 copy-start.10
  78.9 1.0 copy-start.5
  84.3 11.0 %copy-start.14 = (bf16[128,1024]{1,0:T(8,128)(2,1)S(1)}, bf16[128,1024]{1,0:T(8,128)(2,1)}, u32[]{:S(2)}) copy-start(bf16[128,1024]{1,0:T(8,128)(2,1)} %get-tuple-element.32) | copy-start | bytes 786436
  84.3 12.8 %copy-start.6 = (f32[128,1024]{1,0:T(8,128)S(1)}, f32[128,1024]{1,0:T(8,128)}, u32[]{:S(2)}) copy-start(f32[128,1024]{1,0:T(8,128)} %get-tuple-element.33) | copy-start | bytes 1572868
  84.3 27.6 %all-to-all-start.2 = ((bf16[16,48,512]{2,1,0:T(8,128)(2,1)}), bf16[16,48,512]{2,1,0:T(8,128)(2,1)S(1)}, u32[]{:S(2)}, u32[]{:S(2)}) async-start(bf16[16,48,512]{2,1,0:T(8,128)(2,1)} %input_gradient.1), calls=%async_computation.2 | async-start | bytes 1572864 | tf_op jit(solution)/shard_map/all_to_all | solution.py:253
  92.3 6.8 %copy-start.7 = (bf16[1024,256]{1,0:T(8,128)(2,1)S(1)}, bf16[1024,256]{1,0:T(8,128)(2,1)}, u32[]{:S(2)}) copy-start(bf16[1024,256]{1,0:T(8,128)(2,1)} %get-tuple-element.43.w_mine_ref) | copy-start | bytes 1572868
  92.3 17.5 %copy-start.1 = (f32[128,1024]{1,0:T(8,128)S(1)}, f32[128,1024]{1,0:T(8,128)}, u32[]{:S(2)}) copy-start(f32[128,1024]{1,0:T(8,128)} %get-tuple-element.29.own_ref) | copy-start | bytes 1572868
  92.3 8.7 %collective-permute-start.9 = (bf16[128,1024]{1,0:T(8,128)(2,1)}, bf16[128,1024]{1,0:T(8,128)(2,1)S(1)}, u32[]{:S(2)}, u32[]{:S(2)}) collective-permute-start(bf16[128,1024]{1,0:T(8,128)(2,1)} %get-tuple-element.30), channel_id=1, source_target_pairs={{0,64},{64,128},{128,192},{192,0},{1,65},{65,129},{129,193},{193,1... | collective-permute-start | bytes 786440 | tf_op jit(solution)/shard_map/ppermute | solution.py:257
  92.9 14.0 %collective-permute-start.10 = (bf16[128,1024]{1,0:T(8,128)(2,1)}, bf16[128,1024]{1,0:T(8,128)(2,1)S(1)}, u32[]{:S(2)}, u32[]{:S(2)}) collective-permute-start(bf16[128,1024]{1,0:T(8,128)(2,1)} %get-tuple-element.31), channel_id=1, source_target_pairs={{0,128},{64,192},{128,0},{192,64},{1,129},{65,193},{129,1},{193,65... | collective-permute-start | bytes 786440 | tf_op jit(solution)/shard_map/ppermute | solution.py:257
  95.3 11.9 %collective-permute-start.11 = (bf16[128,1024]{1,0:T(8,128)(2,1)S(1)}, bf16[128,1024]{1,0:T(8,128)(2,1)S(1)}, u32[]{:S(2)}, u32[]{:S(2)}) collective-permute-start(bf16[128,1024]{1,0:T(8,128)(2,1)S(1)} %copy-done.14), channel_id=1, source_target_pairs={{0,192},{64,0},{128,64},{192,128},{1,193},{65,1},{129,65},{193,129... | collective-permute-start | bytes 786440 | tf_op jit(solution)/shard_map/ppermute | solution.py:257
  97.2 12.5 %collective-permute-start.15 = (bf16[128,1024]{1,0:T(8,128)(2,1)S(1)}, bf16[128,1024]{1,0:T(8,128)(2,1)S(1)}, u32[]{:S(2)}, u32[]{:S(2)}) collective-permute-start(bf16[128,1024]{1,0:T(8,128)(2,1)S(1)} %add_convert_fusion), channel_id=1, source_target_pairs={{0,32},{32,0},{1,33},{33,1},{2,34},{34,2},{3,35},{35,3},{4,36},{36... | collective-permute-start | bytes 786440 | tf_op jit(solution)/shard_map/ppermute | solution.py:261
  99.1 19.2 %collective-permute-start.18 = (bf16[1024,256]{1,0:T(8,128)(2,1)S(1)}, bf16[1024,256]{1,0:T(8,128)(2,1)S(1)}, u32[]{:S(2)}, u32[]{:S(2)}) collective-permute-start(bf16[1024,256]{1,0:T(8,128)(2,1)S(1)} %copy-done.7), channel_id=1, source_target_pairs={{0,16},{16,0},{1,17},{17,1},{2,18},{18,2},{3,19},{19,3},{4,20},{20... | collective-permute-start | bytes 1572872 | tf_op jit(solution)/shard_map/ppermute | solution.py:249
  112.0 6.4 %copy-start.3 = (bf16[16,48,512]{2,1,0:T(8,128)(2,1)}, bf16[16,48,512]{2,1,0:T(8,128)(2,1)S(1)}, u32[]{:S(2)}) copy-start(bf16[16,48,512]{2,1,0:T(8,128)(2,1)S(1)} %all-to-all-done.2.got_ref) | copy-start | bytes 2359300
  112.0 14.2 %all-to-all-start.3 = ((bf16[16,8,1024]{2,1,0:T(8,128)(2,1)}), bf16[16,8,1024]{2,1,0:T(8,128)(2,1)S(1)}, u32[]{:S(2)}, u32[]{:S(2)}) async-start(bf16[16,8,1024]{2,1,0:T(8,128)(2,1)} %sum_blocks.1), calls=%async_computation.3 | async-start | bytes 524288 | tf_op jit(solution)/shard_map/all_to_all | solution.py:253
  118.3 0.8 copy-start.8
  122.5 9.2 %copy-start.12 = (bf16[4,1536]{1,0:T(4,128)(2,1)S(1)}, bf16[4,1536]{1,0:T(4,128)(2,1)}, u32[]{:S(2)}) copy-start(bf16[4,1536]{1,0:T(4,128)(2,1)} %w_qkv_ref.1) | copy-start | bytes 36868
  126.4 4.6 %collective-permute-start.19 = (f32[4,1024]{1,0:T(4,128)S(1)}, f32[4,1024]{1,0:T(4,128)S(1)}, u32[]{:S(2)}, u32[]{:S(2)}) collective-permute-start(f32[4,1024]{1,0:T(4,128)S(1)} %dynamic-slice_bitcast_fusion.2), channel_id=1, source_target_pairs={{0,16},{16,0},{1,17},{17,1},{2,18},{18,2},{3,19},{19,3},{4,20},{20... | collective-permute-start | bytes 49160 | tf_op jit(solution)/shard_map/ppermute | solution.py:249
  131.8 1.4 %copy-start.11 = (f32[4,1536]{1,0:T(4,128)}, f32[4,1536]{1,0:T(4,128)S(1)}, u32[]{:S(2)}) copy-start(f32[4,1536]{1,0:T(4,128)S(1)} %reshape.79) | copy-start | bytes 73732

commit v4 on v3

--- a/solution.py
+++ b/solution.py
@@ -339,7 +339,7 @@
             pltpu.SemaphoreType.DMA((10,)),
             pltpu.SemaphoreType.DMA((13,)),
         ],
-        compiler_params=vmem_params(),
+        compiler_params=vmem_params(60),
         cost_estimate=pl.CostEstimate(flops=3 * 10**10, bytes_accessed=10 * 2**20, transcendentals=2**19),
         name="layer",
     )(got, got_other, gain_row, token, *pieces)
@@ -371,7 +371,7 @@
             pltpu.VMEM((tm, 3 * per_peer, width // 2), bf16),
             pltpu.SemaphoreType.DMA((11,)),
         ],
-        compiler_params=vmem_params(56),
+        compiler_params=vmem_params(24),
         cost_estimate=pl.CostEstimate(flops=10**9, bytes_accessed=6 * 2**20, transcendentals=0),
         name="input_gradient",
     )(got, d_normed, mixed, d_normed_other, mixed_other, gain_row)

time: 134 us -> 132 us (0.985)
  Pallas kernels: 21.5 us -> 19.1 us
    pallas_call x1, Pallas kernels: 4.42 us -> 1.93 us  [body(): pl.pallas_call(input_kernel, out_shape=shape((tm, 3 * per_peer, width //...]
    unnamed x39 -> x43, local copies, waits for them, and re-layouts: 4.29 us -> 5.4 us
  transfers between devices with their start and end apart: 24 -> 24, of which waited for: 12 -> 12; matrix products, arithmetic and copies ran while one was open for 1% -> 1% of each run, Pallas kernels for 7% -> 5%
where the time goes in v4:
time: 132 us; the launch traced here: 131 us
  starting transfers between devices  60.1 us (46%)
  waiting for transfers between devices  43 us (33%)
  Pallas kernels  19.1 us (14%)
  local copies, waits for them, and re-layouts  5.98 us (5%)
  other arithmetic  2.11 us (2%)
    all_to_all x4, starting transfers between devices, swap(): return lax.all_to_all(value, axes, split_axis=0, concat_axis=0, tiled=True)  28.6 us
    all_to_all x4, waiting for transfers between devices, swap(): return lax.all_to_all(value, axes, split_axis=0, concat_axis=0, tiled=True)  20.5 us
    ppermute x12, starting transfers between devices, along_y(): lax.ppermute(value, 'y', [(i, (i + step) % Y_SIZE) for i in range(Y_SIZE)])  15 us
    ppermute x6, starting transfers between devices, exchange(): return lax.ppermute(value, 'core', [(0, 1), (1, 0)])  12.1 us
    pallas_call x1, Pallas kernels, body(): pl.pallas_call(functools.partial(layer_kernel, patches), in_specs=[ANY, A...  10.8 us
    ppermute x12, waiting for transfers between devices, along_y(): lax.ppermute(value, 'y', [(i, (i + step) % Y_SIZE) for i in range(Y_SIZE)])  10.3 us
    ppermute x2, waiting for transfers between devices, across_x(): return lax.ppermute(value, 'xh', [(0, 1), (1, 0)])  10.1 us
    unnamed x43, local copies, waits for them, and re-layouts  5.4 us
  transfers between devices with their start and end apart: 24, of which 12 were waited for; matrix products, arithmetic and copies ran while one was open for 1% of the time, Pallas kernels for 5%

profile of v4, /device:TPU:1, one launch (start us, length us, event | category | flops | bytes accessed | tf_op | source)
XLA Modules:
  0.0 131.2 jit_solution(6118482209647997976)
XLA Ops:
  0.6 0.0 copy-start
  0.6 0.0 copy-start.8
  0.7 1.5 %pack_weights.1 = bf16[16,8,1024]{2,1,0:T(8,128)(2,1)} custom-call(bf16[4,1536]{1,0:T(4,128)(2,1)} %w_qkv_ref.1, bf16[4,512]{1,0:T(4,128)(2,1)} %bitcast.49), custom_call_target="tpu_custom_call" | custom-call | bytes 262144 | tf_op jit(solution)/shard_map/pack_weights/pallas_call | solution.py:279
  2.2 10.0 %all-to-all-start = ((bf16[16,8,1024]{2,1,0:T(8,128)(2,1)}), bf16[16,8,1024]{2,1,0:T(8,128)(2,1)S(1)}, u32[]{:S(2)}, u32[]{:S(2)}) async-start(bf16[16,8,1024]{2,1,0:T(8,128)(2,1)} %pack_weights.1), calls=%async_computation | async-start | bytes 524288 | tf_op jit(solution)/shard_map/all_to_all | solution.py:253
  12.3 0.1 copy_bitcast_fusion
  12.4 8.6 %all-to-all-done = bf16[16,8,1024]{2,1,0:T(8,128)(2,1)S(1)} async-done(((bf16[16,8,1024]{2,1,0:T(8,128)(2,1)}), bf16[16,8,1024]{2,1,0:T(8,128)(2,1)S(1)}, u32[]{:S(2)}, u32[]{:S(2)}) %all-to-all-start) | async-done | bytes 262176 | tf_op jit(solution)/shard_map/all_to_all | solution.py:253
  21.0 0.1 reshape.73
  21.1 0.1 dynamic-slice_bitcast_fusion.1
  21.2 2.4 %collective-permute-start = (bf16[64,1024]{1,0:T(8,128)(2,1)S(1)}, bf16[64,1024]{1,0:T(8,128)(2,1)S(1)}, u32[]{:S(2)}, u32[]{:S(2)}) collective-permute-start(bf16[64,1024]{1,0:T(8,128)(2,1)S(1)} %reshape.75), channel_id=1, source_target_pairs={{0,16},{16,0},{1,17},{17,1},{2,18},{18,2},{3,19},{19,3},{4,20},{20... | collective-permute-start | bytes 393224 | tf_op jit(solution)/shard_map/ppermute | solution.py:249
  23.7 1.1 pad_maximum_fusion
  24.8 0.0 collective-permute-done
  24.9 4.2 %all-to-all-start.1 = ((bf16[16,32,1024]{2,1,0:T(8,128)(2,1)}), bf16[16,32,1024]{2,1,0:T(8,128)(2,1)S(1)}, u32[]{:S(2)}, u32[]{:S(2)}) async-start(bf16[16,32,1024]{2,1,0:T(8,128)(2,1)} %pad_maximum_fusion), calls=%async_computation.1 | async-start | bytes 2097152 | tf_op jit(solution)/shard_map/all_to_all | solution.py:253
  29.1 2.5 %collective-permute-start.5 = (bf16[128,1024]{1,0:T(8,128)(2,1)S(1)}, bf16[128,1024]{1,0:T(8,128)(2,1)S(1)}, u32[]{:S(2)}, u32[]{:S(2)}) collective-permute-start(bf16[128,1024]{1,0:T(8,128)(2,1)S(1)} %pad_maximum_fusion.1.refs_0_), channel_id=1, source_target_pairs={{0,32},{32,0},{1,33},{33,1},{2,34},{34,2},{3,35},{35,3},{4,36},{36... | collective-permute-start | bytes 786440 | tf_op jit(solution)/shard_map/ppermute | solution.py:261
  31.7 2.7 %collective-permute-start.4 = (bf16[128,1024]{1,0:T(8,128)(2,1)S(1)}, bf16[128,1024]{1,0:T(8,128)(2,1)S(1)}, u32[]{:S(2)}, u32[]{:S(2)}) collective-permute-start(bf16[128,1024]{1,0:T(8,128)(2,1)S(1)} %pad_maximum_fusion.1.refs_0_), channel_id=1, source_target_pairs={{0,192},{64,0},{128,64},{192,128},{1,193},{65,1},{129,65},{193,129... | collective-permute-start | bytes 786440 | tf_op jit(solution)/shard_map/ppermute | solution.py:257
  34.4 0.3 collective-permute-start.3
  34.7 0.7 collective-permute-start.2
  35.4 7.5 %collective-permute-done.5.refs_4_ = bf16[128,1024]{1,0:T(8,128)(2,1)S(1)} collective-permute-done((bf16[128,1024]{1,0:T(8,128)(2,1)S(1)}, bf16[128,1024]{1,0:T(8,128)(2,1)S(1)}, u32[]{:S(2)}, u32[]{:S(2)}) %collective-permute-start.5) | collective-permute-done | bytes 262176 | tf_op jit(solution)/shard_map/ppermute | solution.py:261
  43.0 2.7 %collective-permute-start.8 = (bf16[128,1024]{1,0:T(8,128)(2,1)S(1)}, bf16[128,1024]{1,0:T(8,128)(2,1)}, u32[]{:S(2)}, u32[]{:S(2)}) collective-permute-start(bf16[128,1024]{1,0:T(8,128)(2,1)S(1)} %collective-permute-done.5.refs_4_), channel_id=1, source_target_pairs={{0,192},{64,0},{128,64},{192,128},{1,193},{65,1},{129,65},{193,129... | collective-permute-start | bytes 786440 | tf_op jit(solution)/shard_map/ppermute | solution.py:257
  45.7 0.3 collective-permute-start.7
  46.1 0.0 collective-permute-done.4.refs_3_
  46.1 0.7 collective-permute-start.6
  46.8 0.7 copy-done.19
  47.5 7.0 %all-to-all-done.1.got_own_ref.got_ref = bf16[16,32,1024]{2,1,0:T(8,128)(2,1)S(1)} async-done(((bf16[16,32,1024]{2,1,0:T(8,128)(2,1)}), bf16[16,32,1024]{2,1,0:T(8,128)(2,1)S(1)}, u32[]{:S(2)}, u32[]{:S(2)}) %all-to-all-start.1) | async-done | bytes 1048608 | tf_op jit(solution)/shard_map/all_to_all | solution.py:253
  54.5 2.7 %collective-permute-start.1 = (bf16[16,32,1024]{2,1,0:T(8,128)(2,1)S(1)}, bf16[16,32,1024]{2,1,0:T(8,128)(2,1)S(1)}, u32[]{:S(2)}, u32[]{:S(2)}) collective-permute-start(bf16[16,32,1024]{2,1,0:T(8,128)(2,1)S(1)} %all-to-all-done.1.got_own_ref.got_ref), channel_id=1, source_target_pairs={{0,16},{16,0},{1,17},{17,1},{2,18},{18,2},{3,19},{19,3},{4,20},{20... | collective-permute-start | bytes 3145736 | tf_op jit(solution)/shard_map/ppermute | solution.py:249
  57.2 3.9 %collective-permute-done.6.refs_5_ = bf16[128,1024]{1,0:T(8,128)(2,1)} collective-permute-done((bf16[128,1024]{1,0:T(8,128)(2,1)S(1)}, bf16[128,1024]{1,0:T(8,128)(2,1)}, u32[]{:S(2)}, u32[]{:S(2)}) %collective-permute-start.6) | collective-permute-done | bytes 262176 | tf_op jit(solution)/shard_map/ppermute | solution.py:257
  61.2 0.6 arrived.1.token_ref
  61.8 1.0 copy-done.15
  62.8 10.8 %layer.1 = (bf16[1024,256]{1,0:T(8,128)(2,1)}, bf16[256,256]{1,0:T(8,128)(2,1)}, f32[256,1024]{1,0:T(8,128)}, bf16[256,256]{1,0:T(8,128)(2,1)}, f32[256,1024]{1,...) custom-call(bf16[16,32,1024]{2,1,0:T(8,128)(2,1)} %copy-done.1, ...), custom_call_target="tpu_custom_call" | custom-call | flops 30000001024 | bytes 10485760 | tf_op jit(solution)/shard_map/layer/pallas_call | solution.py:319
  73.5 0.6 collective-permute-start.16
  74.1 1.5 %collective-permute-start.13 = (bf16[128,1024]{1,0:T(8,128)(2,1)}, bf16[128,1024]{1,0:T(8,128)(2,1)S(1)}, u32[]{:S(2)}, u32[]{:S(2)}) collective-permute-start(bf16[128,1024]{1,0:T(8,128)(2,1)} %get-tuple-element.35), channel_id=1, source_target_pairs={{0,128},{64,192},{128,0},{192,64},{1,129},{65,193},{129,1},{193,65... | collective-permute-start | bytes 786440 | tf_op jit(solution)/shard_map/ppermute | solution.py:257
  75.6 1.2 collective-permute-start.14
  76.8 0.9 collective-permute-start.17
  77.7 1.2 collective-permute-done.17.mixed_other
  78.9 1.2 copy-done.3
  80.1 0.9 copy-done.4
  81.0 1.9 %input_gradient.1 = bf16[16,48,512]{2,1,0:T(8,128)(2,1)} custom-call(bf16[16,32,1024]{2,1,0:T(8,128)(2,1)S(1)} %copy-done.2, f32[256,1024]{1,0:T(8,128)S(1)} %copy-done.3, bf16[256,256]{1,0:T(8,128)(2,1)S(1)} %copy-done.4, f32[256,1024]{1,0:T(8,128)S(1)} %collective-permute-done.16.other, bf16[256,256]{1,0:T(8,128)(2,1)S(1)} %collective-permute-done.17.mixed_other, ...), custom_call_target="tpu_custom_call" | custom-call | flops 1000000000 | bytes 6291456 | tf_op jit(solution)/shard_map/input_gradient/pallas_call | solution.py:362
  83.0 0.0 copy-start.9
  83.0 7.9 %all-to-all-start.2 = ((bf16[16,48,512]{2,1,0:T(8,128)(2,1)}), bf16[16,48,512]{2,1,0:T(8,128)(2,1)S(1)}, u32[]{:S(2)}, u32[]{:S(2)}) async-start(bf16[16,48,512]{2,1,0:T(8,128)(2,1)} %input_gradient.1), calls=%async_computation.2 | async-start | bytes 1572864 | tf_op jit(solution)/shard_map/all_to_all | solution.py:253
  90.9 0.0 copy-start.6
  90.9 0.6 collective-permute-start.9
  91.6 2.4 %collective-permute-start.10 = (bf16[128,1024]{1,0:T(8,128)(2,1)}, bf16[128,1024]{1,0:T(8,128)(2,1)S(1)}, u32[]{:S(2)}, u32[]{:S(2)}) collective-permute-start(bf16[128,1024]{1,0:T(8,128)(2,1)} %get-tuple-element.31), channel_id=1, source_target_pairs={{0,128},{64,192},{128,0},{192,64},{1,129},{65,193},{129,1},{193,65... | collective-permute-start | bytes 786440 | tf_op jit(solution)/shard_map/ppermute | solution.py:257
  94.0 1.8 %collective-permute-start.11 = (bf16[128,1024]{1,0:T(8,128)(2,1)S(1)}, bf16[128,1024]{1,0:T(8,128)(2,1)S(1)}, u32[]{:S(2)}, u32[]{:S(2)}) collective-permute-start(bf16[128,1024]{1,0:T(8,128)(2,1)S(1)} %copy-done.16), channel_id=1, source_target_pairs={{0,192},{64,0},{128,64},{192,128},{1,193},{65,1},{129,65},{193,129... | collective-permute-start | bytes 786440 | tf_op jit(solution)/shard_map/ppermute | solution.py:257
  95.7 0.1 add_convert_fusion
  95.9 1.8 %collective-permute-start.15 = (bf16[128,1024]{1,0:T(8,128)(2,1)S(1)}, bf16[128,1024]{1,0:T(8,128)(2,1)S(1)}, u32[]{:S(2)}, u32[]{:S(2)}) collective-permute-start(bf16[128,1024]{1,0:T(8,128)(2,1)S(1)} %add_convert_fusion), channel_id=1, source_target_pairs={{0,32},{32,0},{1,33},{33,1},{2,34},{34,2},{3,35},{35,3},{4,36},{36... | collective-permute-start | bytes 786440 | tf_op jit(solution)/shard_map/ppermute | solution.py:261
  97.7 1.8 %collective-permute-start.18 = (bf16[1024,256]{1,0:T(8,128)(2,1)S(1)}, bf16[1024,256]{1,0:T(8,128)(2,1)S(1)}, u32[]{:S(2)}, u32[]{:S(2)}) collective-permute-start(bf16[1024,256]{1,0:T(8,128)(2,1)S(1)} %copy-done.10), channel_id=1, source_target_pairs={{0,16},{16,0},{1,17},{17,1},{2,18},{18,2},{3,19},{19,3},{4,20},{20... | collective-permute-start | bytes 1572872 | tf_op jit(solution)/shard_map/ppermute | solution.py:249
  99.5 0.2 collective-permute-done.9.a_ref
  99.6 5.9 %collective-permute-done.10.b_ref = bf16[128,1024]{1,0:T(8,128)(2,1)S(1)} collective-permute-done((bf16[128,1024]{1,0:T(8,128)(2,1)}, bf16[128,1024]{1,0:T(8,128)(2,1)S(1)}, u32[]{:S(2)}, u32[]{:S(2)}) %collective-permute-start.10) | collective-permute-done | bytes 262176 | tf_op jit(solution)/shard_map/ppermute | solution.py:257
  105.5 0.3 collective-permute-done.11.c_ref
  105.8 2.6 %collective-permute-done.15.across_ref = bf16[128,1024]{1,0:T(8,128)(2,1)S(1)} collective-permute-done((bf16[128,1024]{1,0:T(8,128)(2,1)S(1)}, bf16[128,1024]{1,0:T(8,128)(2,1)S(1)}, u32[]{:S(2)}, u32[]{:S(2)}) %collective-permute-start.15) | collective-permute-done | bytes 262176 | tf_op jit(solution)/shard_map/ppermute | solution.py:261
  108.4 0.9 sum_blocks.1
  109.3 1.3 all-to-all-done.2.got_ref
  110.6 6.4 %all-to-all-start.3 = ((bf16[16,8,1024]{2,1,0:T(8,128)(2,1)}), bf16[16,8,1024]{2,1,0:T(8,128)(2,1)S(1)}, u32[]{:S(2)}, u32[]{:S(2)}) async-start(bf16[16,8,1024]{2,1,0:T(8,128)(2,1)} %sum_blocks.1), calls=%async_computation.3 | async-start | bytes 524288 | tf_op jit(solution)/shard_map/all_to_all | solution.py:253
  117.0 0.8 copy-done.11
  117.8 3.4 %home.1 = (bf16[2,128,1024]{2,1,0:T(8,128)(2,1)}, bf16[2,128,1024]{2,1,0:T(8,128)(2,1)}) custom-call(bf16[16,48,512]{2,1,0:T(8,128)(2,1)} %copy-done.7, bf16[2,128,1024]{2,1,0:T(8,128)(2,1)} %bitcast.44, bf16[1024,256]{1,0:T(8,128)(2,1)} %get-tuple-element.43.w_mine_ref, bf16[1024,256]{1,0:T(8,128)(2,1)} %copy-done.11), custom_call_target="tpu_custom_call" | custom-call | flops 300000000 | bytes 4194304 | tf_op jit(solution)/shard_map/home/pallas_call | solution.py:381
  121.1 0.0 copy-start.14
  121.2 3.7 %all-to-all-done.3 = bf16[16,8,1024]{2,1,0:T(8,128)(2,1)S(1)} async-done(((bf16[16,8,1024]{2,1,0:T(8,128)(2,1)}), bf16[16,8,1024]{2,1,0:T(8,128)(2,1)S(1)}, u32[]{:S(2)}, u32[]{:S(2)}) %all-to-all-start.3) | async-done | bytes 262176 | tf_op jit(solution)/shard_map/all_to_all | solution.py:253
  124.8 0.2 reshape.80
  125.0 0.1 reduce_sum.18
  125.1 3.8 %collective-permute-start.19 = (f32[4,1024]{1,0:T(4,128)S(1)}, f32[4,1024]{1,0:T(4,128)S(1)}, u32[]{:S(2)}, u32[]{:S(2)}) collective-permute-start(f32[4,1024]{1,0:T(4,128)S(1)} %dynamic-slice_bitcast_fusion.2), channel_id=1, source_target_pairs={{0,16},{16,0},{1,17},{17,1},{2,18},{18,2},{3,19},{19,3},{4,20},{20... | collective-permute-start | bytes 49160 | tf_op jit(solution)/shard_map/ppermute | solution.py:249
  128.9 0.8 collective-permute-done.19
  129.8 0.6 copy.27
  130.5 0.0 copy-start.13
  130.5 0.1 multiply_reduce_fusion
  130.6 0.6 dynamic-slice_divide_fusion
  (54 shorter events, 0.3 us)
Async XLA Ops:
  0.6 11.6 %copy-start = (bf16[1,2,128,1024]{3,2,1,0:T(8,128)(2,1)S(1)}, bf16[1,2,128,1024]{3,2,1,0:T(8,128)(2,1)}, u32[]{:S(2)}) copy-start(bf16[1,2,128,1024]{3,2,1,0:T(8,128)(2,1)} %param.9) | copy-start | bytes 1572868
  0.6 11.6 %copy-start.8 = (bf16[1,2,128,1024]{3,2,1,0:T(8,128)(2,1)S(1)}, bf16[1,2,128,1024]{3,2,1,0:T(8,128)(2,1)}, u32[]{:S(2)}) copy-start(bf16[1,2,128,1024]{3,2,1,0:T(8,128)(2,1)} %param.5) | copy-start | bytes 1572868
  2.2 18.8 %all-to-all-start = ((bf16[16,8,1024]{2,1,0:T(8,128)(2,1)}), bf16[16,8,1024]{2,1,0:T(8,128)(2,1)S(1)}, u32[]{:S(2)}, u32[]{:S(2)}) async-start(bf16[16,8,1024]{2,1,0:T(8,128)(2,1)} %pack_weights.1), calls=%async_computation | async-start | bytes 524288 | tf_op jit(solution)/shard_map/all_to_all | solution.py:253
  21.2 3.6 %collective-permute-start = (bf16[64,1024]{1,0:T(8,128)(2,1)S(1)}, bf16[64,1024]{1,0:T(8,128)(2,1)S(1)}, u32[]{:S(2)}, u32[]{:S(2)}) collective-permute-start(bf16[64,1024]{1,0:T(8,128)(2,1)S(1)} %reshape.75), channel_id=1, source_target_pairs={{0,16},{16,0},{1,17},{17,1},{2,18},{18,2},{3,19},{19,3},{4,20},{20... | collective-permute-start | bytes 393224 | tf_op jit(solution)/shard_map/ppermute | solution.py:249
  24.9 36.3 %copy-start.12 = (bf16[128,1024]{1,0:T(8,128)(2,1)}, bf16[128,1024]{1,0:T(8,128)(2,1)S(1)}, u32[]{:S(2)}) copy-start(bf16[128,1024]{1,0:T(8,128)(2,1)S(1)} %pad_maximum_fusion.1.refs_0_) | copy-start | bytes 786436
  24.9 29.6 %all-to-all-start.1 = ((bf16[16,32,1024]{2,1,0:T(8,128)(2,1)}), bf16[16,32,1024]{2,1,0:T(8,128)(2,1)S(1)}, u32[]{:S(2)}, u32[]{:S(2)}) async-start(bf16[16,32,1024]{2,1,0:T(8,128)(2,1)} %pad_maximum_fusion), calls=%async_computation.1 | async-start | bytes 2097152 | tf_op jit(solution)/shard_map/all_to_all | solution.py:253
  29.1 13.9 %collective-permute-start.5 = (bf16[128,1024]{1,0:T(8,128)(2,1)S(1)}, bf16[128,1024]{1,0:T(8,128)(2,1)S(1)}, u32[]{:S(2)}, u32[]{:S(2)}) collective-permute-start(bf16[128,1024]{1,0:T(8,128)(2,1)S(1)} %pad_maximum_fusion.1.refs_0_), channel_id=1, source_target_pairs={{0,32},{32,0},{1,33},{33,1},{2,34},{34,2},{3,35},{35,3},{4,36},{36... | collective-permute-start | bytes 786440 | tf_op jit(solution)/shard_map/ppermute | solution.py:261
  31.7 14.4 %collective-permute-start.4 = (bf16[128,1024]{1,0:T(8,128)(2,1)S(1)}, bf16[128,1024]{1,0:T(8,128)(2,1)S(1)}, u32[]{:S(2)}, u32[]{:S(2)}) collective-permute-start(bf16[128,1024]{1,0:T(8,128)(2,1)S(1)} %pad_maximum_fusion.1.refs_0_), channel_id=1, source_target_pairs={{0,192},{64,0},{128,64},{192,128},{1,193},{65,1},{129,65},{193,129... | collective-permute-start | bytes 786440 | tf_op jit(solution)/shard_map/ppermute | solution.py:257
  34.4 12.4 %collective-permute-start.3 = (bf16[128,1024]{1,0:T(8,128)(2,1)S(1)}, bf16[128,1024]{1,0:T(8,128)(2,1)S(1)}, u32[]{:S(2)}, u32[]{:S(2)}) collective-permute-start(bf16[128,1024]{1,0:T(8,128)(2,1)S(1)} %pad_maximum_fusion.1.refs_0_), channel_id=1, source_target_pairs={{0,128},{64,192},{128,0},{192,64},{1,129},{65,193},{129,1},{193,65... | collective-permute-start | bytes 786440 | tf_op jit(solution)/shard_map/ppermute | solution.py:257
  34.7 22.5 %collective-permute-start.2 = (bf16[128,1024]{1,0:T(8,128)(2,1)S(1)}, bf16[128,1024]{1,0:T(8,128)(2,1)}, u32[]{:S(2)}, u32[]{:S(2)}) collective-permute-start(bf16[128,1024]{1,0:T(8,128)(2,1)S(1)} %pad_maximum_fusion.1.refs_0_), channel_id=1, source_target_pairs={{0,64},{64,128},{128,192},{192,0},{1,65},{65,129},{129,193},{193,1... | collective-permute-start | bytes 786440 | tf_op jit(solution)/shard_map/ppermute | solution.py:257
  43.0 18.2 %copy-start.17 = (bf16[128,1024]{1,0:T(8,128)(2,1)}, bf16[128,1024]{1,0:T(8,128)(2,1)S(1)}, u32[]{:S(2)}) copy-start(bf16[128,1024]{1,0:T(8,128)(2,1)S(1)} %collective-permute-done.5.refs_4_) | copy-start | bytes 786436
  43.0 14.2 %collective-permute-start.8 = (bf16[128,1024]{1,0:T(8,128)(2,1)S(1)}, bf16[128,1024]{1,0:T(8,128)(2,1)}, u32[]{:S(2)}, u32[]{:S(2)}) collective-permute-start(bf16[128,1024]{1,0:T(8,128)(2,1)S(1)} %collective-permute-done.5.refs_4_), channel_id=1, source_target_pairs={{0,192},{64,0},{128,64},{192,128},{1,193},{65,1},{129,65},{193,129... | collective-permute-start | bytes 786440 | tf_op jit(solution)/shard_map/ppermute | solution.py:257
  45.7 11.5 %collective-permute-start.7 = (bf16[128,1024]{1,0:T(8,128)(2,1)S(1)}, bf16[128,1024]{1,0:T(8,128)(2,1)}, u32[]{:S(2)}, u32[]{:S(2)}) collective-permute-start(bf16[128,1024]{1,0:T(8,128)(2,1)S(1)} %collective-permute-done.5.refs_4_), channel_id=1, source_target_pairs={{0,128},{64,192},{128,0},{192,64},{1,129},{65,193},{129,1},{193,65... | collective-permute-start | bytes 786440 | tf_op jit(solution)/shard_map/ppermute | solution.py:257
  46.1 15.1 %copy-start.18 = (bf16[128,1024]{1,0:T(8,128)(2,1)}, bf16[128,1024]{1,0:T(8,128)(2,1)S(1)}, u32[]{:S(2)}) copy-start(bf16[128,1024]{1,0:T(8,128)(2,1)S(1)} %collective-permute-done.4.refs_3_) | copy-start | bytes 786436
  46.1 15.1 %collective-permute-start.6 = (bf16[128,1024]{1,0:T(8,128)(2,1)S(1)}, bf16[128,1024]{1,0:T(8,128)(2,1)}, u32[]{:S(2)}, u32[]{:S(2)}) collective-permute-start(bf16[128,1024]{1,0:T(8,128)(2,1)S(1)} %collective-permute-done.5.refs_4_), channel_id=1, source_target_pairs={{0,64},{64,128},{128,192},{192,0},{1,65},{65,129},{129,193},{193,1... | collective-permute-start | bytes 786440 | tf_op jit(solution)/shard_map/ppermute | solution.py:257
  46.8 0.7 copy-start.19
  54.5 7.3 %copy-start.1 = (bf16[16,32,1024]{2,1,0:T(8,128)(2,1)}, bf16[16,32,1024]{2,1,0:T(8,128)(2,1)S(1)}, u32[]{:S(2)}) copy-start(bf16[16,32,1024]{2,1,0:T(8,128)(2,1)S(1)} %all-to-all-done.1.got_own_ref.got_ref) | copy-start | bytes 3145732
  54.5 7.3 %collective-permute-start.1 = (bf16[16,32,1024]{2,1,0:T(8,128)(2,1)S(1)}, bf16[16,32,1024]{2,1,0:T(8,128)(2,1)S(1)}, u32[]{:S(2)}, u32[]{:S(2)}) collective-permute-start(bf16[16,32,1024]{2,1,0:T(8,128)(2,1)S(1)} %all-to-all-done.1.got_own_ref.got_ref), channel_id=1, source_target_pairs={{0,16},{16,0},{1,17},{17,1},{2,18},{18,2},{3,19},{19,3},{4,20},{20... | collective-permute-start | bytes 3145736 | tf_op jit(solution)/shard_map/ppermute | solution.py:249
  61.8 1.0 copy-start.15
  62.8 16.1 %copy-start.2 = (bf16[16,32,1024]{2,1,0:T(8,128)(2,1)S(1)}, bf16[16,32,1024]{2,1,0:T(8,128)(2,1)}, u32[]{:S(2)}) copy-start(bf16[16,32,1024]{2,1,0:T(8,128)(2,1)} %copy-done.1) | copy-start | bytes 3145732
  62.8 16.1 %copy-start.5 = (f32[1024]{0:T(1024)S(1)}, f32[1024]{0:T(1024)}, u32[]{:S(2)}) copy-start(f32[1024]{0:T(1024)} %param.6) | copy-start | bytes 12292
  73.5 5.3 %collective-permute-start.16 = (f32[256,1024]{1,0:T(8,128)}, f32[256,1024]{1,0:T(8,128)S(1)}, u32[]{:S(2)}, u32[]{:S(2)}) collective-permute-start(f32[256,1024]{1,0:T(8,128)} %get-tuple-element.39), channel_id=1, source_target_pairs={{0,16},{16,0},{1,17},{17,1},{2,18},{18,2},{3,19},{19,3},{4,20},{20... | collective-permute-start | bytes 3145736 | tf_op jit(solution)/shard_map/ppermute | solution.py:249
  74.1 19.8 %collective-permute-start.12 = (bf16[128,1024]{1,0:T(8,128)(2,1)}, bf16[128,1024]{1,0:T(8,128)(2,1)S(1)}, u32[]{:S(2)}, u32[]{:S(2)}) collective-permute-start(bf16[128,1024]{1,0:T(8,128)(2,1)} %get-tuple-element.34), channel_id=1, source_target_pairs={{0,64},{64,128},{128,192},{192,0},{1,65},{65,129},{129,193},{193,1... | collective-permute-start | bytes 786440 | tf_op jit(solution)/shard_map/ppermute | solution.py:257
  74.1 21.6 %collective-permute-start.13 = (bf16[128,1024]{1,0:T(8,128)(2,1)}, bf16[128,1024]{1,0:T(8,128)(2,1)S(1)}, u32[]{:S(2)}, u32[]{:S(2)}) collective-permute-start(bf16[128,1024]{1,0:T(8,128)(2,1)} %get-tuple-element.35), channel_id=1, source_target_pairs={{0,128},{64,192},{128,0},{192,64},{1,129},{65,193},{129,1},{193,65... | collective-permute-start | bytes 786440 | tf_op jit(solution)/shard_map/ppermute | solution.py:257
  75.6 20.1 %collective-permute-start.14 = (bf16[128,1024]{1,0:T(8,128)(2,1)}, bf16[128,1024]{1,0:T(8,128)(2,1)S(1)}, u32[]{:S(2)}, u32[]{:S(2)}) collective-permute-start(bf16[128,1024]{1,0:T(8,128)(2,1)} %get-tuple-element.36), channel_id=1, source_target_pairs={{0,192},{64,0},{128,64},{192,128},{1,193},{65,1},{129,65},{193,129... | collective-permute-start | bytes 786440 | tf_op jit(solution)/shard_map/ppermute | solution.py:257
  76.8 2.1 %collective-permute-start.17 = (bf16[256,256]{1,0:T(8,128)(2,1)}, bf16[256,256]{1,0:T(8,128)(2,1)S(1)}, u32[]{:S(2)}, u32[]{:S(2)}) collective-permute-start(bf16[256,256]{1,0:T(8,128)(2,1)} %get-tuple-element.40), channel_id=1, source_target_pairs={{0,16},{16,0},{1,17},{17,1},{2,18},{18,2},{3,19},{19,3},{4,20},{20... | collective-permute-start | bytes 393224 | tf_op jit(solution)/shard_map/ppermute | solution.py:249
  78.9 1.2 copy-start.3
  80.1 0.9 copy-start.4
  83.0 11.0 %copy-start.16 = (bf16[128,1024]{1,0:T(8,128)(2,1)S(1)}, bf16[128,1024]{1,0:T(8,128)(2,1)}, u32[]{:S(2)}) copy-start(bf16[128,1024]{1,0:T(8,128)(2,1)} %get-tuple-element.32) | copy-start | bytes 786436
  83.0 12.8 %copy-start.9 = (f32[128,1024]{1,0:T(8,128)S(1)}, f32[128,1024]{1,0:T(8,128)}, u32[]{:S(2)}) copy-start(f32[128,1024]{1,0:T(8,128)} %get-tuple-element.33) | copy-start | bytes 1572868
  83.0 27.6 %all-to-all-start.2 = ((bf16[16,48,512]{2,1,0:T(8,128)(2,1)}), bf16[16,48,512]{2,1,0:T(8,128)(2,1)S(1)}, u32[]{:S(2)}, u32[]{:S(2)}) async-start(bf16[16,48,512]{2,1,0:T(8,128)(2,1)} %input_gradient.1), calls=%async_computation.2 | async-start | bytes 1572864 | tf_op jit(solution)/shard_map/all_to_all | solution.py:253
  90.9 6.8 %copy-start.10 = (bf16[1024,256]{1,0:T(8,128)(2,1)S(1)}, bf16[1024,256]{1,0:T(8,128)(2,1)}, u32[]{:S(2)}) copy-start(bf16[1024,256]{1,0:T(8,128)(2,1)} %get-tuple-element.43.w_mine_ref) | copy-start | bytes 1572868
  90.9 17.5 %copy-start.6 = (f32[128,1024]{1,0:T(8,128)S(1)}, f32[128,1024]{1,0:T(8,128)}, u32[]{:S(2)}) copy-start(f32[128,1024]{1,0:T(8,128)} %get-tuple-element.29.own_ref) | copy-start | bytes 1572868
  90.9 8.7 %collective-permute-start.9 = (bf16[128,1024]{1,0:T(8,128)(2,1)}, bf16[128,1024]{1,0:T(8,128)(2,1)S(1)}, u32[]{:S(2)}, u32[]{:S(2)}) collective-permute-start(bf16[128,1024]{1,0:T(8,128)(2,1)} %get-tuple-element.30), channel_id=1, source_target_pairs={{0,64},{64,128},{128,192},{192,0},{1,65},{65,129},{129,193},{193,1... | collective-permute-start | bytes 786440 | tf_op jit(solution)/shard_map/ppermute | solution.py:257
  91.6 14.0 %collective-permute-start.10 = (bf16[128,1024]{1,0:T(8,128)(2,1)}, bf16[128,1024]{1,0:T(8,128)(2,1)S(1)}, u32[]{:S(2)}, u32[]{:S(2)}) collective-permute-start(bf16[128,1024]{1,0:T(8,128)(2,1)} %get-tuple-element.31), channel_id=1, source_target_pairs={{0,128},{64,192},{128,0},{192,64},{1,129},{65,193},{129,1},{193,65... | collective-permute-start | bytes 786440 | tf_op jit(solution)/shard_map/ppermute | solution.py:257
  94.0 11.9 %collective-permute-start.11 = (bf16[128,1024]{1,0:T(8,128)(2,1)S(1)}, bf16[128,1024]{1,0:T(8,128)(2,1)S(1)}, u32[]{:S(2)}, u32[]{:S(2)}) collective-permute-start(bf16[128,1024]{1,0:T(8,128)(2,1)S(1)} %copy-done.16), channel_id=1, source_target_pairs={{0,192},{64,0},{128,64},{192,128},{1,193},{65,1},{129,65},{193,129... | collective-permute-start | bytes 786440 | tf_op jit(solution)/shard_map/ppermute | solution.py:257
  95.9 12.5 %collective-permute-start.15 = (bf16[128,1024]{1,0:T(8,128)(2,1)S(1)}, bf16[128,1024]{1,0:T(8,128)(2,1)S(1)}, u32[]{:S(2)}, u32[]{:S(2)}) collective-permute-start(bf16[128,1024]{1,0:T(8,128)(2,1)S(1)} %add_convert_fusion), channel_id=1, source_target_pairs={{0,32},{32,0},{1,33},{33,1},{2,34},{34,2},{3,35},{35,3},{4,36},{36... | collective-permute-start | bytes 786440 | tf_op jit(solution)/shard_map/ppermute | solution.py:261
  97.7 19.2 %collective-permute-start.18 = (bf16[1024,256]{1,0:T(8,128)(2,1)S(1)}, bf16[1024,256]{1,0:T(8,128)(2,1)S(1)}, u32[]{:S(2)}, u32[]{:S(2)}) collective-permute-start(bf16[1024,256]{1,0:T(8,128)(2,1)S(1)} %copy-done.10), channel_id=1, source_target_pairs={{0,16},{16,0},{1,17},{17,1},{2,18},{18,2},{3,19},{19,3},{4,20},{20... | collective-permute-start | bytes 1572872 | tf_op jit(solution)/shard_map/ppermute | solution.py:249
  110.6 6.4 %copy-start.7 = (bf16[16,48,512]{2,1,0:T(8,128)(2,1)}, bf16[16,48,512]{2,1,0:T(8,128)(2,1)S(1)}, u32[]{:S(2)}) copy-start(bf16[16,48,512]{2,1,0:T(8,128)(2,1)S(1)} %all-to-all-done.2.got_ref) | copy-start | bytes 2359300
  110.6 14.2 %all-to-all-start.3 = ((bf16[16,8,1024]{2,1,0:T(8,128)(2,1)}), bf16[16,8,1024]{2,1,0:T(8,128)(2,1)S(1)}, u32[]{:S(2)}, u32[]{:S(2)}) async-start(bf16[16,8,1024]{2,1,0:T(8,128)(2,1)} %sum_blocks.1), calls=%async_computation.3 | async-start | bytes 524288 | tf_op jit(solution)/shard_map/all_to_all | solution.py:253
  117.0 0.8 copy-start.11
  121.1 9.3 %copy-start.14 = (bf16[4,1536]{1,0:T(4,128)(2,1)S(1)}, bf16[4,1536]{1,0:T(4,128)(2,1)}, u32[]{:S(2)}) copy-start(bf16[4,1536]{1,0:T(4,128)(2,1)} %w_qkv_ref.1) | copy-start | bytes 36868
  125.1 4.6 %collective-permute-start.19 = (f32[4,1024]{1,0:T(4,128)S(1)}, f32[4,1024]{1,0:T(4,128)S(1)}, u32[]{:S(2)}, u32[]{:S(2)}) collective-permute-start(f32[4,1024]{1,0:T(4,128)S(1)} %dynamic-slice_bitcast_fusion.2), channel_id=1, source_target_pairs={{0,16},{16,0},{1,17},{17,1},{2,18},{18,2},{3,19},{19,3},{4,20},{20... | collective-permute-start | bytes 49160 | tf_op jit(solution)/shard_map/ppermute | solution.py:249
  130.5 0.7 copy-start.13

commit v5 on v4

--- a/solution.py
+++ b/solution.py
@@ -131,10 +131,10 @@
 
 
 def layer_kernel(patches, got_own_ref, got_other_ref, gain_ref, token_ref, *refs):
-    pieces, outs, grad_refs, scratch = refs[:8], refs[8:13], refs[13:21], refs[21:]
-    w_ref, mixed_own_ref, dnormed_own_ref, mixed_other_ref, dnormed_other_ref = outs
-    got, weights, normed, mixed, dpacked, dnormed, grads, own, peers = scratch[:9]
-    slots, (sems, out_sems) = scratch[9:13], scratch[13:]
+    pieces, outs, grad_refs, scratch = refs[:8], refs[8:11], refs[11:19], refs[19:]
+    w_ref, for_own_ref, for_other_ref = outs
+    got, weights, normed, mixed, dpacked, for_own, for_other, grads, own, peers = scratch[:10]
+    slots, (sems, out_sems) = scratch[10:14], scratch[14:]
     copies = fetch([(got_own_ref, got.at[0])], sems)
     block = own.shape[1]
     places = [block_of(-(i % Y_SIZE), i // Y_SIZE) for i in range(8)]
@@ -151,13 +151,15 @@
     copies[0].wait()
     arguments = (got.at[0], gain_ref, weights, normed.at[0], mixed.at[0], dpacked.at[0])
     sample(patches, *arguments, slots, before_weights)
-    dnormed[0] = mm(dpacked[0], weights[:, : 3 * HALF], NT)
-    results += fetch([(mixed.at[0], mixed_own_ref), (dnormed.at[0], dnormed_own_ref)], out_sems, 1)
+    for_own[:, :D] = mm(dpacked[0], weights[:, : 3 * HALF], NT)
+    for_own[:, D:] = mixed[0].astype(f32)
+    results += fetch([(for_own, for_own_ref)], out_sems, 1)
     copies[9].wait()
     arguments = (got.at[1], gain_ref, weights, normed.at[1], mixed.at[1], dpacked.at[1])
     sample(patches, *arguments, slots, lambda: None)
-    dnormed[1] = mm(dpacked[1], weights[:, : 3 * HALF], NT)
-    results += fetch([(mixed.at[1], mixed_other_ref), (dnormed.at[1], dnormed_other_ref)], out_sems, 3)
+    for_other[:, :D] = mm(dpacked[1], weights[:, : 3 * HALF], NT).astype(bf16)
+    for_other[:, D:] = mixed[1]
+    results += fetch([(for_other, for_other_ref)], out_sems, 2)
     rows = normed.shape[1]
     pair_rows = 2 * block
     all_dpacked = dpacked[...].reshape(2 * rows, 3 * HALF)
@@ -176,8 +178,8 @@
     wait_all(results)
 
 
-def input_kernel(got_ref, mine_ref, mixed_ref, other, mixed_other, gain_ref, out_ref, got, mine, mixed, out, sems):
-    copies = fetch([(got_ref, got), (mine_ref, mine), (mixed_ref, mixed)], sems)
+def input_kernel(got_ref, mine_ref, other, gain_ref, out_ref, got, mine, out, sems):
+    copies = fetch([(got_ref, got), (mine_ref, mine)], sems)
     peers, per_peer = got.shape[0], got.shape[1] // 2
     wait_all(copies)
     results = []
@@ -187,7 +189,7 @@
         at = slice(peer, peer + group)
         rows = slice(peer * per_peer, (peer + group) * per_peer)
         normal_x, inv_std = layer_stats(got[at, :per_peer, :].reshape(group * per_peer, D))
-        scaled = (mine[rows, :] + other[rows, :]).astype(bf16).astype(f32) * gain_ref[...]
+        scaled = (mine[rows, :D] + other[rows, :D].astype(f32)).astype(bf16).astype(f32) * gain_ref[...]
         d_input = inv_std * (
             scaled
             - jnp.mean(scaled, axis=-1, keepdims=True)
@@ -196,9 +198,9 @@
         grad_in = (got[at, per_peer:, :].reshape(group * per_peer, D).astype(f32) + d_input).astype(bf16)
         out[at, :per_peer, :] = grad_in[:, : D // 2].reshape(half)
         out[at, per_peer : 2 * per_peer, :] = grad_in[:, D // 2 :].reshape(half)
-        out[at, 2 * per_peer :, :HALF] = mixed[rows, :].reshape(group, per_peer, HALF)
-        out[at, 2 * per_peer :, HALF:] = mixed_other[rows, :].reshape(group, per_peer, HALF)
-        results += fetch([(out.at[at], out_ref.at[at])], sems, 3 + len(results))
+        out[at, 2 * per_peer :, :HALF] = mine[rows, D:].astype(bf16).reshape(group, per_peer, HALF)
+        out[at, 2 * per_peer :, HALF:] = other[rows, D:].reshape(group, per_peer, HALF)
+        results += fetch([(out.at[at], out_ref.at[at])], sems, 2 + len(results))
     wait_all(results)
 
 
@@ -314,21 +316,22 @@
         name="arrived",
     )(*pieces)
 
-    sample_shapes = (shape((rows, HALF), bf16), shape((rows, width), f32))
+    sample_shapes = (shape((rows, width + HALF), f32), shape((rows, width + HALF), bf16))
     half_shape, own_shape = shape((block, width), bf16), shape((block, width), f32)
-    w_mine, mixed, d_normed, mixed_2, d_normed_2, *grad_pieces = pl.pallas_call(
+    w_mine, for_own, for_other, *grad_pieces = pl.pallas_call(
         functools.partial(layer_kernel, patches),
         in_specs=[ANY, ANY, VMEM, VMEM] + [ANY] * 8,
-        out_specs=(ANY,) * 13,
+        out_specs=(ANY,) * 11,
         out_shape=(shape((width, HALF), bf16),)
-        + sample_shapes * 2 + ((own_shape,) + (half_shape,) * (Y_SIZE - 1)) * 2,
+        + sample_shapes + ((own_shape,) + (half_shape,) * (Y_SIZE - 1)) * 2,
         scratch_shapes=[
             pltpu.VMEM((2,) + got.shape, bf16),
             pltpu.VMEM((width, width), bf16),
             pltpu.VMEM((2, rows, width), bf16),
             pltpu.VMEM((2, rows, HALF), bf16),
             pltpu.VMEM((2, rows, 3 * HALF), bf16),
-            pltpu.VMEM((2, rows, width), f32),
+            pltpu.VMEM((rows, width + HALF), f32),
+            pltpu.VMEM((rows, width + HALF), bf16),
             pltpu.VMEM((2 * block, width), f32),
             pltpu.VMEM((2, block, width), f32),
             pltpu.VMEM((6, block, width), bf16),
@@ -337,15 +340,14 @@
             pltpu.VMEM((HALF // DH, rows, rows), bf16),
             pltpu.VMEM((HALF // DH, rows, rows), bf16),
             pltpu.SemaphoreType.DMA((10,)),
-            pltpu.SemaphoreType.DMA((13,)),
+            pltpu.SemaphoreType.DMA((11,)),
         ],
         compiler_params=vmem_params(60),
         cost_estimate=pl.CostEstimate(flops=3 * 10**10, bytes_accessed=10 * 2**20, transcendentals=2**19),
         name="layer",
     )(got, got_other, gain_row, token, *pieces)
     w_other = exchange(w_mine)
-    d_normed_other = exchange(d_normed_2)
-    mixed_other = exchange(mixed_2)
+    from_other = exchange(for_other)
 
     received = [along_y(grad_pieces[Y_SIZE + step], step) for step in range(1, Y_SIZE)]
     partial = grad_pieces[Y_SIZE] + sum(piece.astype(f32) for piece in received)
@@ -362,19 +364,18 @@
     sent = pl.pallas_call(
         input_kernel,
         out_shape=shape((tm, 3 * per_peer, width // 2), bf16),
-        in_specs=[ANY] * 3 + [VMEM] * 3,
+        in_specs=[ANY] * 2 + [VMEM] * 2,
         out_specs=ANY,
         scratch_shapes=[
             pltpu.VMEM(got.shape, bf16),
-            pltpu.VMEM((rows, width), f32),
-            pltpu.VMEM((rows, HALF), bf16),
+            pltpu.VMEM((rows, width + HALF), f32),
             pltpu.VMEM((tm, 3 * per_peer, width // 2), bf16),
-            pltpu.SemaphoreType.DMA((11,)),
+            pltpu.SemaphoreType.DMA((6,)),
         ],
         compiler_params=vmem_params(24),
         cost_estimate=pl.CostEstimate(flops=10**9, bytes_accessed=6 * 2**20, transcendentals=0),
         name="input_gradient",
-    )(got, d_normed, mixed, d_normed_other, mixed_other, gain_row)
+    )(got, for_own, from_other, gain_row)
     got = swap(sent.reshape(-1, width // 2), TM).reshape(sent.shape)
     grads, got = lax.optimization_barrier((grads, got))
     local = shape(frames_in.shape[1:], bf16)

time: 132 us -> 130 us (0.985)
  waiting for transfers between devices: 43 us -> 39.6 us
    all_to_all x4, waiting for transfers between devices: 20.5 us -> 18.2 us  [swap(): return lax.all_to_all(value, axes, split_axis=0, concat_axis=0, tiled=True)]
    unnamed x43 -> x37, local copies, waits for them, and re-layouts: 5.4 us -> 4.55 us
    ppermute x6 -> x5, starting transfers between devices: 12.1 us -> 11.8 us  [exchange(): return lax.ppermute(value, 'core', [(0, 1), (1, 0)])]
  transfers between devices with their start and end apart: 24 -> 23, of which waited for: 12 -> 9; matrix products, arithmetic and copies ran while one was open for 1% -> 3% of each run, Pallas kernels for 5% -> 5%
where the time goes in v5:
time: 130 us; the launch traced here: 129 us
  starting transfers between devices  60.2 us (46%)
  waiting for transfers between devices  39.6 us (30%)
  Pallas kernels  18.9 us (15%)
  local copies, waits for them, and re-layouts  6.21 us (5%)
  other arithmetic  3.06 us (2%)
    all_to_all x4, starting transfers between devices, swap(): return lax.all_to_all(value, axes, split_axis=0, concat_axis=0, tiled=True)  29.3 us
    all_to_all x4, waiting for transfers between devices, swap(): return lax.all_to_all(value, axes, split_axis=0, concat_axis=0, tiled=True)  18.2 us
    ppermute x12, starting transfers between devices, along_y(): lax.ppermute(value, 'y', [(i, (i + step) % Y_SIZE) for i in range(Y_SIZE)])  14.8 us
    ppermute x5, starting transfers between devices, exchange(): return lax.ppermute(value, 'core', [(0, 1), (1, 0)])  11.8 us
    ppermute x2, waiting for transfers between devices, across_x(): return lax.ppermute(value, 'xh', [(0, 1), (1, 0)])  11.4 us
    pallas_call x1, Pallas kernels, body(): pl.pallas_call(functools.partial(layer_kernel, patches), in_specs=[ANY, A...  10.8 us
    ppermute x12, waiting for transfers between devices, along_y(): lax.ppermute(value, 'y', [(i, (i + step) % Y_SIZE) for i in range(Y_SIZE)])  9.16 us
    unnamed x37, local copies, waits for them, and re-layouts  4.55 us
  transfers between devices with their start and end apart: 23, of which 9 were waited for; matrix products, arithmetic and copies ran while one was open for 3% of the time, Pallas kernels for 5%

profile of v5, /device:TPU:1, one launch (start us, length us, event | category | flops | bytes accessed | tf_op | source)
XLA Modules:
  0.0 129.0 jit_solution(9497255151612798909)
XLA Ops:
  0.6 0.0 copy-start
  0.6 1.5 %pack_weights.1 = bf16[16,8,1024]{2,1,0:T(8,128)(2,1)} custom-call(bf16[4,1536]{1,0:T(4,128)(2,1)} %w_qkv_ref.1, bf16[4,512]{1,0:T(4,128)(2,1)} %bitcast.49), custom_call_target="tpu_custom_call" | custom-call | bytes 262144 | tf_op jit(solution)/shard_map/pack_weights/pallas_call | solution.py:281
  2.1 10.0 %all-to-all-start = ((bf16[16,8,1024]{2,1,0:T(8,128)(2,1)}), bf16[16,8,1024]{2,1,0:T(8,128)(2,1)S(1)}, u32[]{:S(2)}, u32[]{:S(2)}) async-start(bf16[16,8,1024]{2,1,0:T(8,128)(2,1)} %pack_weights.1), calls=%async_computation | async-start | bytes 524288 | tf_op jit(solution)/shard_map/all_to_all | solution.py:255
  12.2 1.2 copy_bitcast_fusion
  13.4 7.5 %all-to-all-done = bf16[16,8,1024]{2,1,0:T(8,128)(2,1)S(1)} async-done(((bf16[16,8,1024]{2,1,0:T(8,128)(2,1)}), bf16[16,8,1024]{2,1,0:T(8,128)(2,1)S(1)}, u32[]{:S(2)}, u32[]{:S(2)}) %all-to-all-start) | async-done | bytes 262176 | tf_op jit(solution)/shard_map/all_to_all | solution.py:255
  20.9 0.1 reshape.73
  21.0 0.1 dynamic-slice_bitcast_fusion.1
  21.2 2.4 %collective-permute-start = (bf16[64,1024]{1,0:T(8,128)(2,1)S(1)}, bf16[64,1024]{1,0:T(8,128)(2,1)S(1)}, u32[]{:S(2)}, u32[]{:S(2)}) collective-permute-start(bf16[64,1024]{1,0:T(8,128)(2,1)S(1)} %reshape.75), channel_id=1, source_target_pairs={{0,16},{16,0},{1,17},{17,1},{2,18},{18,2},{3,19},{19,3},{4,20},{20... | collective-permute-start | bytes 393224 | tf_op jit(solution)/shard_map/ppermute | solution.py:251
  23.6 1.1 pad_maximum_fusion
  24.7 0.0 collective-permute-done
  24.8 4.2 %all-to-all-start.1 = ((bf16[16,32,1024]{2,1,0:T(8,128)(2,1)}), bf16[16,32,1024]{2,1,0:T(8,128)(2,1)S(1)}, u32[]{:S(2)}, u32[]{:S(2)}) async-start(bf16[16,32,1024]{2,1,0:T(8,128)(2,1)} %pad_maximum_fusion), calls=%async_computation.1 | async-start | bytes 2097152 | tf_op jit(solution)/shard_map/all_to_all | solution.py:255
  29.1 2.5 %collective-permute-start.5 = (bf16[128,1024]{1,0:T(8,128)(2,1)S(1)}, bf16[128,1024]{1,0:T(8,128)(2,1)S(1)}, u32[]{:S(2)}, u32[]{:S(2)}) collective-permute-start(bf16[128,1024]{1,0:T(8,128)(2,1)S(1)} %pad_maximum_fusion.1.refs_0_), channel_id=1, source_target_pairs={{0,32},{32,0},{1,33},{33,1},{2,34},{34,2},{3,35},{35,3},{4,36},{36... | collective-permute-start | bytes 786440 | tf_op jit(solution)/shard_map/ppermute | solution.py:263
  31.6 2.7 %collective-permute-start.4 = (bf16[128,1024]{1,0:T(8,128)(2,1)S(1)}, bf16[128,1024]{1,0:T(8,128)(2,1)S(1)}, u32[]{:S(2)}, u32[]{:S(2)}) collective-permute-start(bf16[128,1024]{1,0:T(8,128)(2,1)S(1)} %pad_maximum_fusion.1.refs_0_), channel_id=1, source_target_pairs={{0,192},{64,0},{128,64},{192,128},{1,193},{65,1},{129,65},{193,129... | collective-permute-start | bytes 786440 | tf_op jit(solution)/shard_map/ppermute | solution.py:259
  34.3 0.3 collective-permute-start.3
  34.7 0.7 collective-permute-start.2
  35.4 7.5 %collective-permute-done.5.refs_4_ = bf16[128,1024]{1,0:T(8,128)(2,1)S(1)} collective-permute-done((bf16[128,1024]{1,0:T(8,128)(2,1)S(1)}, bf16[128,1024]{1,0:T(8,128)(2,1)S(1)}, u32[]{:S(2)}, u32[]{:S(2)}) %collective-permute-start.5) | collective-permute-done | bytes 262176 | tf_op jit(solution)/shard_map/ppermute | solution.py:263
  42.9 2.7 %collective-permute-start.8 = (bf16[128,1024]{1,0:T(8,128)(2,1)S(1)}, bf16[128,1024]{1,0:T(8,128)(2,1)}, u32[]{:S(2)}, u32[]{:S(2)}) collective-permute-start(bf16[128,1024]{1,0:T(8,128)(2,1)S(1)} %collective-permute-done.5.refs_4_), channel_id=1, source_target_pairs={{0,192},{64,0},{128,64},{192,128},{1,193},{65,1},{129,65},{193,129... | collective-permute-start | bytes 786440 | tf_op jit(solution)/shard_map/ppermute | solution.py:259
  45.6 0.3 collective-permute-start.7
  46.0 0.0 collective-permute-done.4.refs_3_
  46.0 0.7 collective-permute-start.6
  46.7 0.7 copy-done.16
  47.4 7.0 %all-to-all-done.1.got_own_ref.got_ref = bf16[16,32,1024]{2,1,0:T(8,128)(2,1)S(1)} async-done(((bf16[16,32,1024]{2,1,0:T(8,128)(2,1)}), bf16[16,32,1024]{2,1,0:T(8,128)(2,1)S(1)}, u32[]{:S(2)}, u32[]{:S(2)}) %all-to-all-start.1) | async-done | bytes 1048608 | tf_op jit(solution)/shard_map/all_to_all | solution.py:255
  54.4 2.7 %collective-permute-start.1 = (bf16[16,32,1024]{2,1,0:T(8,128)(2,1)S(1)}, bf16[16,32,1024]{2,1,0:T(8,128)(2,1)S(1)}, u32[]{:S(2)}, u32[]{:S(2)}) collective-permute-start(bf16[16,32,1024]{2,1,0:T(8,128)(2,1)S(1)} %all-to-all-done.1.got_own_ref.got_ref), channel_id=1, source_target_pairs={{0,16},{16,0},{1,17},{17,1},{2,18},{18,2},{3,19},{19,3},{4,20},{20... | collective-permute-start | bytes 3145736 | tf_op jit(solution)/shard_map/ppermute | solution.py:251
  57.2 0.0 collective-permute-done.2.refs_1_
  57.2 0.0 collective-permute-done.8.refs_7_
  57.2 0.0 collective-permute-done.7.refs_6_
  57.2 3.9 %collective-permute-done.6.refs_5_ = bf16[128,1024]{1,0:T(8,128)(2,1)} collective-permute-done((bf16[128,1024]{1,0:T(8,128)(2,1)S(1)}, bf16[128,1024]{1,0:T(8,128)(2,1)}, u32[]{:S(2)}, u32[]{:S(2)}) %collective-permute-start.6) | collective-permute-done | bytes 262176 | tf_op jit(solution)/shard_map/ppermute | solution.py:259
  61.1 0.6 arrived.1.token_ref
  61.7 1.0 copy-done.13
  62.7 10.8 %layer.1 = (bf16[1024,256]{1,0:T(8,128)(2,1)}, f32[256,1280]{1,0:T(8,128)}, bf16[256,1280]{1,0:T(8,128)(2,1)}, f32[128,1024]{1,0:T(8,128)}, bf16[128,1024]{1,0:T...) custom-call(bf16[16,32,1024]{2,1,0:T(8,128)(2,1)} %copy-done.1, ...), custom_call_target="tpu_custom_call" | custom-call | flops 30000001024 | bytes 10485760 | tf_op jit(solution)/shard_map/layer/pallas_call | solution.py:321
  73.5 0.6 collective-permute-start.16
  74.1 0.0 collective-permute-start.12
  74.1 1.5 %collective-permute-start.13 = (bf16[128,1024]{1,0:T(8,128)(2,1)}, bf16[128,1024]{1,0:T(8,128)(2,1)S(1)}, u32[]{:S(2)}, u32[]{:S(2)}) collective-permute-start(bf16[128,1024]{1,0:T(8,128)(2,1)} %get-tuple-element.33), channel_id=1, source_target_pairs={{0,128},{64,192},{128,0},{192,64},{1,129},{65,193},{129,1},{193,65... | collective-permute-start | bytes 786440 | tf_op jit(solution)/shard_map/ppermute | solution.py:259
  75.6 1.2 collective-permute-start.14
  76.8 0.0 collective-permute-done.16.other
  76.8 1.3 %copy-done.3 = f32[256,1280]{1,0:T(8,128)S(1)} copy-done((f32[256,1280]{1,0:T(8,128)S(1)}, f32[256,1280]{1,0:T(8,128)}, u32[]{:S(2)}) %copy-start.3) | copy-done | bytes 1310744
  78.1 1.8 %input_gradient.1 = bf16[16,48,512]{2,1,0:T(8,128)(2,1)} custom-call(bf16[16,32,1024]{2,1,0:T(8,128)(2,1)S(1)} %copy-done.2, f32[256,1280]{1,0:T(8,128)S(1)} %copy-done.3, bf16[256,1280]{1,0:T(8,128)(2,1)S(1)} %collective-permute-done.16.other, f32[1,1024]{1,0:T(1,128)S(1)} %bitcast.43), custom_call_target="tpu_custom_call" | custom-call | flops 1000000000 | bytes 6291456 | tf_op jit(solution)/shard_map/input_gradient/pallas_call | solution.py:364
  79.9 0.0 copy-start.7
  79.9 0.0 copy-start.5
  79.9 8.1 %all-to-all-start.2 = ((bf16[16,48,512]{2,1,0:T(8,128)(2,1)}), bf16[16,48,512]{2,1,0:T(8,128)(2,1)S(1)}, u32[]{:S(2)}, u32[]{:S(2)}) async-start(bf16[16,48,512]{2,1,0:T(8,128)(2,1)} %input_gradient.1), calls=%async_computation.2 | async-start | bytes 1572864 | tf_op jit(solution)/shard_map/all_to_all | solution.py:255
  88.1 0.7 collective-permute-start.9
  88.7 1.9 %collective-permute-start.10 = (bf16[128,1024]{1,0:T(8,128)(2,1)}, bf16[128,1024]{1,0:T(8,128)(2,1)S(1)}, u32[]{:S(2)}, u32[]{:S(2)}) collective-permute-start(bf16[128,1024]{1,0:T(8,128)(2,1)} %get-tuple-element.29), channel_id=1, source_target_pairs={{0,128},{64,192},{128,0},{192,64},{1,129},{65,193},{129,1},{193,65... | collective-permute-start | bytes 786440 | tf_op jit(solution)/shard_map/ppermute | solution.py:259
  90.6 2.0 %collective-permute-start.11 = (bf16[128,1024]{1,0:T(8,128)(2,1)}, bf16[128,1024]{1,0:T(8,128)(2,1)S(1)}, u32[]{:S(2)}, u32[]{:S(2)}) collective-permute-start(bf16[128,1024]{1,0:T(8,128)(2,1)} %get-tuple-element.30), channel_id=1, source_target_pairs={{0,192},{64,0},{128,64},{192,128},{1,193},{65,1},{129,65},{193,129... | collective-permute-start | bytes 786440 | tf_op jit(solution)/shard_map/ppermute | solution.py:259
  92.6 0.0 collective-permute-done.13
  92.6 1.1 add_convert_fusion
  93.7 1.8 %collective-permute-start.15 = (bf16[128,1024]{1,0:T(8,128)(2,1)S(1)}, bf16[128,1024]{1,0:T(8,128)(2,1)S(1)}, u32[]{:S(2)}, u32[]{:S(2)}) collective-permute-start(bf16[128,1024]{1,0:T(8,128)(2,1)S(1)} %add_convert_fusion), channel_id=1, source_target_pairs={{0,32},{32,0},{1,33},{33,1},{2,34},{34,2},{3,35},{35,3},{4,36},{36... | collective-permute-start | bytes 786440 | tf_op jit(solution)/shard_map/ppermute | solution.py:263
  95.6 2.3 %collective-permute-start.17 = (bf16[1024,256]{1,0:T(8,128)(2,1)S(1)}, bf16[1024,256]{1,0:T(8,128)(2,1)S(1)}, u32[]{:S(2)}, u32[]{:S(2)}) collective-permute-start(bf16[1024,256]{1,0:T(8,128)(2,1)S(1)} %copy-done.8), channel_id=1, source_target_pairs={{0,16},{16,0},{1,17},{17,1},{2,18},{18,2},{3,19},{19,3},{4,20},{20... | collective-permute-start | bytes 1572872 | tf_op jit(solution)/shard_map/ppermute | solution.py:251
  97.9 3.9 %collective-permute-done.10.b_ref = bf16[128,1024]{1,0:T(8,128)(2,1)S(1)} collective-permute-done((bf16[128,1024]{1,0:T(8,128)(2,1)}, bf16[128,1024]{1,0:T(8,128)(2,1)S(1)}, u32[]{:S(2)}, u32[]{:S(2)}) %collective-permute-start.10) | collective-permute-done | bytes 262176 | tf_op jit(solution)/shard_map/ppermute | solution.py:259
  101.8 1.3 collective-permute-done.11.c_ref
  103.1 3.9 %collective-permute-done.15.across_ref = bf16[128,1024]{1,0:T(8,128)(2,1)S(1)} collective-permute-done((bf16[128,1024]{1,0:T(8,128)(2,1)S(1)}, bf16[128,1024]{1,0:T(8,128)(2,1)S(1)}, u32[]{:S(2)}, u32[]{:S(2)}) %collective-permute-start.15) | collective-permute-done | bytes 262176 | tf_op jit(solution)/shard_map/ppermute | solution.py:263
  106.9 0.9 sum_blocks.1
  107.9 6.9 %all-to-all-start.3 = ((bf16[16,8,1024]{2,1,0:T(8,128)(2,1)}), bf16[16,8,1024]{2,1,0:T(8,128)(2,1)S(1)}, u32[]{:S(2)}, u32[]{:S(2)}) async-start(bf16[16,8,1024]{2,1,0:T(8,128)(2,1)} %sum_blocks.1), calls=%async_computation.3 | async-start | bytes 524288 | tf_op jit(solution)/shard_map/all_to_all | solution.py:255
  114.8 0.8 copy-done.9
  115.5 3.4 %home.1 = (bf16[2,128,1024]{2,1,0:T(8,128)(2,1)}, bf16[2,128,1024]{2,1,0:T(8,128)(2,1)}) custom-call(bf16[16,48,512]{2,1,0:T(8,128)(2,1)} %copy-done.6, bf16[2,128,1024]{2,1,0:T(8,128)(2,1)} %bitcast.44, bf16[1024,256]{1,0:T(8,128)(2,1)} %get-tuple-element.39.w_mine_ref, bf16[1024,256]{1,0:T(8,128)(2,1)} %copy-done.9), custom_call_target="tpu_custom_call" | custom-call | flops 300000000 | bytes 4194304 | tf_op jit(solution)/shard_map/home/pallas_call | solution.py:382
  118.9 0.0 copy-start.12
  118.9 3.7 %all-to-all-done.3 = bf16[16,8,1024]{2,1,0:T(8,128)(2,1)S(1)} async-done(((bf16[16,8,1024]{2,1,0:T(8,128)(2,1)}), bf16[16,8,1024]{2,1,0:T(8,128)(2,1)S(1)}, u32[]{:S(2)}, u32[]{:S(2)}) %all-to-all-start.3) | async-done | bytes 262176 | tf_op jit(solution)/shard_map/all_to_all | solution.py:255
  122.6 0.2 reshape.80
  122.8 0.1 reduce_sum.18
  122.9 3.7 %collective-permute-start.18 = (f32[4,1024]{1,0:T(4,128)S(1)}, f32[4,1024]{1,0:T(4,128)S(1)}, u32[]{:S(2)}, u32[]{:S(2)}) collective-permute-start(f32[4,1024]{1,0:T(4,128)S(1)} %dynamic-slice_bitcast_fusion.2), channel_id=1, source_target_pairs={{0,16},{16,0},{1,17},{17,1},{2,18},{18,2},{3,19},{19,3},{4,20},{20... | collective-permute-start | bytes 49160 | tf_op jit(solution)/shard_map/ppermute | solution.py:251
  126.6 0.8 collective-permute-done.18
  127.6 0.6 copy.27
  128.3 0.0 copy-start.11
  128.3 0.1 multiply_reduce_fusion
  128.4 0.6 dynamic-slice_divide_fusion
  (46 shorter events, 0.3 us)
Async XLA Ops:
  0.6 11.6 %copy-start = (bf16[1,2,128,1024]{3,2,1,0:T(8,128)(2,1)S(1)}, bf16[1,2,128,1024]{3,2,1,0:T(8,128)(2,1)}, u32[]{:S(2)}) copy-start(bf16[1,2,128,1024]{3,2,1,0:T(8,128)(2,1)} %param.9) | copy-start | bytes 1572868
  2.1 18.8 %all-to-all-start = ((bf16[16,8,1024]{2,1,0:T(8,128)(2,1)}), bf16[16,8,1024]{2,1,0:T(8,128)(2,1)S(1)}, u32[]{:S(2)}, u32[]{:S(2)}) async-start(bf16[16,8,1024]{2,1,0:T(8,128)(2,1)} %pack_weights.1), calls=%async_computation | async-start | bytes 524288 | tf_op jit(solution)/shard_map/all_to_all | solution.py:255
  21.2 3.6 %collective-permute-start = (bf16[64,1024]{1,0:T(8,128)(2,1)S(1)}, bf16[64,1024]{1,0:T(8,128)(2,1)S(1)}, u32[]{:S(2)}, u32[]{:S(2)}) collective-permute-start(bf16[64,1024]{1,0:T(8,128)(2,1)S(1)} %reshape.75), channel_id=1, source_target_pairs={{0,16},{16,0},{1,17},{17,1},{2,18},{18,2},{3,19},{19,3},{4,20},{20... | collective-permute-start | bytes 393224 | tf_op jit(solution)/shard_map/ppermute | solution.py:251
  24.8 36.3 %copy-start.10 = (bf16[128,1024]{1,0:T(8,128)(2,1)}, bf16[128,1024]{1,0:T(8,128)(2,1)S(1)}, u32[]{:S(2)}) copy-start(bf16[128,1024]{1,0:T(8,128)(2,1)S(1)} %pad_maximum_fusion.1.refs_0_) | copy-start | bytes 786436
  24.8 29.6 %all-to-all-start.1 = ((bf16[16,32,1024]{2,1,0:T(8,128)(2,1)}), bf16[16,32,1024]{2,1,0:T(8,128)(2,1)S(1)}, u32[]{:S(2)}, u32[]{:S(2)}) async-start(bf16[16,32,1024]{2,1,0:T(8,128)(2,1)} %pad_maximum_fusion), calls=%async_computation.1 | async-start | bytes 2097152 | tf_op jit(solution)/shard_map/all_to_all | solution.py:255
  29.1 13.8 %collective-permute-start.5 = (bf16[128,1024]{1,0:T(8,128)(2,1)S(1)}, bf16[128,1024]{1,0:T(8,128)(2,1)S(1)}, u32[]{:S(2)}, u32[]{:S(2)}) collective-permute-start(bf16[128,1024]{1,0:T(8,128)(2,1)S(1)} %pad_maximum_fusion.1.refs_0_), channel_id=1, source_target_pairs={{0,32},{32,0},{1,33},{33,1},{2,34},{34,2},{3,35},{35,3},{4,36},{36... | collective-permute-start | bytes 786440 | tf_op jit(solution)/shard_map/ppermute | solution.py:263
  31.6 14.4 %collective-permute-start.4 = (bf16[128,1024]{1,0:T(8,128)(2,1)S(1)}, bf16[128,1024]{1,0:T(8,128)(2,1)S(1)}, u32[]{:S(2)}, u32[]{:S(2)}) collective-permute-start(bf16[128,1024]{1,0:T(8,128)(2,1)S(1)} %pad_maximum_fusion.1.refs_0_), channel_id=1, source_target_pairs={{0,192},{64,0},{128,64},{192,128},{1,193},{65,1},{129,65},{193,129... | collective-permute-start | bytes 786440 | tf_op jit(solution)/shard_map/ppermute | solution.py:259
  34.3 12.3 %collective-permute-start.3 = (bf16[128,1024]{1,0:T(8,128)(2,1)S(1)}, bf16[128,1024]{1,0:T(8,128)(2,1)S(1)}, u32[]{:S(2)}, u32[]{:S(2)}) collective-permute-start(bf16[128,1024]{1,0:T(8,128)(2,1)S(1)} %pad_maximum_fusion.1.refs_0_), channel_id=1, source_target_pairs={{0,128},{64,192},{128,0},{192,64},{1,129},{65,193},{129,1},{193,65... | collective-permute-start | bytes 786440 | tf_op jit(solution)/shard_map/ppermute | solution.py:259
  34.7 22.5 %collective-permute-start.2 = (bf16[128,1024]{1,0:T(8,128)(2,1)S(1)}, bf16[128,1024]{1,0:T(8,128)(2,1)}, u32[]{:S(2)}, u32[]{:S(2)}) collective-permute-start(bf16[128,1024]{1,0:T(8,128)(2,1)S(1)} %pad_maximum_fusion.1.refs_0_), channel_id=1, source_target_pairs={{0,64},{64,128},{128,192},{192,0},{1,65},{65,129},{129,193},{193,1... | collective-permute-start | bytes 786440 | tf_op jit(solution)/shard_map/ppermute | solution.py:259
  42.9 18.2 %copy-start.14 = (bf16[128,1024]{1,0:T(8,128)(2,1)}, bf16[128,1024]{1,0:T(8,128)(2,1)S(1)}, u32[]{:S(2)}) copy-start(bf16[128,1024]{1,0:T(8,128)(2,1)S(1)} %collective-permute-done.5.refs_4_) | copy-start | bytes 786436
  42.9 14.3 %collective-permute-start.8 = (bf16[128,1024]{1,0:T(8,128)(2,1)S(1)}, bf16[128,1024]{1,0:T(8,128)(2,1)}, u32[]{:S(2)}, u32[]{:S(2)}) collective-permute-start(bf16[128,1024]{1,0:T(8,128)(2,1)S(1)} %collective-permute-done.5.refs_4_), channel_id=1, source_target_pairs={{0,192},{64,0},{128,64},{192,128},{1,193},{65,1},{129,65},{193,129... | collective-permute-start | bytes 786440 | tf_op jit(solution)/shard_map/ppermute | solution.py:259
  45.6 11.5 %collective-permute-start.7 = (bf16[128,1024]{1,0:T(8,128)(2,1)S(1)}, bf16[128,1024]{1,0:T(8,128)(2,1)}, u32[]{:S(2)}, u32[]{:S(2)}) collective-permute-start(bf16[128,1024]{1,0:T(8,128)(2,1)S(1)} %collective-permute-done.5.refs_4_), channel_id=1, source_target_pairs={{0,128},{64,192},{128,0},{192,64},{1,129},{65,193},{129,1},{193,65... | collective-permute-start | bytes 786440 | tf_op jit(solution)/shard_map/ppermute | solution.py:259
  46.0 15.1 %copy-start.15 = (bf16[128,1024]{1,0:T(8,128)(2,1)}, bf16[128,1024]{1,0:T(8,128)(2,1)S(1)}, u32[]{:S(2)}) copy-start(bf16[128,1024]{1,0:T(8,128)(2,1)S(1)} %collective-permute-done.4.refs_3_) | copy-start | bytes 786436
  46.0 15.1 %collective-permute-start.6 = (bf16[128,1024]{1,0:T(8,128)(2,1)S(1)}, bf16[128,1024]{1,0:T(8,128)(2,1)}, u32[]{:S(2)}, u32[]{:S(2)}) collective-permute-start(bf16[128,1024]{1,0:T(8,128)(2,1)S(1)} %collective-permute-done.5.refs_4_), channel_id=1, source_target_pairs={{0,64},{64,128},{128,192},{192,0},{1,65},{65,129},{129,193},{193,1... | collective-permute-start | bytes 786440 | tf_op jit(solution)/shard_map/ppermute | solution.py:259
  46.7 0.7 copy-start.16
  54.4 7.3 %copy-start.1 = (bf16[16,32,1024]{2,1,0:T(8,128)(2,1)}, bf16[16,32,1024]{2,1,0:T(8,128)(2,1)S(1)}, u32[]{:S(2)}) copy-start(bf16[16,32,1024]{2,1,0:T(8,128)(2,1)S(1)} %all-to-all-done.1.got_own_ref.got_ref) | copy-start | bytes 3145732
  54.4 7.3 %collective-permute-start.1 = (bf16[16,32,1024]{2,1,0:T(8,128)(2,1)S(1)}, bf16[16,32,1024]{2,1,0:T(8,128)(2,1)S(1)}, u32[]{:S(2)}, u32[]{:S(2)}) collective-permute-start(bf16[16,32,1024]{2,1,0:T(8,128)(2,1)S(1)} %all-to-all-done.1.got_own_ref.got_ref), channel_id=1, source_target_pairs={{0,16},{16,0},{1,17},{17,1},{2,18},{18,2},{3,19},{19,3},{4,20},{20... | collective-permute-start | bytes 3145736 | tf_op jit(solution)/shard_map/ppermute | solution.py:251
  61.7 1.0 copy-start.13
  62.7 14.1 %copy-start.2 = (bf16[16,32,1024]{2,1,0:T(8,128)(2,1)S(1)}, bf16[16,32,1024]{2,1,0:T(8,128)(2,1)}, u32[]{:S(2)}) copy-start(bf16[16,32,1024]{2,1,0:T(8,128)(2,1)} %copy-done.1) | copy-start | bytes 3145732
  62.7 14.1 %copy-start.4 = (f32[1024]{0:T(1024)S(1)}, f32[1024]{0:T(1024)}, u32[]{:S(2)}) copy-start(f32[1024]{0:T(1024)} %param.6) | copy-start | bytes 12292
  73.5 3.3 %collective-permute-start.16 = (bf16[256,1280]{1,0:T(8,128)(2,1)}, bf16[256,1280]{1,0:T(8,128)(2,1)S(1)}, u32[]{:S(2)}, u32[]{:S(2)}) collective-permute-start(bf16[256,1280]{1,0:T(8,128)(2,1)} %get-tuple-element.36), channel_id=1, source_target_pairs={{0,16},{16,0},{1,17},{17,1},{2,18},{18,2},{3,19},{19,3},{4,20},{20... | collective-permute-start | bytes 1966088 | tf_op jit(solution)/shard_map/ppermute | solution.py:251
  74.1 16.5 %collective-permute-start.12 = (bf16[128,1024]{1,0:T(8,128)(2,1)}, bf16[128,1024]{1,0:T(8,128)(2,1)S(1)}, u32[]{:S(2)}, u32[]{:S(2)}) collective-permute-start(bf16[128,1024]{1,0:T(8,128)(2,1)} %get-tuple-element.32), channel_id=1, source_target_pairs={{0,64},{64,128},{128,192},{192,0},{1,65},{65,129},{129,193},{193,1... | collective-permute-start | bytes 786440 | tf_op jit(solution)/shard_map/ppermute | solution.py:259
  74.1 18.5 %collective-permute-start.13 = (bf16[128,1024]{1,0:T(8,128)(2,1)}, bf16[128,1024]{1,0:T(8,128)(2,1)S(1)}, u32[]{:S(2)}, u32[]{:S(2)}) collective-permute-start(bf16[128,1024]{1,0:T(8,128)(2,1)} %get-tuple-element.33), channel_id=1, source_target_pairs={{0,128},{64,192},{128,0},{192,64},{1,129},{65,193},{129,1},{193,65... | collective-permute-start | bytes 786440 | tf_op jit(solution)/shard_map/ppermute | solution.py:259
  75.6 17.0 %collective-permute-start.14 = (bf16[128,1024]{1,0:T(8,128)(2,1)}, bf16[128,1024]{1,0:T(8,128)(2,1)}, u32[]{:S(2)}, u32[]{:S(2)}) collective-permute-start(bf16[128,1024]{1,0:T(8,128)(2,1)} %get-tuple-element.34), channel_id=1, source_target_pairs={{0,192},{64,0},{128,64},{192,128},{1,193},{65,1},{129,65},{193,129... | collective-permute-start | bytes 786440 | tf_op jit(solution)/shard_map/ppermute | solution.py:259
  76.8 1.3 %copy-start.3 = (f32[256,1280]{1,0:T(8,128)S(1)}, f32[256,1280]{1,0:T(8,128)}, u32[]{:S(2)}) copy-start(f32[256,1280]{1,0:T(8,128)} %get-tuple-element.35.mine_ref) | copy-start | bytes 3932164
  79.9 12.7 %copy-start.7 = (f32[128,1024]{1,0:T(8,128)S(1)}, f32[128,1024]{1,0:T(8,128)}, u32[]{:S(2)}) copy-start(f32[128,1024]{1,0:T(8,128)} %get-tuple-element.31) | copy-start | bytes 1572868
  79.9 15.7 %copy-start.8 = (bf16[1024,256]{1,0:T(8,128)(2,1)S(1)}, bf16[1024,256]{1,0:T(8,128)(2,1)}, u32[]{:S(2)}) copy-start(bf16[1024,256]{1,0:T(8,128)(2,1)} %get-tuple-element.39.w_mine_ref) | copy-start | bytes 1572868
  79.9 27.0 %copy-start.5 = (f32[128,1024]{1,0:T(8,128)S(1)}, f32[128,1024]{1,0:T(8,128)}, u32[]{:S(2)}) copy-start(f32[128,1024]{1,0:T(8,128)} %get-tuple-element.27.own_ref) | copy-start | bytes 1572868
  79.9 27.9 %all-to-all-start.2 = ((bf16[16,48,512]{2,1,0:T(8,128)(2,1)}), bf16[16,48,512]{2,1,0:T(8,128)(2,1)S(1)}, u32[]{:S(2)}, u32[]{:S(2)}) async-start(bf16[16,48,512]{2,1,0:T(8,128)(2,1)} %input_gradient.1), calls=%async_computation.2 | async-start | bytes 1572864 | tf_op jit(solution)/shard_map/all_to_all | solution.py:255
  88.1 9.8 %collective-permute-start.9 = (bf16[128,1024]{1,0:T(8,128)(2,1)}, bf16[128,1024]{1,0:T(8,128)(2,1)S(1)}, u32[]{:S(2)}, u32[]{:S(2)}) collective-permute-start(bf16[128,1024]{1,0:T(8,128)(2,1)} %get-tuple-element.28), channel_id=1, source_target_pairs={{0,64},{64,128},{128,192},{192,0},{1,65},{65,129},{129,193},{193,1... | collective-permute-start | bytes 786440 | tf_op jit(solution)/shard_map/ppermute | solution.py:259
  88.7 13.1 %collective-permute-start.10 = (bf16[128,1024]{1,0:T(8,128)(2,1)}, bf16[128,1024]{1,0:T(8,128)(2,1)S(1)}, u32[]{:S(2)}, u32[]{:S(2)}) collective-permute-start(bf16[128,1024]{1,0:T(8,128)(2,1)} %get-tuple-element.29), channel_id=1, source_target_pairs={{0,128},{64,192},{128,0},{192,64},{1,129},{65,193},{129,1},{193,65... | collective-permute-start | bytes 786440 | tf_op jit(solution)/shard_map/ppermute | solution.py:259
  90.6 12.5 %collective-permute-start.11 = (bf16[128,1024]{1,0:T(8,128)(2,1)}, bf16[128,1024]{1,0:T(8,128)(2,1)S(1)}, u32[]{:S(2)}, u32[]{:S(2)}) collective-permute-start(bf16[128,1024]{1,0:T(8,128)(2,1)} %get-tuple-element.30), channel_id=1, source_target_pairs={{0,192},{64,0},{128,64},{192,128},{1,193},{65,1},{129,65},{193,129... | collective-permute-start | bytes 786440 | tf_op jit(solution)/shard_map/ppermute | solution.py:259
  93.7 13.2 %collective-permute-start.15 = (bf16[128,1024]{1,0:T(8,128)(2,1)S(1)}, bf16[128,1024]{1,0:T(8,128)(2,1)S(1)}, u32[]{:S(2)}, u32[]{:S(2)}) collective-permute-start(bf16[128,1024]{1,0:T(8,128)(2,1)S(1)} %add_convert_fusion), channel_id=1, source_target_pairs={{0,32},{32,0},{1,33},{33,1},{2,34},{34,2},{3,35},{35,3},{4,36},{36... | collective-permute-start | bytes 786440 | tf_op jit(solution)/shard_map/ppermute | solution.py:263
  95.6 19.2 %collective-permute-start.17 = (bf16[1024,256]{1,0:T(8,128)(2,1)S(1)}, bf16[1024,256]{1,0:T(8,128)(2,1)S(1)}, u32[]{:S(2)}, u32[]{:S(2)}) collective-permute-start(bf16[1024,256]{1,0:T(8,128)(2,1)S(1)} %copy-done.8), channel_id=1, source_target_pairs={{0,16},{16,0},{1,17},{17,1},{2,18},{18,2},{3,19},{19,3},{4,20},{20... | collective-permute-start | bytes 1572872 | tf_op jit(solution)/shard_map/ppermute | solution.py:251
  107.9 6.9 %copy-start.6 = (bf16[16,48,512]{2,1,0:T(8,128)(2,1)}, bf16[16,48,512]{2,1,0:T(8,128)(2,1)S(1)}, u32[]{:S(2)}) copy-start(bf16[16,48,512]{2,1,0:T(8,128)(2,1)S(1)} %all-to-all-done.2.got_ref) | copy-start | bytes 2359300
  107.9 14.7 %all-to-all-start.3 = ((bf16[16,8,1024]{2,1,0:T(8,128)(2,1)}), bf16[16,8,1024]{2,1,0:T(8,128)(2,1)S(1)}, u32[]{:S(2)}, u32[]{:S(2)}) async-start(bf16[16,8,1024]{2,1,0:T(8,128)(2,1)} %sum_blocks.1), calls=%async_computation.3 | async-start | bytes 524288 | tf_op jit(solution)/shard_map/all_to_all | solution.py:255
  114.7 0.8 copy-start.9
  118.9 9.3 %copy-start.12 = (bf16[4,1536]{1,0:T(4,128)(2,1)S(1)}, bf16[4,1536]{1,0:T(4,128)(2,1)}, u32[]{:S(2)}) copy-start(bf16[4,1536]{1,0:T(4,128)(2,1)} %w_qkv_ref.1) | copy-start | bytes 36868
  122.9 4.6 %collective-permute-start.18 = (f32[4,1024]{1,0:T(4,128)S(1)}, f32[4,1024]{1,0:T(4,128)S(1)}, u32[]{:S(2)}, u32[]{:S(2)}) collective-permute-start(f32[4,1024]{1,0:T(4,128)S(1)} %dynamic-slice_bitcast_fusion.2), channel_id=1, source_target_pairs={{0,16},{16,0},{1,17},{17,1},{2,18},{18,2},{3,19},{19,3},{4,20},{20... | collective-permute-start | bytes 49160 | tf_op jit(solution)/shard_map/ppermute | solution.py:251
  128.3 0.7 copy-start.11

commit v6 on v5

--- a/solution.py
+++ b/solution.py
@@ -164,14 +164,13 @@
     pair_rows = 2 * block
     all_dpacked = dpacked[...].reshape(2 * rows, 3 * HALF)
     all_mixed = mixed[...].reshape(2 * rows, HALF)
-    y, xh = lax.axis_index("y"), lax.axis_index("xh")
+    for part in range(Y_SIZE):
+        columns = slice(part * pair_rows, (part + 1) * pair_rows)
+        grads[columns, : 3 * HALF] = mm(normed[:, :, columns].reshape(2 * rows, pair_rows), all_dpacked, TN)
+        grads[columns, 3 * HALF :] = mm(got[:, :, per_peer:, columns].reshape(2 * rows, pair_rows), all_mixed, TN)
     for step in (1, 2, 3, 0):
-        start = pl.multiple_of(lax.rem(y + step, Y_SIZE) * pair_rows, pair_rows)
-        columns = pl.ds(start, pair_rows)
-        grads[:, : 3 * HALF] = mm(normed[:, :, columns].reshape(2 * rows, pair_rows), all_dpacked, TN)
-        grads[:, 3 * HALF :] = mm(got[:, :, per_peer:, columns].reshape(2 * rows, pair_rows), all_mixed, TN)
         for side in range(XH_SIZE):
-            start = pl.multiple_of(lax.rem(xh + side, XH_SIZE) * block, block)
+            start = pl.multiple_of(block_of(step, side) * block, block)
             slot = own.at[side] if step == 0 else peers.at[side * (Y_SIZE - 1) + step - 1]
             slot[...] = grads[pl.ds(start, block), :].astype(slot.dtype)
             results += fetch([(slot, grad_refs[side * Y_SIZE + step])], out_sems, len(results))
@@ -288,6 +287,9 @@
     )(w_qkv, w_out.T)
     w_got = swap(w_parts.reshape(-1, width), TM).reshape(tm, 2, shard, width)
 
+    sent = jnp.concatenate([by_patch(frames_in), by_patch(out_grad)], axis=1)
+    sent, w_got = lax.optimization_barrier((sent, w_got))
+
     w_keep = lax.dynamic_index_in_dim(w_got, core, 1, keepdims=False).reshape(tm * shard, width)
     w_send = lax.dynamic_index_in_dim(w_got, 1 - core, 1, keepdims=False).reshape(tm * shard, width)
     w_recv = exchange(w_send)
@@ -296,8 +298,6 @@
     )
     block = w_block.shape[0]
 
-    sent = jnp.concatenate([by_patch(frames_in), by_patch(out_grad)], axis=1)
-    sent, w_block = lax.optimization_barrier((sent, w_block))
     got = swap(sent.reshape(-1, width), TM).reshape(tm, 2 * per_peer, width)
 
     pieces = []
@@ -332,7 +332,7 @@
             pltpu.VMEM((2, rows, 3 * HALF), bf16),
             pltpu.VMEM((rows, width + HALF), f32),
             pltpu.VMEM((rows, width + HALF), bf16),
-            pltpu.VMEM((2 * block, width), f32),
+            pltpu.VMEM((width, width), f32),
             pltpu.VMEM((2, block, width), f32),
             pltpu.VMEM((6, block, width), bf16),
             pltpu.VMEM((HALF // DH, rows, rows), f32),

time: 130 us -> 129 us (level)
  waiting for transfers between devices: 39.6 us -> 37.8 us
  starting transfers between devices: 60.2 us -> 62 us
    all_to_all x4, waiting for transfers between devices: 18.2 us -> 14 us  [swap(): return lax.all_to_all(value, axes, split_axis=0, concat_axis=0, tiled=True)]
    ppermute x12, waiting for transfers between devices: 9.16 us -> 10.9 us  [along_y(): lax.ppermute(value, 'y', [(i, (i + step) % Y_SIZE) for i in range(Y_SIZE)])]
    ppermute x2, starting transfers between devices: 4.38 us -> 6.09 us  [across_x(): return lax.ppermute(value, 'xh', [(0, 1), (1, 0)])]
    unnamed x37 -> x36, local copies, waits for them, and re-layouts: 4.55 us -> 4.44 us
  transfers between devices with their start and end apart: 23 -> 23, of which waited for: 9 -> 11; matrix products, arithmetic and copies ran while one was open for 3% -> 3% of each run, Pallas kernels for 5% -> 5%
where the time goes in v6:
time: 129 us
  starting transfers between devices  62 us (48%)
  waiting for transfers between devices  37.8 us (29%)
  Pallas kernels  18.7 us (14%)
  local copies, waits for them, and re-layouts  6.2 us (5%)
  other arithmetic  3.06 us (2%)
    all_to_all x4, starting transfers between devices, swap(): return lax.all_to_all(value, axes, split_axis=0, concat_axis=0, tiled=True)  29.5 us
    ppermute x12, starting transfers between devices, along_y(): lax.ppermute(value, 'y', [(i, (i + step) % Y_SIZE) for i in range(Y_SIZE)])  14.8 us
    all_to_all x4, waiting for transfers between devices, swap(): return lax.all_to_all(value, axes, split_axis=0, concat_axis=0, tiled=True)  14 us
    ppermute x5, starting transfers between devices, exchange(): return lax.ppermute(value, 'core', [(0, 1), (1, 0)])  11.7 us
    ppermute x2, waiting for transfers between devices, across_x(): return lax.ppermute(value, 'xh', [(0, 1), (1, 0)])  11.2 us
    ppermute x12, waiting for transfers between devices, along_y(): lax.ppermute(value, 'y', [(i, (i + step) % Y_SIZE) for i in range(Y_SIZE)])  10.9 us
    pallas_call x1, Pallas kernels, body(): pl.pallas_call(functools.partial(layer_kernel, patches), in_specs=[ANY, A...  10.6 us
    ppermute x2, starting transfers between devices, across_x(): return lax.ppermute(value, 'xh', [(0, 1), (1, 0)])  6.09 us
  transfers between devices with their start and end apart: 23, of which 11 were waited for; matrix products, arithmetic and copies ran while one was open for 3% of the time, Pallas kernels for 5%

profile of v6, /device:TPU:1, one launch (start us, length us, event | category | flops | bytes accessed | tf_op | source)
XLA Modules:
  0.0 128.7 jit_solution(7895426206209257925)
XLA Ops:
  0.6 0.0 copy-start
  0.6 1.5 %pack_weights.1 = bf16[16,8,1024]{2,1,0:T(8,128)(2,1)} custom-call(bf16[4,1536]{1,0:T(4,128)(2,1)} %w_qkv_ref.1, bf16[4,512]{1,0:T(4,128)(2,1)} %bitcast.45), custom_call_target="tpu_custom_call" | custom-call | bytes 262144 | tf_op jit(solution)/shard_map/pack_weights/pallas_call | solution.py:280
  2.1 10.0 %all-to-all-start = ((bf16[16,8,1024]{2,1,0:T(8,128)(2,1)}), bf16[16,8,1024]{2,1,0:T(8,128)(2,1)S(1)}, u32[]{:S(2)}, u32[]{:S(2)}) async-start(bf16[16,8,1024]{2,1,0:T(8,128)(2,1)} %pack_weights.1), calls=%async_computation | async-start | bytes 524288 | tf_op jit(solution)/shard_map/all_to_all | solution.py:254
  12.2 1.2 copy_bitcast_fusion
  13.4 1.1 pad_maximum_fusion
  14.5 6.4 %all-to-all-done = bf16[16,8,1024]{2,1,0:T(8,128)(2,1)S(1)} async-done(((bf16[16,8,1024]{2,1,0:T(8,128)(2,1)}), bf16[16,8,1024]{2,1,0:T(8,128)(2,1)S(1)}, u32[]{:S(2)}, u32[]{:S(2)}) %all-to-all-start) | async-done | bytes 262176 | tf_op jit(solution)/shard_map/all_to_all | solution.py:254
  20.9 0.1 reshape.73
  21.0 5.4 %all-to-all-start.1 = ((bf16[16,32,1024]{2,1,0:T(8,128)(2,1)}), bf16[16,32,1024]{2,1,0:T(8,128)(2,1)S(1)}, u32[]{:S(2)}, u32[]{:S(2)}) async-start(bf16[16,32,1024]{2,1,0:T(8,128)(2,1)} %pad_maximum_fusion), calls=%async_computation.1 | async-start | bytes 2097152 | tf_op jit(solution)/shard_map/all_to_all | solution.py:254
  26.4 0.1 constant_dynamic-slice_fusion.1
  26.6 1.6 %collective-permute-start.1 = (bf16[64,1024]{1,0:T(8,128)(2,1)S(1)}, bf16[64,1024]{1,0:T(8,128)(2,1)S(1)}, u32[]{:S(2)}, u32[]{:S(2)}) collective-permute-start(bf16[64,1024]{1,0:T(8,128)(2,1)S(1)} %reshape.76), channel_id=1, source_target_pairs={{0,16},{16,0},{1,17},{17,1},{2,18},{18,2},{3,19},{19,3},{4,20},{20... | collective-permute-start | bytes 393224 | tf_op jit(solution)/shard_map/ppermute | solution.py:250
  28.2 1.0 collective-permute-done.1
  29.2 2.5 %collective-permute-start.5 = (bf16[128,1024]{1,0:T(8,128)(2,1)S(1)}, bf16[128,1024]{1,0:T(8,128)(2,1)S(1)}, u32[]{:S(2)}, u32[]{:S(2)}) collective-permute-start(bf16[128,1024]{1,0:T(8,128)(2,1)S(1)} %pad_maximum_fusion.1.refs_0_), channel_id=1, source_target_pairs={{0,32},{32,0},{1,33},{33,1},{2,34},{34,2},{3,35},{35,3},{4,36},{36... | collective-permute-start | bytes 786440 | tf_op jit(solution)/shard_map/ppermute | solution.py:262
  31.7 2.7 %collective-permute-start.4 = (bf16[128,1024]{1,0:T(8,128)(2,1)S(1)}, bf16[128,1024]{1,0:T(8,128)(2,1)S(1)}, u32[]{:S(2)}, u32[]{:S(2)}) collective-permute-start(bf16[128,1024]{1,0:T(8,128)(2,1)S(1)} %pad_maximum_fusion.1.refs_0_), channel_id=1, source_target_pairs={{0,192},{64,0},{128,64},{192,128},{1,193},{65,1},{129,65},{193,129... | collective-permute-start | bytes 786440 | tf_op jit(solution)/shard_map/ppermute | solution.py:258
  34.5 0.3 collective-permute-start.3
  34.8 0.7 collective-permute-start.2
  35.5 7.0 %collective-permute-done.5.refs_4_ = bf16[128,1024]{1,0:T(8,128)(2,1)S(1)} collective-permute-done((bf16[128,1024]{1,0:T(8,128)(2,1)S(1)}, bf16[128,1024]{1,0:T(8,128)(2,1)S(1)}, u32[]{:S(2)}, u32[]{:S(2)}) %collective-permute-start.5) | collective-permute-done | bytes 262176 | tf_op jit(solution)/shard_map/ppermute | solution.py:262
  42.5 2.7 %collective-permute-start.8 = (bf16[128,1024]{1,0:T(8,128)(2,1)S(1)}, bf16[128,1024]{1,0:T(8,128)(2,1)}, u32[]{:S(2)}, u32[]{:S(2)}) collective-permute-start(bf16[128,1024]{1,0:T(8,128)(2,1)S(1)} %collective-permute-done.5.refs_4_), channel_id=1, source_target_pairs={{0,192},{64,0},{128,64},{192,128},{1,193},{65,1},{129,65},{193,129... | collective-permute-start | bytes 786440 | tf_op jit(solution)/shard_map/ppermute | solution.py:258
  45.3 0.3 collective-permute-start.7
  45.6 0.0 collective-permute-done.4.refs_3_
  45.6 0.7 collective-permute-start.6
  46.3 0.7 copy-done.16
  47.0 4.0 %all-to-all-done.1.got_own_ref.got_ref = bf16[16,32,1024]{2,1,0:T(8,128)(2,1)S(1)} async-done(((bf16[16,32,1024]{2,1,0:T(8,128)(2,1)}), bf16[16,32,1024]{2,1,0:T(8,128)(2,1)S(1)}, u32[]{:S(2)}, u32[]{:S(2)}) %all-to-all-start.1) | async-done | bytes 1048608 | tf_op jit(solution)/shard_map/all_to_all | solution.py:254
  51.0 2.7 %collective-permute-start = (bf16[16,32,1024]{2,1,0:T(8,128)(2,1)S(1)}, bf16[16,32,1024]{2,1,0:T(8,128)(2,1)S(1)}, u32[]{:S(2)}, u32[]{:S(2)}) collective-permute-start(bf16[16,32,1024]{2,1,0:T(8,128)(2,1)S(1)} %all-to-all-done.1.got_own_ref.got_ref), channel_id=1, source_target_pairs={{0,16},{16,0},{1,17},{17,1},{2,18},{18,2},{3,19},{19,3},{4,20},{20... | collective-permute-start | bytes 3145736 | tf_op jit(solution)/shard_map/ppermute | solution.py:250
  53.7 0.0 collective-permute-done.2.refs_1_
  53.7 0.0 collective-permute-done.8.refs_7_
  53.7 0.5 collective-permute-done.7.refs_6_
  54.2 6.8 %collective-permute-done.6.refs_5_ = bf16[128,1024]{1,0:T(8,128)(2,1)} collective-permute-done((bf16[128,1024]{1,0:T(8,128)(2,1)S(1)}, bf16[128,1024]{1,0:T(8,128)(2,1)}, u32[]{:S(2)}, u32[]{:S(2)}) %collective-permute-start.6) | collective-permute-done | bytes 262176 | tf_op jit(solution)/shard_map/ppermute | solution.py:258
  61.1 0.6 arrived.1.token_ref
  61.7 0.0 collective-permute-done.got_other_ref
  61.7 1.0 copy-done.13
  62.7 10.6 %layer.1 = (bf16[1024,256]{1,0:T(8,128)(2,1)}, f32[256,1280]{1,0:T(8,128)}, bf16[256,1280]{1,0:T(8,128)(2,1)}, f32[128,1024]{1,0:T(8,128)}, bf16[128,1024]{1,0:T...) custom-call(bf16[16,32,1024]{2,1,0:T(8,128)(2,1)} %copy-done.1, ...), custom_call_target="tpu_custom_call" | custom-call | flops 30000001024 | bytes 10485760 | tf_op jit(solution)/shard_map/layer/pallas_call | solution.py:321
  73.3 0.7 collective-permute-start.16
  73.9 1.6 %collective-permute-start.13 = (bf16[128,1024]{1,0:T(8,128)(2,1)}, bf16[128,1024]{1,0:T(8,128)(2,1)S(1)}, u32[]{:S(2)}, u32[]{:S(2)}) collective-permute-start(bf16[128,1024]{1,0:T(8,128)(2,1)} %get-tuple-element.33), channel_id=1, source_target_pairs={{0,128},{64,192},{128,0},{192,64},{1,129},{65,193},{129,1},{193,65... | collective-permute-start | bytes 786440 | tf_op jit(solution)/shard_map/ppermute | solution.py:258
  75.5 1.1 collective-permute-start.14
  76.7 1.3 %copy-done.3 = f32[256,1280]{1,0:T(8,128)S(1)} copy-done((f32[256,1280]{1,0:T(8,128)S(1)}, f32[256,1280]{1,0:T(8,128)}, u32[]{:S(2)}) %copy-start.3) | copy-done | bytes 1310744
  78.0 1.8 %input_gradient.1 = bf16[16,48,512]{2,1,0:T(8,128)(2,1)} custom-call(bf16[16,32,1024]{2,1,0:T(8,128)(2,1)S(1)} %copy-done.2, f32[256,1280]{1,0:T(8,128)S(1)} %copy-done.3, bf16[256,1280]{1,0:T(8,128)(2,1)S(1)} %collective-permute-done.16.other, f32[1,1024]{1,0:T(1,128)S(1)} %bitcast.39), custom_call_target="tpu_custom_call" | custom-call | flops 1000000000 | bytes 6291456 | tf_op jit(solution)/shard_map/input_gradient/pallas_call | solution.py:364
  79.8 0.0 copy-start.7
  79.8 0.0 copy-start.5
  79.8 7.4 %all-to-all-start.2 = ((bf16[16,48,512]{2,1,0:T(8,128)(2,1)}), bf16[16,48,512]{2,1,0:T(8,128)(2,1)S(1)}, u32[]{:S(2)}, u32[]{:S(2)}) async-start(bf16[16,48,512]{2,1,0:T(8,128)(2,1)} %input_gradient.1), calls=%async_computation.2 | async-start | bytes 1572864 | tf_op jit(solution)/shard_map/all_to_all | solution.py:254
  87.2 0.7 collective-permute-start.9
  87.8 1.9 %collective-permute-start.10 = (bf16[128,1024]{1,0:T(8,128)(2,1)}, bf16[128,1024]{1,0:T(8,128)(2,1)S(1)}, u32[]{:S(2)}, u32[]{:S(2)}) collective-permute-start(bf16[128,1024]{1,0:T(8,128)(2,1)} %get-tuple-element.29), channel_id=1, source_target_pairs={{0,128},{64,192},{128,0},{192,64},{1,129},{65,193},{129,1},{193,65... | collective-permute-start | bytes 786440 | tf_op jit(solution)/shard_map/ppermute | solution.py:258
  89.7 2.0 %collective-permute-start.11 = (bf16[128,1024]{1,0:T(8,128)(2,1)}, bf16[128,1024]{1,0:T(8,128)(2,1)S(1)}, u32[]{:S(2)}, u32[]{:S(2)}) collective-permute-start(bf16[128,1024]{1,0:T(8,128)(2,1)} %get-tuple-element.30), channel_id=1, source_target_pairs={{0,192},{64,0},{128,64},{192,128},{1,193},{65,1},{129,65},{193,129... | collective-permute-start | bytes 786440 | tf_op jit(solution)/shard_map/ppermute | solution.py:258
  91.7 0.0 collective-permute-done.13
  91.7 0.0 collective-permute-done.14
  91.7 1.1 add_convert_fusion
  92.8 3.5 %collective-permute-start.15 = (bf16[128,1024]{1,0:T(8,128)(2,1)S(1)}, bf16[128,1024]{1,0:T(8,128)(2,1)S(1)}, u32[]{:S(2)}, u32[]{:S(2)}) collective-permute-start(bf16[128,1024]{1,0:T(8,128)(2,1)S(1)} %add_convert_fusion), channel_id=1, source_target_pairs={{0,32},{32,0},{1,33},{33,1},{2,34},{34,2},{3,35},{35,3},{4,36},{36... | collective-permute-start | bytes 786440 | tf_op jit(solution)/shard_map/ppermute | solution.py:262
  96.4 2.3 %collective-permute-start.17 = (bf16[1024,256]{1,0:T(8,128)(2,1)S(1)}, bf16[1024,256]{1,0:T(8,128)(2,1)S(1)}, u32[]{:S(2)}, u32[]{:S(2)}) collective-permute-start(bf16[1024,256]{1,0:T(8,128)(2,1)S(1)} %copy-done.8), channel_id=1, source_target_pairs={{0,16},{16,0},{1,17},{17,1},{2,18},{18,2},{3,19},{19,3},{4,20},{20... | collective-permute-start | bytes 1572872 | tf_op jit(solution)/shard_map/ppermute | solution.py:250
  98.7 2.2 %collective-permute-done.10.b_ref = bf16[128,1024]{1,0:T(8,128)(2,1)S(1)} collective-permute-done((bf16[128,1024]{1,0:T(8,128)(2,1)}, bf16[128,1024]{1,0:T(8,128)(2,1)S(1)}, u32[]{:S(2)}, u32[]{:S(2)}) %collective-permute-start.10) | collective-permute-done | bytes 262176 | tf_op jit(solution)/shard_map/ppermute | solution.py:258
  100.9 1.3 collective-permute-done.11.c_ref
  102.2 4.1 %collective-permute-done.15.across_ref = bf16[128,1024]{1,0:T(8,128)(2,1)S(1)} collective-permute-done((bf16[128,1024]{1,0:T(8,128)(2,1)S(1)}, bf16[128,1024]{1,0:T(8,128)(2,1)S(1)}, u32[]{:S(2)}, u32[]{:S(2)}) %collective-permute-start.15) | collective-permute-done | bytes 262176 | tf_op jit(solution)/shard_map/ppermute | solution.py:262
  106.3 0.9 sum_blocks.1
  107.3 6.6 %all-to-all-start.3 = ((bf16[16,8,1024]{2,1,0:T(8,128)(2,1)}), bf16[16,8,1024]{2,1,0:T(8,128)(2,1)S(1)}, u32[]{:S(2)}, u32[]{:S(2)}) async-start(bf16[16,8,1024]{2,1,0:T(8,128)(2,1)} %sum_blocks.1), calls=%async_computation.3 | async-start | bytes 524288 | tf_op jit(solution)/shard_map/all_to_all | solution.py:254
  113.9 0.8 copy-done.9
  114.7 3.4 %home.1 = (bf16[2,128,1024]{2,1,0:T(8,128)(2,1)}, bf16[2,128,1024]{2,1,0:T(8,128)(2,1)}) custom-call(bf16[16,48,512]{2,1,0:T(8,128)(2,1)} %copy-done.6, bf16[2,128,1024]{2,1,0:T(8,128)(2,1)} %bitcast.40, bf16[1024,256]{1,0:T(8,128)(2,1)} %get-tuple-element.39.w_mine_ref, bf16[1024,256]{1,0:T(8,128)(2,1)} %copy-done.9), custom_call_target="tpu_custom_call" | custom-call | flops 300000000 | bytes 4194304 | tf_op jit(solution)/shard_map/home/pallas_call | solution.py:382
  118.1 0.0 copy-start.12
  118.1 3.6 %all-to-all-done.3 = bf16[16,8,1024]{2,1,0:T(8,128)(2,1)S(1)} async-done(((bf16[16,8,1024]{2,1,0:T(8,128)(2,1)}), bf16[16,8,1024]{2,1,0:T(8,128)(2,1)S(1)}, u32[]{:S(2)}, u32[]{:S(2)}) %all-to-all-start.3) | async-done | bytes 262176 | tf_op jit(solution)/shard_map/all_to_all | solution.py:254
  121.7 0.2 reshape.80
  121.8 0.1 reduce_sum.18
  122.0 4.4 %collective-permute-start.18 = (f32[4,1024]{1,0:T(4,128)S(1)}, f32[4,1024]{1,0:T(4,128)S(1)}, u32[]{:S(2)}, u32[]{:S(2)}) collective-permute-start(f32[4,1024]{1,0:T(4,128)S(1)} %dynamic-slice_bitcast_fusion), channel_id=1, source_target_pairs={{0,16},{16,0},{1,17},{17,1},{2,18},{18,2},{3,19},{19,3},{4,20},{20... | collective-permute-start | bytes 49160 | tf_op jit(solution)/shard_map/ppermute | solution.py:250
  126.4 0.8 collective-permute-done.18
  127.3 0.6 copy.25
  128.0 0.0 copy-start.11
  128.0 0.1 multiply_reduce_fusion
  128.1 0.6 dynamic-slice_divide_fusion
  (46 shorter events, 0.3 us)
Async XLA Ops:
  0.6 11.6 %copy-start = (bf16[1,2,128,1024]{3,2,1,0:T(8,128)(2,1)S(1)}, bf16[1,2,128,1024]{3,2,1,0:T(8,128)(2,1)}, u32[]{:S(2)}) copy-start(bf16[1,2,128,1024]{3,2,1,0:T(8,128)(2,1)} %param.9) | copy-start | bytes 1572868
  2.1 18.8 %all-to-all-start = ((bf16[16,8,1024]{2,1,0:T(8,128)(2,1)}), bf16[16,8,1024]{2,1,0:T(8,128)(2,1)S(1)}, u32[]{:S(2)}, u32[]{:S(2)}) async-start(bf16[16,8,1024]{2,1,0:T(8,128)(2,1)} %pack_weights.1), calls=%async_computation | async-start | bytes 524288 | tf_op jit(solution)/shard_map/all_to_all | solution.py:254
  21.0 30.0 %all-to-all-start.1 = ((bf16[16,32,1024]{2,1,0:T(8,128)(2,1)}), bf16[16,32,1024]{2,1,0:T(8,128)(2,1)S(1)}, u32[]{:S(2)}, u32[]{:S(2)}) async-start(bf16[16,32,1024]{2,1,0:T(8,128)(2,1)} %pad_maximum_fusion), calls=%async_computation.1 | async-start | bytes 2097152 | tf_op jit(solution)/shard_map/all_to_all | solution.py:254
  26.6 2.5 %collective-permute-start.1 = (bf16[64,1024]{1,0:T(8,128)(2,1)S(1)}, bf16[64,1024]{1,0:T(8,128)(2,1)S(1)}, u32[]{:S(2)}, u32[]{:S(2)}) collective-permute-start(bf16[64,1024]{1,0:T(8,128)(2,1)S(1)} %reshape.76), channel_id=1, source_target_pairs={{0,16},{16,0},{1,17},{17,1},{2,18},{18,2},{3,19},{19,3},{4,20},{20... | collective-permute-start | bytes 393224 | tf_op jit(solution)/shard_map/ppermute | solution.py:250
  29.2 31.9 %copy-start.10 = (bf16[128,1024]{1,0:T(8,128)(2,1)}, bf16[128,1024]{1,0:T(8,128)(2,1)S(1)}, u32[]{:S(2)}) copy-start(bf16[128,1024]{1,0:T(8,128)(2,1)S(1)} %pad_maximum_fusion.1.refs_0_) | copy-start | bytes 786436
  29.2 13.3 %collective-permute-start.5 = (bf16[128,1024]{1,0:T(8,128)(2,1)S(1)}, bf16[128,1024]{1,0:T(8,128)(2,1)S(1)}, u32[]{:S(2)}, u32[]{:S(2)}) collective-permute-start(bf16[128,1024]{1,0:T(8,128)(2,1)S(1)} %pad_maximum_fusion.1.refs_0_), channel_id=1, source_target_pairs={{0,32},{32,0},{1,33},{33,1},{2,34},{34,2},{3,35},{35,3},{4,36},{36... | collective-permute-start | bytes 786440 | tf_op jit(solution)/shard_map/ppermute | solution.py:262
  31.7 13.9 %collective-permute-start.4 = (bf16[128,1024]{1,0:T(8,128)(2,1)S(1)}, bf16[128,1024]{1,0:T(8,128)(2,1)S(1)}, u32[]{:S(2)}, u32[]{:S(2)}) collective-permute-start(bf16[128,1024]{1,0:T(8,128)(2,1)S(1)} %pad_maximum_fusion.1.refs_0_), channel_id=1, source_target_pairs={{0,192},{64,0},{128,64},{192,128},{1,193},{65,1},{129,65},{193,129... | collective-permute-start | bytes 786440 | tf_op jit(solution)/shard_map/ppermute | solution.py:258
  34.5 11.8 %collective-permute-start.3 = (bf16[128,1024]{1,0:T(8,128)(2,1)S(1)}, bf16[128,1024]{1,0:T(8,128)(2,1)S(1)}, u32[]{:S(2)}, u32[]{:S(2)}) collective-permute-start(bf16[128,1024]{1,0:T(8,128)(2,1)S(1)} %pad_maximum_fusion.1.refs_0_), channel_id=1, source_target_pairs={{0,128},{64,192},{128,0},{192,64},{1,129},{65,193},{129,1},{193,65... | collective-permute-start | bytes 786440 | tf_op jit(solution)/shard_map/ppermute | solution.py:258
  34.8 18.9 %collective-permute-start.2 = (bf16[128,1024]{1,0:T(8,128)(2,1)S(1)}, bf16[128,1024]{1,0:T(8,128)(2,1)}, u32[]{:S(2)}, u32[]{:S(2)}) collective-permute-start(bf16[128,1024]{1,0:T(8,128)(2,1)S(1)} %pad_maximum_fusion.1.refs_0_), channel_id=1, source_target_pairs={{0,64},{64,128},{128,192},{192,0},{1,65},{65,129},{129,193},{193,1... | collective-permute-start | bytes 786440 | tf_op jit(solution)/shard_map/ppermute | solution.py:258
  42.5 18.5 %copy-start.14 = (bf16[128,1024]{1,0:T(8,128)(2,1)}, bf16[128,1024]{1,0:T(8,128)(2,1)S(1)}, u32[]{:S(2)}) copy-start(bf16[128,1024]{1,0:T(8,128)(2,1)S(1)} %collective-permute-done.5.refs_4_) | copy-start | bytes 786436
  42.5 11.2 %collective-permute-start.8 = (bf16[128,1024]{1,0:T(8,128)(2,1)S(1)}, bf16[128,1024]{1,0:T(8,128)(2,1)}, u32[]{:S(2)}, u32[]{:S(2)}) collective-permute-start(bf16[128,1024]{1,0:T(8,128)(2,1)S(1)} %collective-permute-done.5.refs_4_), channel_id=1, source_target_pairs={{0,192},{64,0},{128,64},{192,128},{1,193},{65,1},{129,65},{193,129... | collective-permute-start | bytes 786440 | tf_op jit(solution)/shard_map/ppermute | solution.py:258
  45.3 9.0 %collective-permute-start.7 = (bf16[128,1024]{1,0:T(8,128)(2,1)S(1)}, bf16[128,1024]{1,0:T(8,128)(2,1)}, u32[]{:S(2)}, u32[]{:S(2)}) collective-permute-start(bf16[128,1024]{1,0:T(8,128)(2,1)S(1)} %collective-permute-done.5.refs_4_), channel_id=1, source_target_pairs={{0,128},{64,192},{128,0},{192,64},{1,129},{65,193},{129,1},{193,65... | collective-permute-start | bytes 786440 | tf_op jit(solution)/shard_map/ppermute | solution.py:258
  45.6 15.4 %copy-start.15 = (bf16[128,1024]{1,0:T(8,128)(2,1)}, bf16[128,1024]{1,0:T(8,128)(2,1)S(1)}, u32[]{:S(2)}) copy-start(bf16[128,1024]{1,0:T(8,128)(2,1)S(1)} %collective-permute-done.4.refs_3_) | copy-start | bytes 786436
  45.6 15.4 %collective-permute-start.6 = (bf16[128,1024]{1,0:T(8,128)(2,1)S(1)}, bf16[128,1024]{1,0:T(8,128)(2,1)}, u32[]{:S(2)}, u32[]{:S(2)}) collective-permute-start(bf16[128,1024]{1,0:T(8,128)(2,1)S(1)} %collective-permute-done.5.refs_4_), channel_id=1, source_target_pairs={{0,64},{64,128},{128,192},{192,0},{1,65},{65,129},{129,193},{193,1... | collective-permute-start | bytes 786440 | tf_op jit(solution)/shard_map/ppermute | solution.py:258
  46.3 0.7 copy-start.16
  51.0 10.7 %copy-start.1 = (bf16[16,32,1024]{2,1,0:T(8,128)(2,1)}, bf16[16,32,1024]{2,1,0:T(8,128)(2,1)S(1)}, u32[]{:S(2)}) copy-start(bf16[16,32,1024]{2,1,0:T(8,128)(2,1)S(1)} %all-to-all-done.1.got_own_ref.got_ref) | copy-start | bytes 3145732
  51.0 10.7 %collective-permute-start = (bf16[16,32,1024]{2,1,0:T(8,128)(2,1)S(1)}, bf16[16,32,1024]{2,1,0:T(8,128)(2,1)S(1)}, u32[]{:S(2)}, u32[]{:S(2)}) collective-permute-start(bf16[16,32,1024]{2,1,0:T(8,128)(2,1)S(1)} %all-to-all-done.1.got_own_ref.got_ref), channel_id=1, source_target_pairs={{0,16},{16,0},{1,17},{17,1},{2,18},{18,2},{3,19},{19,3},{4,20},{20... | collective-permute-start | bytes 3145736 | tf_op jit(solution)/shard_map/ppermute | solution.py:250
  61.7 1.0 copy-start.13
  62.6 14.0 %copy-start.2 = (bf16[16,32,1024]{2,1,0:T(8,128)(2,1)S(1)}, bf16[16,32,1024]{2,1,0:T(8,128)(2,1)}, u32[]{:S(2)}) copy-start(bf16[16,32,1024]{2,1,0:T(8,128)(2,1)} %copy-done.1) | copy-start | bytes 3145732
  62.6 14.0 %copy-start.4 = (f32[1024]{0:T(1024)S(1)}, f32[1024]{0:T(1024)}, u32[]{:S(2)}) copy-start(f32[1024]{0:T(1024)} %param.6) | copy-start | bytes 12292
  73.3 3.4 %collective-permute-start.16 = (bf16[256,1280]{1,0:T(8,128)(2,1)}, bf16[256,1280]{1,0:T(8,128)(2,1)S(1)}, u32[]{:S(2)}, u32[]{:S(2)}) collective-permute-start(bf16[256,1280]{1,0:T(8,128)(2,1)} %get-tuple-element.36), channel_id=1, source_target_pairs={{0,16},{16,0},{1,17},{17,1},{2,18},{18,2},{3,19},{19,3},{4,20},{20... | collective-permute-start | bytes 1966088 | tf_op jit(solution)/shard_map/ppermute | solution.py:250
  73.9 15.8 %collective-permute-start.12 = (bf16[128,1024]{1,0:T(8,128)(2,1)}, bf16[128,1024]{1,0:T(8,128)(2,1)S(1)}, u32[]{:S(2)}, u32[]{:S(2)}) collective-permute-start(bf16[128,1024]{1,0:T(8,128)(2,1)} %get-tuple-element.32), channel_id=1, source_target_pairs={{0,64},{64,128},{128,192},{192,0},{1,65},{65,129},{129,193},{193,1... | collective-permute-start | bytes 786440 | tf_op jit(solution)/shard_map/ppermute | solution.py:258
  73.9 17.8 %collective-permute-start.13 = (bf16[128,1024]{1,0:T(8,128)(2,1)}, bf16[128,1024]{1,0:T(8,128)(2,1)S(1)}, u32[]{:S(2)}, u32[]{:S(2)}) collective-permute-start(bf16[128,1024]{1,0:T(8,128)(2,1)} %get-tuple-element.33), channel_id=1, source_target_pairs={{0,128},{64,192},{128,0},{192,64},{1,129},{65,193},{129,1},{193,65... | collective-permute-start | bytes 786440 | tf_op jit(solution)/shard_map/ppermute | solution.py:258
  75.5 16.2 %collective-permute-start.14 = (bf16[128,1024]{1,0:T(8,128)(2,1)}, bf16[128,1024]{1,0:T(8,128)(2,1)}, u32[]{:S(2)}, u32[]{:S(2)}) collective-permute-start(bf16[128,1024]{1,0:T(8,128)(2,1)} %get-tuple-element.34), channel_id=1, source_target_pairs={{0,192},{64,0},{128,64},{192,128},{1,193},{65,1},{129,65},{193,129... | collective-permute-start | bytes 786440 | tf_op jit(solution)/shard_map/ppermute | solution.py:258
  76.6 1.3 %copy-start.3 = (f32[256,1280]{1,0:T(8,128)S(1)}, f32[256,1280]{1,0:T(8,128)}, u32[]{:S(2)}) copy-start(f32[256,1280]{1,0:T(8,128)} %get-tuple-element.35.mine_ref) | copy-start | bytes 3932164
  79.8 11.9 %copy-start.7 = (f32[128,1024]{1,0:T(8,128)S(1)}, f32[128,1024]{1,0:T(8,128)}, u32[]{:S(2)}) copy-start(f32[128,1024]{1,0:T(8,128)} %get-tuple-element.31) | copy-start | bytes 1572868
  79.8 16.6 %copy-start.8 = (bf16[1024,256]{1,0:T(8,128)(2,1)S(1)}, bf16[1024,256]{1,0:T(8,128)(2,1)}, u32[]{:S(2)}) copy-start(bf16[1024,256]{1,0:T(8,128)(2,1)} %get-tuple-element.39.w_mine_ref) | copy-start | bytes 1572868
  79.8 26.6 %copy-start.5 = (f32[128,1024]{1,0:T(8,128)S(1)}, f32[128,1024]{1,0:T(8,128)}, u32[]{:S(2)}) copy-start(f32[128,1024]{1,0:T(8,128)} %get-tuple-element.27.own_ref) | copy-start | bytes 1572868
  79.8 27.5 %all-to-all-start.2 = ((bf16[16,48,512]{2,1,0:T(8,128)(2,1)}), bf16[16,48,512]{2,1,0:T(8,128)(2,1)S(1)}, u32[]{:S(2)}, u32[]{:S(2)}) async-start(bf16[16,48,512]{2,1,0:T(8,128)(2,1)} %input_gradient.1), calls=%async_computation.2 | async-start | bytes 1572864 | tf_op jit(solution)/shard_map/all_to_all | solution.py:254
  87.2 11.5 %collective-permute-start.9 = (bf16[128,1024]{1,0:T(8,128)(2,1)}, bf16[128,1024]{1,0:T(8,128)(2,1)S(1)}, u32[]{:S(2)}, u32[]{:S(2)}) collective-permute-start(bf16[128,1024]{1,0:T(8,128)(2,1)} %get-tuple-element.28), channel_id=1, source_target_pairs={{0,64},{64,128},{128,192},{192,0},{1,65},{65,129},{129,193},{193,1... | collective-permute-start | bytes 786440 | tf_op jit(solution)/shard_map/ppermute | solution.py:258
  87.8 13.1 %collective-permute-start.10 = (bf16[128,1024]{1,0:T(8,128)(2,1)}, bf16[128,1024]{1,0:T(8,128)(2,1)S(1)}, u32[]{:S(2)}, u32[]{:S(2)}) collective-permute-start(bf16[128,1024]{1,0:T(8,128)(2,1)} %get-tuple-element.29), channel_id=1, source_target_pairs={{0,128},{64,192},{128,0},{192,64},{1,129},{65,193},{129,1},{193,65... | collective-permute-start | bytes 786440 | tf_op jit(solution)/shard_map/ppermute | solution.py:258
  89.7 12.5 %collective-permute-start.11 = (bf16[128,1024]{1,0:T(8,128)(2,1)}, bf16[128,1024]{1,0:T(8,128)(2,1)S(1)}, u32[]{:S(2)}, u32[]{:S(2)}) collective-permute-start(bf16[128,1024]{1,0:T(8,128)(2,1)} %get-tuple-element.30), channel_id=1, source_target_pairs={{0,192},{64,0},{128,64},{192,128},{1,193},{65,1},{129,65},{193,129... | collective-permute-start | bytes 786440 | tf_op jit(solution)/shard_map/ppermute | solution.py:258
  92.8 13.5 %collective-permute-start.15 = (bf16[128,1024]{1,0:T(8,128)(2,1)S(1)}, bf16[128,1024]{1,0:T(8,128)(2,1)S(1)}, u32[]{:S(2)}, u32[]{:S(2)}) collective-permute-start(bf16[128,1024]{1,0:T(8,128)(2,1)S(1)} %add_convert_fusion), channel_id=1, source_target_pairs={{0,32},{32,0},{1,33},{33,1},{2,34},{34,2},{3,35},{35,3},{4,36},{36... | collective-permute-start | bytes 786440 | tf_op jit(solution)/shard_map/ppermute | solution.py:262
  96.4 17.5 %collective-permute-start.17 = (bf16[1024,256]{1,0:T(8,128)(2,1)S(1)}, bf16[1024,256]{1,0:T(8,128)(2,1)S(1)}, u32[]{:S(2)}, u32[]{:S(2)}) collective-permute-start(bf16[1024,256]{1,0:T(8,128)(2,1)S(1)} %copy-done.8), channel_id=1, source_target_pairs={{0,16},{16,0},{1,17},{17,1},{2,18},{18,2},{3,19},{19,3},{4,20},{20... | collective-permute-start | bytes 1572872 | tf_op jit(solution)/shard_map/ppermute | solution.py:250
  107.3 6.7 %copy-start.6 = (bf16[16,48,512]{2,1,0:T(8,128)(2,1)}, bf16[16,48,512]{2,1,0:T(8,128)(2,1)S(1)}, u32[]{:S(2)}) copy-start(bf16[16,48,512]{2,1,0:T(8,128)(2,1)S(1)} %all-to-all-done.2.got_ref) | copy-start | bytes 2359300
  107.3 14.4 %all-to-all-start.3 = ((bf16[16,8,1024]{2,1,0:T(8,128)(2,1)}), bf16[16,8,1024]{2,1,0:T(8,128)(2,1)S(1)}, u32[]{:S(2)}, u32[]{:S(2)}) async-start(bf16[16,8,1024]{2,1,0:T(8,128)(2,1)} %sum_blocks.1), calls=%async_computation.3 | async-start | bytes 524288 | tf_op jit(solution)/shard_map/all_to_all | solution.py:254
  113.9 0.8 copy-start.9
  118.1 9.9 %copy-start.12 = (bf16[4,1536]{1,0:T(4,128)(2,1)S(1)}, bf16[4,1536]{1,0:T(4,128)(2,1)}, u32[]{:S(2)}) copy-start(bf16[4,1536]{1,0:T(4,128)(2,1)} %w_qkv_ref.1) | copy-start | bytes 36868
  122.0 5.3 %collective-permute-start.18 = (f32[4,1024]{1,0:T(4,128)S(1)}, f32[4,1024]{1,0:T(4,128)S(1)}, u32[]{:S(2)}, u32[]{:S(2)}) collective-permute-start(f32[4,1024]{1,0:T(4,128)S(1)} %dynamic-slice_bitcast_fusion), channel_id=1, source_target_pairs={{0,16},{16,0},{1,17},{17,1},{2,18},{18,2},{3,19},{19,3},{4,20},{20... | collective-permute-start | bytes 49160 | tf_op jit(solution)/shard_map/ppermute | solution.py:250
  128.0 0.7 copy-start.11

commit v7 on v6

--- a/solution.py
+++ b/solution.py
@@ -288,7 +288,9 @@
     w_got = swap(w_parts.reshape(-1, width), TM).reshape(tm, 2, shard, width)
 
     sent = jnp.concatenate([by_patch(frames_in), by_patch(out_grad)], axis=1)
-    sent, w_got = lax.optimization_barrier((sent, w_got))
+    own_row = lax.axis_index(DP + TM) * shard
+    gain_inverse = 1.0 / lax.dynamic_slice_in_dim(gain, own_row, shard)
+    sent, w_got, gain_inverse = lax.optimization_barrier((sent, w_got, gain_inverse))
 
     w_keep = lax.dynamic_index_in_dim(w_got, core, 1, keepdims=False).reshape(tm * shard, width)
     w_send = lax.dynamic_index_in_dim(w_got, 1 - core, 1, keepdims=False).reshape(tm * shard, width)
@@ -403,13 +405,11 @@
     total = jnp.sum(grads.reshape(tm, 2, shard, width).astype(f32), axis=0)
     keep = lax.dynamic_index_in_dim(total, core, 0, keepdims=False)
     recv = exchange(lax.dynamic_index_in_dim(total, 1 - core, 0, keepdims=False))
-    low = jnp.where(first, keep, recv).reshape(shard, 4, 1, HALF)
-    high = jnp.where(first, recv, keep).reshape(shard, 4, 1, HALF)
-    whole = jnp.concatenate([low, high], axis=2)
-    grad_qkv = whole[:, :3].reshape(shard, 6 * HALF)
-    grad_out = whole[:, 3].reshape(shard, 2 * HALF).T
-    own_row = lax.axis_index(DP + TM) * shard
-    grad_gain = jnp.sum(w_qkv.astype(f32) * grad_qkv, axis=1) / lax.dynamic_slice_in_dim(gain, own_row, shard)
+    low, high = jnp.where(first, keep, recv), jnp.where(first, recv, keep)
+    whole = [half[:, part * HALF : (part + 1) * HALF] for part in range(4) for half in (low, high)]
+    grad_qkv = jnp.concatenate(whole[:6], axis=1)
+    grad_out = jnp.concatenate(whole[6:], axis=1).T
+    grad_gain = jnp.sum(w_qkv.astype(f32) * grad_qkv * gain_inverse[:, None], axis=1)
     return (result[None], grad_in[None], grad_qkv, grad_out, grad_gain)
 
 

time: 129 us -> 129 us (level)
  other arithmetic: 3.06 us -> 4.44 us
    unnamed x36 -> x38, local copies, waits for them, and re-layouts: 4.44 us -> 3.88 us
where the time goes in v7:
time: 129 us
  starting transfers between devices  61.9 us (48%)
  waiting for transfers between devices  37 us (29%)
  Pallas kernels  18.7 us (14%)
  local copies, waits for them, and re-layouts  5.54 us (4%)
  other arithmetic  4.44 us (3%)
    all_to_all x4, starting transfers between devices, swap(): return lax.all_to_all(value, axes, split_axis=0, concat_axis=0, tiled=True)  29.5 us
    ppermute x12, starting transfers between devices, along_y(): lax.ppermute(value, 'y', [(i, (i + step) % Y_SIZE) for i in range(Y_SIZE)])  14.8 us
    all_to_all x4, waiting for transfers between devices, swap(): return lax.all_to_all(value, axes, split_axis=0, concat_axis=0, tiled=True)  13.2 us
    ppermute x5, starting transfers between devices, exchange(): return lax.ppermute(value, 'core', [(0, 1), (1, 0)])  11.6 us
    ppermute x2, waiting for transfers between devices, across_x(): return lax.ppermute(value, 'xh', [(0, 1), (1, 0)])  11.2 us
    ppermute x12, waiting for transfers between devices, along_y(): lax.ppermute(value, 'y', [(i, (i + step) % Y_SIZE) for i in range(Y_SIZE)])  10.9 us
    pallas_call x1, Pallas kernels, body(): pl.pallas_call(functools.partial(layer_kernel, patches), in_specs=[ANY, A...  10.6 us
    ppermute x2, starting transfers between devices, across_x(): return lax.ppermute(value, 'xh', [(0, 1), (1, 0)])  6.1 us
  transfers between devices with their start and end apart: 23, of which 11 were waited for; matrix products, arithmetic and copies ran while one was open for 3% of the time, Pallas kernels for 5%

profile of v7, /device:TPU:1, one launch (start us, length us, event | category | flops | bytes accessed | tf_op | source)
XLA Modules:
  0.0 128.6 jit_solution(5437392872350722657)
XLA Ops:
  0.6 0.0 copy-start
  0.6 1.5 %pack_weights.1 = bf16[16,8,1024]{2,1,0:T(8,128)(2,1)} custom-call(bf16[4,1536]{1,0:T(4,128)(2,1)} %w_qkv_ref.1, bf16[4,512]{1,0:T(4,128)(2,1)} %bitcast.35), custom_call_target="tpu_custom_call" | custom-call | bytes 262144 | tf_op jit(solution)/shard_map/pack_weights/pallas_call | solution.py:280
  2.1 10.0 %all-to-all-start = ((bf16[16,8,1024]{2,1,0:T(8,128)(2,1)}), bf16[16,8,1024]{2,1,0:T(8,128)(2,1)S(1)}, u32[]{:S(2)}, u32[]{:S(2)}) async-start(bf16[16,8,1024]{2,1,0:T(8,128)(2,1)} %pack_weights.1), calls=%async_computation | async-start | bytes 524288 | tf_op jit(solution)/shard_map/all_to_all | solution.py:254
  12.2 0.8 dynamic-slice_divide_fusion
  13.0 1.2 copy_bitcast_fusion
  14.2 1.1 pad_maximum_fusion
  15.3 5.6 %all-to-all-done = bf16[16,8,1024]{2,1,0:T(8,128)(2,1)S(1)} async-done(((bf16[16,8,1024]{2,1,0:T(8,128)(2,1)}), bf16[16,8,1024]{2,1,0:T(8,128)(2,1)S(1)}, u32[]{:S(2)}, u32[]{:S(2)}) %all-to-all-start) | async-done | bytes 262176 | tf_op jit(solution)/shard_map/all_to_all | solution.py:254
  20.9 0.1 reshape.65
  21.0 5.4 %all-to-all-start.1 = ((bf16[16,32,1024]{2,1,0:T(8,128)(2,1)}), bf16[16,32,1024]{2,1,0:T(8,128)(2,1)S(1)}, u32[]{:S(2)}, u32[]{:S(2)}) async-start(bf16[16,32,1024]{2,1,0:T(8,128)(2,1)} %pad_maximum_fusion), calls=%async_computation.1 | async-start | bytes 2097152 | tf_op jit(solution)/shard_map/all_to_all | solution.py:254
  26.4 0.1 constant_dynamic-slice_fusion.1
  26.6 1.6 %collective-permute-start.1 = (bf16[64,1024]{1,0:T(8,128)(2,1)S(1)}, bf16[64,1024]{1,0:T(8,128)(2,1)S(1)}, u32[]{:S(2)}, u32[]{:S(2)}) collective-permute-start(bf16[64,1024]{1,0:T(8,128)(2,1)S(1)} %reshape.68), channel_id=1, source_target_pairs={{0,16},{16,0},{1,17},{17,1},{2,18},{18,2},{3,19},{19,3},{4,20},{20... | collective-permute-start | bytes 393224 | tf_op jit(solution)/shard_map/ppermute | solution.py:250
  28.2 1.0 collective-permute-done.1
  29.2 2.5 %collective-permute-start.5 = (bf16[128,1024]{1,0:T(8,128)(2,1)S(1)}, bf16[128,1024]{1,0:T(8,128)(2,1)S(1)}, u32[]{:S(2)}, u32[]{:S(2)}) collective-permute-start(bf16[128,1024]{1,0:T(8,128)(2,1)S(1)} %pad_maximum_fusion.1.refs_0_), channel_id=1, source_target_pairs={{0,32},{32,0},{1,33},{33,1},{2,34},{34,2},{3,35},{35,3},{4,36},{36... | collective-permute-start | bytes 786440 | tf_op jit(solution)/shard_map/ppermute | solution.py:262
  31.7 2.7 %collective-permute-start.4 = (bf16[128,1024]{1,0:T(8,128)(2,1)S(1)}, bf16[128,1024]{1,0:T(8,128)(2,1)S(1)}, u32[]{:S(2)}, u32[]{:S(2)}) collective-permute-start(bf16[128,1024]{1,0:T(8,128)(2,1)S(1)} %pad_maximum_fusion.1.refs_0_), channel_id=1, source_target_pairs={{0,192},{64,0},{128,64},{192,128},{1,193},{65,1},{129,65},{193,129... | collective-permute-start | bytes 786440 | tf_op jit(solution)/shard_map/ppermute | solution.py:258
  34.5 0.3 collective-permute-start.3
  34.8 0.7 collective-permute-start.2
  35.5 7.0 %collective-permute-done.5.refs_4_ = bf16[128,1024]{1,0:T(8,128)(2,1)S(1)} collective-permute-done((bf16[128,1024]{1,0:T(8,128)(2,1)S(1)}, bf16[128,1024]{1,0:T(8,128)(2,1)S(1)}, u32[]{:S(2)}, u32[]{:S(2)}) %collective-permute-start.5) | collective-permute-done | bytes 262176 | tf_op jit(solution)/shard_map/ppermute | solution.py:262
  42.5 2.7 %collective-permute-start.8 = (bf16[128,1024]{1,0:T(8,128)(2,1)S(1)}, bf16[128,1024]{1,0:T(8,128)(2,1)}, u32[]{:S(2)}, u32[]{:S(2)}) collective-permute-start(bf16[128,1024]{1,0:T(8,128)(2,1)S(1)} %collective-permute-done.5.refs_4_), channel_id=1, source_target_pairs={{0,192},{64,0},{128,64},{192,128},{1,193},{65,1},{129,65},{193,129... | collective-permute-start | bytes 786440 | tf_op jit(solution)/shard_map/ppermute | solution.py:258
  45.3 0.3 collective-permute-start.7
  45.6 0.0 collective-permute-done.4.refs_3_
  45.6 0.7 collective-permute-start.6
  46.3 0.7 copy-done.16
  47.0 4.0 %all-to-all-done.1.got_own_ref.got_ref = bf16[16,32,1024]{2,1,0:T(8,128)(2,1)S(1)} async-done(((bf16[16,32,1024]{2,1,0:T(8,128)(2,1)}), bf16[16,32,1024]{2,1,0:T(8,128)(2,1)S(1)}, u32[]{:S(2)}, u32[]{:S(2)}) %all-to-all-start.1) | async-done | bytes 1048608 | tf_op jit(solution)/shard_map/all_to_all | solution.py:254
  51.0 2.7 %collective-permute-start = (bf16[16,32,1024]{2,1,0:T(8,128)(2,1)S(1)}, bf16[16,32,1024]{2,1,0:T(8,128)(2,1)S(1)}, u32[]{:S(2)}, u32[]{:S(2)}) collective-permute-start(bf16[16,32,1024]{2,1,0:T(8,128)(2,1)S(1)} %all-to-all-done.1.got_own_ref.got_ref), channel_id=1, source_target_pairs={{0,16},{16,0},{1,17},{17,1},{2,18},{18,2},{3,19},{19,3},{4,20},{20... | collective-permute-start | bytes 3145736 | tf_op jit(solution)/shard_map/ppermute | solution.py:250
  53.7 0.0 collective-permute-done.2.refs_1_
  53.7 0.0 collective-permute-done.8.refs_7_
  53.7 0.5 collective-permute-done.7.refs_6_
  54.2 6.8 %collective-permute-done.6.refs_5_ = bf16[128,1024]{1,0:T(8,128)(2,1)} collective-permute-done((bf16[128,1024]{1,0:T(8,128)(2,1)S(1)}, bf16[128,1024]{1,0:T(8,128)(2,1)}, u32[]{:S(2)}, u32[]{:S(2)}) %collective-permute-start.6) | collective-permute-done | bytes 262176 | tf_op jit(solution)/shard_map/ppermute | solution.py:258
  61.1 0.6 arrived.1.token_ref
  61.7 1.0 copy-done.13
  62.6 10.6 %layer.1 = (bf16[1024,256]{1,0:T(8,128)(2,1)}, f32[256,1280]{1,0:T(8,128)}, bf16[256,1280]{1,0:T(8,128)(2,1)}, f32[128,1024]{1,0:T(8,128)}, bf16[128,1024]{1,0:T...) custom-call(bf16[16,32,1024]{2,1,0:T(8,128)(2,1)} %copy-done.1, ...), custom_call_target="tpu_custom_call" | custom-call | flops 30000001024 | bytes 10485760 | tf_op jit(solution)/shard_map/layer/pallas_call | solution.py:323
  73.3 0.7 collective-permute-start.16
  73.9 0.0 collective-permute-start.12
  73.9 1.6 %collective-permute-start.13 = (bf16[128,1024]{1,0:T(8,128)(2,1)}, bf16[128,1024]{1,0:T(8,128)(2,1)S(1)}, u32[]{:S(2)}, u32[]{:S(2)}) collective-permute-start(bf16[128,1024]{1,0:T(8,128)(2,1)} %get-tuple-element.34), channel_id=1, source_target_pairs={{0,128},{64,192},{128,0},{192,64},{1,129},{65,193},{129,1},{193,65... | collective-permute-start | bytes 786440 | tf_op jit(solution)/shard_map/ppermute | solution.py:258
  75.5 1.1 collective-permute-start.14
  76.6 0.0 collective-permute-done.16.other
  76.7 1.3 %copy-done.3 = f32[256,1280]{1,0:T(8,128)S(1)} copy-done((f32[256,1280]{1,0:T(8,128)S(1)}, f32[256,1280]{1,0:T(8,128)}, u32[]{:S(2)}) %copy-start.3) | copy-done | bytes 1310744
  78.0 1.8 %input_gradient.1 = bf16[16,48,512]{2,1,0:T(8,128)(2,1)} custom-call(bf16[16,32,1024]{2,1,0:T(8,128)(2,1)S(1)} %copy-done.2, f32[256,1280]{1,0:T(8,128)S(1)} %copy-done.3, bf16[256,1280]{1,0:T(8,128)(2,1)S(1)} %collective-permute-done.16.other, f32[1,1024]{1,0:T(1,128)S(1)} %bitcast.32), custom_call_target="tpu_custom_call" | custom-call | flops 1000000000 | bytes 6291456 | tf_op jit(solution)/shard_map/input_gradient/pallas_call | solution.py:366
  79.7 0.0 copy-start.7
  79.8 0.0 copy-start.5
  79.8 7.4 %all-to-all-start.2 = ((bf16[16,48,512]{2,1,0:T(8,128)(2,1)}), bf16[16,48,512]{2,1,0:T(8,128)(2,1)S(1)}, u32[]{:S(2)}, u32[]{:S(2)}) async-start(bf16[16,48,512]{2,1,0:T(8,128)(2,1)} %input_gradient.1), calls=%async_computation.2 | async-start | bytes 1572864 | tf_op jit(solution)/shard_map/all_to_all | solution.py:254
  87.2 0.7 collective-permute-start.9
  87.8 1.9 %collective-permute-start.10 = (bf16[128,1024]{1,0:T(8,128)(2,1)}, bf16[128,1024]{1,0:T(8,128)(2,1)S(1)}, u32[]{:S(2)}, u32[]{:S(2)}) collective-permute-start(bf16[128,1024]{1,0:T(8,128)(2,1)} %get-tuple-element.30), channel_id=1, source_target_pairs={{0,128},{64,192},{128,0},{192,64},{1,129},{65,193},{129,1},{193,65... | collective-permute-start | bytes 786440 | tf_op jit(solution)/shard_map/ppermute | solution.py:258
  89.7 2.0 %collective-permute-start.11 = (bf16[128,1024]{1,0:T(8,128)(2,1)}, bf16[128,1024]{1,0:T(8,128)(2,1)S(1)}, u32[]{:S(2)}, u32[]{:S(2)}) collective-permute-start(bf16[128,1024]{1,0:T(8,128)(2,1)} %get-tuple-element.31), channel_id=1, source_target_pairs={{0,192},{64,0},{128,64},{192,128},{1,193},{65,1},{129,65},{193,129... | collective-permute-start | bytes 786440 | tf_op jit(solution)/shard_map/ppermute | solution.py:258
  91.7 0.0 collective-permute-done.13
  91.7 1.1 add_convert_fusion
  92.8 3.6 %collective-permute-start.15 = (bf16[128,1024]{1,0:T(8,128)(2,1)S(1)}, bf16[128,1024]{1,0:T(8,128)(2,1)S(1)}, u32[]{:S(2)}, u32[]{:S(2)}) collective-permute-start(bf16[128,1024]{1,0:T(8,128)(2,1)S(1)} %add_convert_fusion), channel_id=1, source_target_pairs={{0,32},{32,0},{1,33},{33,1},{2,34},{34,2},{3,35},{35,3},{4,36},{36... | collective-permute-start | bytes 786440 | tf_op jit(solution)/shard_map/ppermute | solution.py:262
  96.4 2.3 %collective-permute-start.17 = (bf16[1024,256]{1,0:T(8,128)(2,1)S(1)}, bf16[1024,256]{1,0:T(8,128)(2,1)S(1)}, u32[]{:S(2)}, u32[]{:S(2)}) collective-permute-start(bf16[1024,256]{1,0:T(8,128)(2,1)S(1)} %copy-done.8), channel_id=1, source_target_pairs={{0,16},{16,0},{1,17},{17,1},{2,18},{18,2},{3,19},{19,3},{4,20},{20... | collective-permute-start | bytes 1572872 | tf_op jit(solution)/shard_map/ppermute | solution.py:250
  98.7 2.2 %collective-permute-done.10.b_ref = bf16[128,1024]{1,0:T(8,128)(2,1)S(1)} collective-permute-done((bf16[128,1024]{1,0:T(8,128)(2,1)}, bf16[128,1024]{1,0:T(8,128)(2,1)S(1)}, u32[]{:S(2)}, u32[]{:S(2)}) %collective-permute-start.10) | collective-permute-done | bytes 262176 | tf_op jit(solution)/shard_map/ppermute | solution.py:258
  100.9 1.3 collective-permute-done.11.c_ref
  102.2 4.2 %collective-permute-done.15.across_ref = bf16[128,1024]{1,0:T(8,128)(2,1)S(1)} collective-permute-done((bf16[128,1024]{1,0:T(8,128)(2,1)S(1)}, bf16[128,1024]{1,0:T(8,128)(2,1)S(1)}, u32[]{:S(2)}, u32[]{:S(2)}) %collective-permute-start.15) | collective-permute-done | bytes 262176 | tf_op jit(solution)/shard_map/ppermute | solution.py:262
  106.3 0.9 sum_blocks.1
  107.2 6.6 %all-to-all-start.3 = ((bf16[16,8,1024]{2,1,0:T(8,128)(2,1)}), bf16[16,8,1024]{2,1,0:T(8,128)(2,1)S(1)}, u32[]{:S(2)}, u32[]{:S(2)}) async-start(bf16[16,8,1024]{2,1,0:T(8,128)(2,1)} %sum_blocks.1), calls=%async_computation.3 | async-start | bytes 524288 | tf_op jit(solution)/shard_map/all_to_all | solution.py:254
  113.9 0.8 copy-done.9
  114.7 3.4 %home.1 = (bf16[2,128,1024]{2,1,0:T(8,128)(2,1)}, bf16[2,128,1024]{2,1,0:T(8,128)(2,1)}) custom-call(bf16[16,48,512]{2,1,0:T(8,128)(2,1)} %copy-done.6, bf16[2,128,1024]{2,1,0:T(8,128)(2,1)} %bitcast.33, bf16[1024,256]{1,0:T(8,128)(2,1)} %get-tuple-element.40.w_mine_ref, bf16[1024,256]{1,0:T(8,128)(2,1)} %copy-done.9), custom_call_target="tpu_custom_call" | custom-call | flops 300000000 | bytes 4194304 | tf_op jit(solution)/shard_map/home/pallas_call | solution.py:384
  118.1 0.0 copy-start.11
  118.1 3.6 %all-to-all-done.3 = bf16[16,8,1024]{2,1,0:T(8,128)(2,1)S(1)} async-done(((bf16[16,8,1024]{2,1,0:T(8,128)(2,1)}), bf16[16,8,1024]{2,1,0:T(8,128)(2,1)S(1)}, u32[]{:S(2)}, u32[]{:S(2)}) %all-to-all-start.3) | async-done | bytes 262176 | tf_op jit(solution)/shard_map/all_to_all | solution.py:254
  121.7 0.2 reshape.69
  121.9 0.1 reduce_sum.18
  122.0 4.4 %collective-permute-start.18 = (f32[4,1024]{1,0:T(4,128)S(1)}, f32[4,1024]{1,0:T(4,128)S(1)}, u32[]{:S(2)}, u32[]{:S(2)}) collective-permute-start(f32[4,1024]{1,0:T(4,128)S(1)} %dynamic-slice_bitcast_fusion), channel_id=1, source_target_pairs={{0,16},{16,0},{1,17},{17,1},{2,18},{18,2},{3,19},{19,3},{4,20},{20... | collective-permute-start | bytes 49160 | tf_op jit(solution)/shard_map/ppermute | solution.py:250
  126.3 0.8 collective-permute-done.18
  127.2 0.0 copy-start.12
  127.3 0.6 maximum_bitcast_fusion
  127.9 0.7 multiply_reduce_fusion
  (44 shorter events, 0.2 us)
Async XLA Ops:
  0.6 12.4 %copy-start = (bf16[1,2,128,1024]{3,2,1,0:T(8,128)(2,1)S(1)}, bf16[1,2,128,1024]{3,2,1,0:T(8,128)(2,1)}, u32[]{:S(2)}) copy-start(bf16[1,2,128,1024]{3,2,1,0:T(8,128)(2,1)} %param.9) | copy-start | bytes 1572868
  2.1 18.8 %all-to-all-start = ((bf16[16,8,1024]{2,1,0:T(8,128)(2,1)}), bf16[16,8,1024]{2,1,0:T(8,128)(2,1)S(1)}, u32[]{:S(2)}, u32[]{:S(2)}) async-start(bf16[16,8,1024]{2,1,0:T(8,128)(2,1)} %pack_weights.1), calls=%async_computation | async-start | bytes 524288 | tf_op jit(solution)/shard_map/all_to_all | solution.py:254
  21.0 30.0 %all-to-all-start.1 = ((bf16[16,32,1024]{2,1,0:T(8,128)(2,1)}), bf16[16,32,1024]{2,1,0:T(8,128)(2,1)S(1)}, u32[]{:S(2)}, u32[]{:S(2)}) async-start(bf16[16,32,1024]{2,1,0:T(8,128)(2,1)} %pad_maximum_fusion), calls=%async_computation.1 | async-start | bytes 2097152 | tf_op jit(solution)/shard_map/all_to_all | solution.py:254
  26.6 2.5 %collective-permute-start.1 = (bf16[64,1024]{1,0:T(8,128)(2,1)S(1)}, bf16[64,1024]{1,0:T(8,128)(2,1)S(1)}, u32[]{:S(2)}, u32[]{:S(2)}) collective-permute-start(bf16[64,1024]{1,0:T(8,128)(2,1)S(1)} %reshape.68), channel_id=1, source_target_pairs={{0,16},{16,0},{1,17},{17,1},{2,18},{18,2},{3,19},{19,3},{4,20},{20... | collective-permute-start | bytes 393224 | tf_op jit(solution)/shard_map/ppermute | solution.py:250
  29.2 31.9 %copy-start.10 = (bf16[128,1024]{1,0:T(8,128)(2,1)}, bf16[128,1024]{1,0:T(8,128)(2,1)S(1)}, u32[]{:S(2)}) copy-start(bf16[128,1024]{1,0:T(8,128)(2,1)S(1)} %pad_maximum_fusion.1.refs_0_) | copy-start | bytes 786436
  29.2 13.3 %collective-permute-start.5 = (bf16[128,1024]{1,0:T(8,128)(2,1)S(1)}, bf16[128,1024]{1,0:T(8,128)(2,1)S(1)}, u32[]{:S(2)}, u32[]{:S(2)}) collective-permute-start(bf16[128,1024]{1,0:T(8,128)(2,1)S(1)} %pad_maximum_fusion.1.refs_0_), channel_id=1, source_target_pairs={{0,32},{32,0},{1,33},{33,1},{2,34},{34,2},{3,35},{35,3},{4,36},{36... | collective-permute-start | bytes 786440 | tf_op jit(solution)/shard_map/ppermute | solution.py:262
  31.7 13.9 %collective-permute-start.4 = (bf16[128,1024]{1,0:T(8,128)(2,1)S(1)}, bf16[128,1024]{1,0:T(8,128)(2,1)S(1)}, u32[]{:S(2)}, u32[]{:S(2)}) collective-permute-start(bf16[128,1024]{1,0:T(8,128)(2,1)S(1)} %pad_maximum_fusion.1.refs_0_), channel_id=1, source_target_pairs={{0,192},{64,0},{128,64},{192,128},{1,193},{65,1},{129,65},{193,129... | collective-permute-start | bytes 786440 | tf_op jit(solution)/shard_map/ppermute | solution.py:258
  34.5 11.8 %collective-permute-start.3 = (bf16[128,1024]{1,0:T(8,128)(2,1)S(1)}, bf16[128,1024]{1,0:T(8,128)(2,1)S(1)}, u32[]{:S(2)}, u32[]{:S(2)}) collective-permute-start(bf16[128,1024]{1,0:T(8,128)(2,1)S(1)} %pad_maximum_fusion.1.refs_0_), channel_id=1, source_target_pairs={{0,128},{64,192},{128,0},{192,64},{1,129},{65,193},{129,1},{193,65... | collective-permute-start | bytes 786440 | tf_op jit(solution)/shard_map/ppermute | solution.py:258
  34.8 18.9 %collective-permute-start.2 = (bf16[128,1024]{1,0:T(8,128)(2,1)S(1)}, bf16[128,1024]{1,0:T(8,128)(2,1)}, u32[]{:S(2)}, u32[]{:S(2)}) collective-permute-start(bf16[128,1024]{1,0:T(8,128)(2,1)S(1)} %pad_maximum_fusion.1.refs_0_), channel_id=1, source_target_pairs={{0,64},{64,128},{128,192},{192,0},{1,65},{65,129},{129,193},{193,1... | collective-permute-start | bytes 786440 | tf_op jit(solution)/shard_map/ppermute | solution.py:258
  42.5 18.5 %copy-start.14 = (bf16[128,1024]{1,0:T(8,128)(2,1)}, bf16[128,1024]{1,0:T(8,128)(2,1)S(1)}, u32[]{:S(2)}) copy-start(bf16[128,1024]{1,0:T(8,128)(2,1)S(1)} %collective-permute-done.5.refs_4_) | copy-start | bytes 786436
  42.5 11.2 %collective-permute-start.8 = (bf16[128,1024]{1,0:T(8,128)(2,1)S(1)}, bf16[128,1024]{1,0:T(8,128)(2,1)}, u32[]{:S(2)}, u32[]{:S(2)}) collective-permute-start(bf16[128,1024]{1,0:T(8,128)(2,1)S(1)} %collective-permute-done.5.refs_4_), channel_id=1, source_target_pairs={{0,192},{64,0},{128,64},{192,128},{1,193},{65,1},{129,65},{193,129... | collective-permute-start | bytes 786440 | tf_op jit(solution)/shard_map/ppermute | solution.py:258
  45.3 8.9 %collective-permute-start.7 = (bf16[128,1024]{1,0:T(8,128)(2,1)S(1)}, bf16[128,1024]{1,0:T(8,128)(2,1)}, u32[]{:S(2)}, u32[]{:S(2)}) collective-permute-start(bf16[128,1024]{1,0:T(8,128)(2,1)S(1)} %collective-permute-done.5.refs_4_), channel_id=1, source_target_pairs={{0,128},{64,192},{128,0},{192,64},{1,129},{65,193},{129,1},{193,65... | collective-permute-start | bytes 786440 | tf_op jit(solution)/shard_map/ppermute | solution.py:258
  45.6 15.4 %copy-start.15 = (bf16[128,1024]{1,0:T(8,128)(2,1)}, bf16[128,1024]{1,0:T(8,128)(2,1)S(1)}, u32[]{:S(2)}) copy-start(bf16[128,1024]{1,0:T(8,128)(2,1)S(1)} %collective-permute-done.4.refs_3_) | copy-start | bytes 786436
  45.6 15.4 %collective-permute-start.6 = (bf16[128,1024]{1,0:T(8,128)(2,1)S(1)}, bf16[128,1024]{1,0:T(8,128)(2,1)}, u32[]{:S(2)}, u32[]{:S(2)}) collective-permute-start(bf16[128,1024]{1,0:T(8,128)(2,1)S(1)} %collective-permute-done.5.refs_4_), channel_id=1, source_target_pairs={{0,64},{64,128},{128,192},{192,0},{1,65},{65,129},{129,193},{193,1... | collective-permute-start | bytes 786440 | tf_op jit(solution)/shard_map/ppermute | solution.py:258
  46.3 0.7 copy-start.16
  51.0 10.7 %copy-start.1 = (bf16[16,32,1024]{2,1,0:T(8,128)(2,1)}, bf16[16,32,1024]{2,1,0:T(8,128)(2,1)S(1)}, u32[]{:S(2)}) copy-start(bf16[16,32,1024]{2,1,0:T(8,128)(2,1)S(1)} %all-to-all-done.1.got_own_ref.got_ref) | copy-start | bytes 3145732
  51.0 10.7 %collective-permute-start = (bf16[16,32,1024]{2,1,0:T(8,128)(2,1)S(1)}, bf16[16,32,1024]{2,1,0:T(8,128)(2,1)S(1)}, u32[]{:S(2)}, u32[]{:S(2)}) collective-permute-start(bf16[16,32,1024]{2,1,0:T(8,128)(2,1)S(1)} %all-to-all-done.1.got_own_ref.got_ref), channel_id=1, source_target_pairs={{0,16},{16,0},{1,17},{17,1},{2,18},{18,2},{3,19},{19,3},{4,20},{20... | collective-permute-start | bytes 3145736 | tf_op jit(solution)/shard_map/ppermute | solution.py:250
  61.7 1.0 copy-start.13
  62.6 14.0 %copy-start.2 = (bf16[16,32,1024]{2,1,0:T(8,128)(2,1)S(1)}, bf16[16,32,1024]{2,1,0:T(8,128)(2,1)}, u32[]{:S(2)}) copy-start(bf16[16,32,1024]{2,1,0:T(8,128)(2,1)} %copy-done.1) | copy-start | bytes 3145732
  62.6 14.0 %copy-start.4 = (f32[1024]{0:T(1024)S(1)}, f32[1024]{0:T(1024)}, u32[]{:S(2)}) copy-start(f32[1024]{0:T(1024)} %param.6) | copy-start | bytes 12292
  73.3 3.4 %collective-permute-start.16 = (bf16[256,1280]{1,0:T(8,128)(2,1)}, bf16[256,1280]{1,0:T(8,128)(2,1)S(1)}, u32[]{:S(2)}, u32[]{:S(2)}) collective-permute-start(bf16[256,1280]{1,0:T(8,128)(2,1)} %get-tuple-element.37), channel_id=1, source_target_pairs={{0,16},{16,0},{1,17},{17,1},{2,18},{18,2},{3,19},{19,3},{4,20},{20... | collective-permute-start | bytes 1966088 | tf_op jit(solution)/shard_map/ppermute | solution.py:250
  73.9 15.8 %collective-permute-start.12 = (bf16[128,1024]{1,0:T(8,128)(2,1)}, bf16[128,1024]{1,0:T(8,128)(2,1)S(1)}, u32[]{:S(2)}, u32[]{:S(2)}) collective-permute-start(bf16[128,1024]{1,0:T(8,128)(2,1)} %get-tuple-element.33), channel_id=1, source_target_pairs={{0,64},{64,128},{128,192},{192,0},{1,65},{65,129},{129,193},{193,1... | collective-permute-start | bytes 786440 | tf_op jit(solution)/shard_map/ppermute | solution.py:258
  73.9 17.7 %collective-permute-start.13 = (bf16[128,1024]{1,0:T(8,128)(2,1)}, bf16[128,1024]{1,0:T(8,128)(2,1)S(1)}, u32[]{:S(2)}, u32[]{:S(2)}) collective-permute-start(bf16[128,1024]{1,0:T(8,128)(2,1)} %get-tuple-element.34), channel_id=1, source_target_pairs={{0,128},{64,192},{128,0},{192,64},{1,129},{65,193},{129,1},{193,65... | collective-permute-start | bytes 786440 | tf_op jit(solution)/shard_map/ppermute | solution.py:258
  75.5 16.2 %collective-permute-start.14 = (bf16[128,1024]{1,0:T(8,128)(2,1)}, bf16[128,1024]{1,0:T(8,128)(2,1)}, u32[]{:S(2)}, u32[]{:S(2)}) collective-permute-start(bf16[128,1024]{1,0:T(8,128)(2,1)} %get-tuple-element.35), channel_id=1, source_target_pairs={{0,192},{64,0},{128,64},{192,128},{1,193},{65,1},{129,65},{193,129... | collective-permute-start | bytes 786440 | tf_op jit(solution)/shard_map/ppermute | solution.py:258
  76.6 1.3 %copy-start.3 = (f32[256,1280]{1,0:T(8,128)S(1)}, f32[256,1280]{1,0:T(8,128)}, u32[]{:S(2)}) copy-start(f32[256,1280]{1,0:T(8,128)} %get-tuple-element.36.mine_ref) | copy-start | bytes 3932164
  79.7 11.9 %copy-start.7 = (f32[128,1024]{1,0:T(8,128)S(1)}, f32[128,1024]{1,0:T(8,128)}, u32[]{:S(2)}) copy-start(f32[128,1024]{1,0:T(8,128)} %get-tuple-element.32) | copy-start | bytes 1572868
  79.8 16.6 %copy-start.8 = (bf16[1024,256]{1,0:T(8,128)(2,1)S(1)}, bf16[1024,256]{1,0:T(8,128)(2,1)}, u32[]{:S(2)}) copy-start(bf16[1024,256]{1,0:T(8,128)(2,1)} %get-tuple-element.40.w_mine_ref) | copy-start | bytes 1572868
  79.8 26.6 %copy-start.5 = (f32[128,1024]{1,0:T(8,128)S(1)}, f32[128,1024]{1,0:T(8,128)}, u32[]{:S(2)}) copy-start(f32[128,1024]{1,0:T(8,128)} %get-tuple-element.28.own_ref) | copy-start | bytes 1572868
  79.8 27.5 %all-to-all-start.2 = ((bf16[16,48,512]{2,1,0:T(8,128)(2,1)}), bf16[16,48,512]{2,1,0:T(8,128)(2,1)S(1)}, u32[]{:S(2)}, u32[]{:S(2)}) async-start(bf16[16,48,512]{2,1,0:T(8,128)(2,1)} %input_gradient.1), calls=%async_computation.2 | async-start | bytes 1572864 | tf_op jit(solution)/shard_map/all_to_all | solution.py:254
  87.2 11.5 %collective-permute-start.9 = (bf16[128,1024]{1,0:T(8,128)(2,1)}, bf16[128,1024]{1,0:T(8,128)(2,1)S(1)}, u32[]{:S(2)}, u32[]{:S(2)}) collective-permute-start(bf16[128,1024]{1,0:T(8,128)(2,1)} %get-tuple-element.29), channel_id=1, source_target_pairs={{0,64},{64,128},{128,192},{192,0},{1,65},{65,129},{129,193},{193,1... | collective-permute-start | bytes 786440 | tf_op jit(solution)/shard_map/ppermute | solution.py:258
  87.8 13.1 %collective-permute-start.10 = (bf16[128,1024]{1,0:T(8,128)(2,1)}, bf16[128,1024]{1,0:T(8,128)(2,1)S(1)}, u32[]{:S(2)}, u32[]{:S(2)}) collective-permute-start(bf16[128,1024]{1,0:T(8,128)(2,1)} %get-tuple-element.30), channel_id=1, source_target_pairs={{0,128},{64,192},{128,0},{192,64},{1,129},{65,193},{129,1},{193,65... | collective-permute-start | bytes 786440 | tf_op jit(solution)/shard_map/ppermute | solution.py:258
  89.7 12.5 %collective-permute-start.11 = (bf16[128,1024]{1,0:T(8,128)(2,1)}, bf16[128,1024]{1,0:T(8,128)(2,1)S(1)}, u32[]{:S(2)}, u32[]{:S(2)}) collective-permute-start(bf16[128,1024]{1,0:T(8,128)(2,1)} %get-tuple-element.31), channel_id=1, source_target_pairs={{0,192},{64,0},{128,64},{192,128},{1,193},{65,1},{129,65},{193,129... | collective-permute-start | bytes 786440 | tf_op jit(solution)/shard_map/ppermute | solution.py:258
  92.8 13.5 %collective-permute-start.15 = (bf16[128,1024]{1,0:T(8,128)(2,1)S(1)}, bf16[128,1024]{1,0:T(8,128)(2,1)S(1)}, u32[]{:S(2)}, u32[]{:S(2)}) collective-permute-start(bf16[128,1024]{1,0:T(8,128)(2,1)S(1)} %add_convert_fusion), channel_id=1, source_target_pairs={{0,32},{32,0},{1,33},{33,1},{2,34},{34,2},{3,35},{35,3},{4,36},{36... | collective-permute-start | bytes 786440 | tf_op jit(solution)/shard_map/ppermute | solution.py:262
  96.4 17.5 %collective-permute-start.17 = (bf16[1024,256]{1,0:T(8,128)(2,1)S(1)}, bf16[1024,256]{1,0:T(8,128)(2,1)S(1)}, u32[]{:S(2)}, u32[]{:S(2)}) collective-permute-start(bf16[1024,256]{1,0:T(8,128)(2,1)S(1)} %copy-done.8), channel_id=1, source_target_pairs={{0,16},{16,0},{1,17},{17,1},{2,18},{18,2},{3,19},{19,3},{4,20},{20... | collective-permute-start | bytes 1572872 | tf_op jit(solution)/shard_map/ppermute | solution.py:250
  107.2 6.7 %copy-start.6 = (bf16[16,48,512]{2,1,0:T(8,128)(2,1)}, bf16[16,48,512]{2,1,0:T(8,128)(2,1)S(1)}, u32[]{:S(2)}) copy-start(bf16[16,48,512]{2,1,0:T(8,128)(2,1)S(1)} %all-to-all-done.2.got_ref) | copy-start | bytes 2359300
  107.2 14.4 %all-to-all-start.3 = ((bf16[16,8,1024]{2,1,0:T(8,128)(2,1)}), bf16[16,8,1024]{2,1,0:T(8,128)(2,1)S(1)}, u32[]{:S(2)}, u32[]{:S(2)}) async-start(bf16[16,8,1024]{2,1,0:T(8,128)(2,1)} %sum_blocks.1), calls=%async_computation.3 | async-start | bytes 524288 | tf_op jit(solution)/shard_map/all_to_all | solution.py:254
  113.9 0.8 copy-start.9
  118.1 9.8 %copy-start.11 = (bf16[4,1536]{1,0:T(4,128)(2,1)S(1)}, bf16[4,1536]{1,0:T(4,128)(2,1)}, u32[]{:S(2)}) copy-start(bf16[4,1536]{1,0:T(4,128)(2,1)} %w_qkv_ref.1) | copy-start | bytes 36868
  122.0 5.2 %collective-permute-start.18 = (f32[4,1024]{1,0:T(4,128)S(1)}, f32[4,1024]{1,0:T(4,128)S(1)}, u32[]{:S(2)}, u32[]{:S(2)}) collective-permute-start(f32[4,1024]{1,0:T(4,128)S(1)} %dynamic-slice_bitcast_fusion), channel_id=1, source_target_pairs={{0,16},{16,0},{1,17},{17,1},{2,18},{18,2},{3,19},{19,3},{4,20},{20... | collective-permute-start | bytes 49160 | tf_op jit(solution)/shard_map/ppermute | solution.py:250
  127.2 1.3 %copy-start.12 = (f32[4,1536]{1,0:T(4,128)}, f32[4,1536]{1,0:T(4,128)S(1)}, u32[]{:S(2)}) copy-start(f32[4,1536]{1,0:T(4,128)S(1)} %get-tuple-element.56) | copy-start | bytes 73732
